TPU v7x, 32 devices: a whole 2x2x4 slice. The times are simulated.
32 devices in a mesh: dp: 8 (over z, y), tensor: 4 (over x, core).
Axes of the slice: x: 2, y: 2, z: 4, core: 2. Of those that a mesh axis runs over, the one named last changes fastest.
Arguments:
- tokens: bfloat16 [336, 96, 512], P('tensor', 'dp'), may hold values from -6 to 6
- seq_counts: int32 [8], P('dp'), may hold values from 1 to 12, as said below
- first_frame: int32 [96], P('dp'), may hold values from 0 to 5
- norm1_gain: float32 [512], replicated, may hold values from 0.5 to 1.5
- norm1_bias: float32 [512], replicated, may hold values from -2 to 2
- qkv_weight: bfloat16 [512, 1536], P(None, 'tensor'), may hold values from -0.25 to 0.25
- out_weight: bfloat16 [512, 512], P('tensor'), may hold values from -2 to 2
- out_bias: float32 [512], replicated, may hold values from -2 to 2
- norm2_gain: float32 [512], replicated, may hold values from 0.5 to 1.5
- norm2_bias: float32 [512], replicated, may hold values from -2 to 2
- up_weight: bfloat16 [512, 2048], P(None, 'tensor'), may hold values from -0.25 to 0.25
- up_bias: float32 [2048], P('tensor'), may hold values from -2 to 2
- down_weight: bfloat16 [2048, 512], P('tensor'), may hold values from -0.125 to 0.125
- down_bias: float32 [512], replicated, may hold values from -2 to 2
- out_cotangent: bfloat16 [336, 96, 512], P('tensor', 'dp'), may hold values from -6 to 6
Outputs:
- block_output: bfloat16 [336, 96, 512], P('tensor', 'dp')
- input_grad: bfloat16 [336, 96, 512], P('tensor', 'dp')
- qkv_weight_grad: float32 [512, 1536], P(None, 'tensor')
- out_weight_grad: float32 [512, 512], P('tensor')
- up_weight_grad: float32 [512, 2048], P(None, 'tensor')
- down_weight_grad: float32 [2048, 512], P('tensor')
- up_bias_grad: float32 [2048], P('tensor')
- out_bias_grad: float32 [512], replicated
- down_bias_grad: float32 [512], replicated
- norm1_gain_grad: float32 [512], replicated
- norm1_bias_grad: float32 [512], replicated
- norm2_gain_grad: float32 [512], replicated
- norm2_bias_grad: float32 [512], replicated
Inputs may be any that keep to these rules, and one draw needn't show every extreme that they name: `seq_counts`: entry i is how many of the first sequence slots of data index i are live, out of 12; some index is full in every draw.
All inputs are finite; a program needn't handle non-finite values.
Results may differ from a plain program's by a relative error of at most 0.02.
Values may be sent and summed in bfloat16 or wider, within the bound.
No kernel may reach another device: no remote copies, remote signals or barrier semaphores. Data moves between devices by JAX's collectives and lax.ppermute only.
A program may use at most 192 MiB of HBM per device.

v0:
```python
import math

import jax
import jax.numpy as jnp
from jax import lax
from jax.sharding import PartitionSpec as P

HD = 64
FRAME_TOK = 56


def layer_stats(values):
    centered = values - jnp.mean(values, axis=-1, keepdims=True)
    inv_std = lax.rsqrt(jnp.mean(centered * centered, axis=-1, keepdims=True) + 1e-05)
    return (centered * inv_std, inv_std)


def norm_back(d_normed, normed_hat, inv_std, gain):
    scaled = d_normed * gain
    return inv_std * (
        scaled
        - jnp.mean(scaled, axis=-1, keepdims=True)
        - normed_hat * jnp.mean(scaled * normed_hat, axis=-1, keepdims=True)
    )


def shards(
    tokens,
    seq_counts,
    first_frame,
    norm1_gain,
    norm1_bias,
    qkv_weight,
    out_weight,
    out_bias,
    norm2_gain,
    norm2_bias,
    up_weight,
    up_bias,
    down_weight,
    down_bias,
    out_cotangent,
):
    seq_here = tokens.shape[1]
    rows_here = tokens.shape[0]
    length = rows_here * lax.axis_size("tensor")
    heads = out_weight.shape[0] // HD
    scale = 1.0 / math.sqrt(HD)
    live = (jnp.arange(seq_here, dtype=jnp.int32) < seq_counts[0]).astype(jnp.float32)[
        None, :, None
    ]
    residual_in = tokens.astype(jnp.float32)
    hat_one, inv_one = layer_stats(residual_in)
    a_one = (hat_one * norm1_gain + norm1_bias).astype(jnp.bfloat16)
    a_one = lax.all_gather(a_one, "tensor", axis=0, tiled=True)
    qkv = jnp.einsum("psd,de->pse", a_one, qkv_weight, preferred_element_type=jnp.float32).astype(
        jnp.bfloat16
    )
    qkv = qkv.reshape(length, seq_here, heads, 3, HD)
    queries = qkv[:, :, :, 0]
    keys = qkv[:, :, :, 1]
    values = qkv[:, :, :, 2]
    positions = jnp.arange(length, dtype=jnp.int32)
    causal = positions[None, :] <= positions[:, None]
    diagonal = positions[None, :] == positions[:, None]
    starts = (first_frame * FRAME_TOK)[:, None, None]
    allowed = (causal[None] & ((positions[None, None, :] >= starts) | diagonal[None]))[:, None]
    raw_scores = (
        jnp.einsum("pshe,qshe->shpq", queries, keys, preferred_element_type=jnp.float32) * scale
    )
    masked = jnp.where(allowed, raw_scores, -1e30)
    row_top = jnp.max(masked, axis=-1, keepdims=True)
    exponent = jnp.exp(masked - row_top)
    row_total = jnp.sum(exponent, axis=-1, keepdims=True)
    log_total = row_top + jnp.log(row_total)
    weights = (exponent / row_total).astype(jnp.bfloat16)
    attended = jnp.einsum("shpq,qshe->pshe", weights, values, preferred_element_type=jnp.float32)
    attended = attended.astype(jnp.bfloat16).reshape(length, seq_here, heads * HD)
    rows = attended
    attn = lax.psum_scatter(
        jnp.einsum("pse,ed->psd", rows, out_weight, preferred_element_type=jnp.float32).astype(
            jnp.bfloat16
        ),
        "tensor",
        scatter_dimension=0,
        tiled=True,
    ).astype(jnp.float32)
    after_attn = residual_in + attn + out_bias
    hat_two, inv_two = layer_stats(after_attn)
    a_two = (hat_two * norm2_gain + norm2_bias).astype(jnp.bfloat16)
    a_two = lax.all_gather(a_two, "tensor", axis=0, tiled=True)
    pre_act = (
        jnp.einsum("psd,df->psf", a_two, up_weight, preferred_element_type=jnp.float32) + up_bias
    )
    hidden = jax.nn.gelu(pre_act, approximate=True).astype(jnp.bfloat16)
    rows = hidden
    mlp = lax.psum_scatter(
        jnp.einsum("psf,fd->psd", rows, down_weight, preferred_element_type=jnp.float32).astype(
            jnp.bfloat16
        ),
        "tensor",
        scatter_dimension=0,
        tiled=True,
    ).astype(jnp.float32)
    block_output = (live * (after_attn + mlp + down_bias)).astype(jnp.bfloat16)
    grad_live = out_cotangent.astype(jnp.float32) * live
    grad_mlp = grad_live.astype(jnp.bfloat16)
    down_bias_grad = jnp.sum(grad_mlp.astype(jnp.float32), axis=(0, 1))
    d_mlp = lax.all_gather(grad_mlp, "tensor", axis=0, tiled=True)
    down_weight_grad = jnp.einsum("psf,psd->fd", hidden, d_mlp, preferred_element_type=jnp.float32)
    d_hidden = jnp.einsum("psd,fd->psf", d_mlp, down_weight, preferred_element_type=jnp.float32)
    _, gelu_pull = jax.vjp(lambda inner: jax.nn.gelu(inner, approximate=True), pre_act)
    d_pre = gelu_pull(d_hidden)[0].astype(jnp.bfloat16)
    up_bias_grad = jnp.sum(d_pre.astype(jnp.float32), axis=(0, 1))
    up_weight_grad = jnp.einsum("psd,psf->df", a_two, d_pre, preferred_element_type=jnp.float32)
    rows = d_pre
    d_norm_two = lax.psum_scatter(
        jnp.einsum("psf,df->psd", rows, up_weight, preferred_element_type=jnp.float32).astype(
            jnp.bfloat16
        ),
        "tensor",
        scatter_dimension=0,
        tiled=True,
    ).astype(jnp.float32)
    norm2_gain_grad = jnp.sum(d_norm_two * hat_two, axis=(0, 1))
    norm2_bias_grad = jnp.sum(d_norm_two, axis=(0, 1))
    d_after = grad_live + norm_back(d_norm_two, hat_two, inv_two, norm2_gain)
    grad_attn = d_after.astype(jnp.bfloat16)
    out_bias_grad = jnp.sum(grad_attn.astype(jnp.float32), axis=(0, 1))
    d_attn = lax.all_gather(grad_attn, "tensor", axis=0, tiled=True)
    out_weight_grad = jnp.einsum(
        "pse,psd->ed", attended, d_attn, preferred_element_type=jnp.float32
    )
    d_attended = jnp.einsum("psd,ed->pse", d_attn, out_weight, preferred_element_type=jnp.float32)
    d_attended = d_attended.astype(jnp.bfloat16).reshape(length, seq_here, heads, HD)
    again_scores = (
        jnp.einsum("pshe,qshe->shpq", queries, keys, preferred_element_type=jnp.float32) * scale
    )
    probs = jnp.exp(jnp.where(allowed, again_scores, -1e30) - log_total)
    d_probs = jnp.einsum("pshe,qshe->shpq", d_attended, values, preferred_element_type=jnp.float32)
    d_values = jnp.einsum(
        "shpq,pshe->qshe",
        probs.astype(jnp.bfloat16),
        d_attended,
        preferred_element_type=jnp.float32,
    )
    d_scores = probs * (d_probs - jnp.sum(probs * d_probs, axis=-1, keepdims=True))
    d_scores = d_scores.astype(jnp.bfloat16)
    d_queries = (
        jnp.einsum("shpq,qshe->pshe", d_scores, keys, preferred_element_type=jnp.float32) * scale
    )
    d_keys = (
        jnp.einsum("shpq,pshe->qshe", d_scores, queries, preferred_element_type=jnp.float32) * scale
    )
    d_qkv = jnp.stack([d_queries, d_keys, d_values], axis=3).astype(jnp.bfloat16)
    d_qkv = d_qkv.reshape(length, seq_here, heads * 3 * HD)
    qkv_weight_grad = jnp.einsum("psd,pse->de", a_one, d_qkv, preferred_element_type=jnp.float32)
    rows = d_qkv
    d_norm_one = lax.psum_scatter(
        jnp.einsum("pse,de->psd", rows, qkv_weight, preferred_element_type=jnp.float32).astype(
            jnp.bfloat16
        ),
        "tensor",
        scatter_dimension=0,
        tiled=True,
    ).astype(jnp.float32)
    norm1_gain_grad = jnp.sum(d_norm_one * hat_one, axis=(0, 1))
    norm1_bias_grad = jnp.sum(d_norm_one, axis=(0, 1))
    input_grad = (d_after + norm_back(d_norm_one, hat_one, inv_one, norm1_gain)).astype(
        jnp.bfloat16
    )
    (
        norm1_gain_grad,
        norm1_bias_grad,
        norm2_gain_grad,
        norm2_bias_grad,
        out_bias_grad,
        down_bias_grad,
    ) = lax.psum(
        (
            norm1_gain_grad,
            norm1_bias_grad,
            norm2_gain_grad,
            norm2_bias_grad,
            out_bias_grad,
            down_bias_grad,
        ),
        ("dp", "tensor"),
    )
    qkv_weight_grad, out_weight_grad, up_weight_grad, down_weight_grad, up_bias_grad = lax.psum(
        (qkv_weight_grad, out_weight_grad, up_weight_grad, down_weight_grad, up_bias_grad), "dp"
    )
    return (
        block_output,
        input_grad,
        qkv_weight_grad,
        out_weight_grad,
        up_weight_grad,
        down_weight_grad,
        up_bias_grad,
        out_bias_grad,
        down_bias_grad,
        norm1_gain_grad,
        norm1_bias_grad,
        norm2_gain_grad,
        norm2_bias_grad,
    )


def solution(mesh):
    return jax.shard_map(
        shards,
        mesh=mesh,
        in_specs=(
            P("tensor", "dp", None),
            P("dp"),
            P("dp"),
            P(),
            P(),
            P(None, "tensor"),
            P("tensor", None),
            P(),
            P(),
            P(),
            P(None, "tensor"),
            P("tensor"),
            P("tensor", None),
            P(),
            P("tensor", "dp", None),
        ),
        out_specs=(
            P("tensor", "dp", None),
            P("tensor", "dp", None),
            P(None, "tensor"),
            P("tensor", None),
            P(None, "tensor"),
            P("tensor", None),
            P("tensor"),
            P(),
            P(),
            P(),
            P(),
            P(),
            P(),
        ),
        check_vma=False,
    )
```

profile of v0, /device:TPU:0, one launch (start us, length us, event | category | flops | bytes accessed | tf_op | source)
XLA Modules:
  0.0 773.2 jit_solution(13719573942419904953)
XLA Ops:
  7.3 1.7 convert_reduce_fusion.3
  9.0 2.0 fusion.44
  11.0 2.6 fusion.39
  13.8 2.5 or_and_fusion
  16.3 42.1 %all-gather.5.cloned.1.call-done = bf16[336,12,512]{2,1,0:T(8,128)(2,1)} async-done(((bf16[84,12,512]{2,1,0:T(8,128)(2,1)}), bf16[336,12,512]{2,1,0:T(8,128)(2,1)}) %all-gather.5.cloned.1.call-update) | async-done | bytes 4128784 | tf_op jit(solution)/shard_map/all_gather | solution.py:55
  58.4 9.3 %fusion.54 = bf16[336,12,384]{2,0,1:T(8,128)(2,1)} fusion(bf16[336,12,512]{2,1,0:T(8,128)(2,1)} %all-gather.5.cloned.1.call-done, bf16[512,384]{1,0:T(8,128)(2,1)S(1)} %copy-done.17), kind=kOutput, calls=%fused_computation.87 | convolution fusion | flops 1586995200 | bytes 7618560 | tf_op jit(solution)/shard_map/psd,de->pse/dot_general | solution.py:56
  67.7 6.0 copy.55
  73.7 4.9 fusion.94
  78.6 2.1 fusion
  80.8 2.4 copy-done.2
  83.1 3.8 fusion.57
  86.9 1.0 copy-done.12
  88.0 3.2 convolution_convert_fusion.3
  91.2 0.6 copy-done.28
  91.8 0.6 dynamic-slice
  93.1 82.7 %all-reduce.12.cloned.1.call-done = bf16[336,12,512]{2,0,1:T(8,128)(2,1)} async-done(((bf16[336,12,512]{2,0,1:T(8,128)(2,1)}), bf16[336,12,512]{2,0,1:T(8,128)(2,1)}) %all-reduce.12.cloned.1.call-update) | async-done | bytes 4128784
  175.8 1.5 constant_dynamic-slice_fusion.3
  177.3 0.7 fusion.82
  178.1 1.1 multiply_reduce_fusion.1
  179.2 3.2 add_convert_fusion
  182.4 0.4 all-gather.9.cloned.1.call-start
  183.6 2.9 convert_reduce_fusion.4
  186.5 38.2 %all-gather.7.cloned.1.call-done = bf16[336,12,512]{2,1,0:T(8,128)(2,1)} async-done(((bf16[84,12,512]{2,1,0:T(8,128)(2,1)}), bf16[336,12,512]{2,1,0:T(8,128)(2,1)}) %all-gather.7.cloned.1.call-update) | async-done | bytes 4128784 | tf_op jit(solution)/shard_map/all_gather | solution.py:91
  224.7 11.8 %fusion.32 = f32[336,12,512]{2,0,1:T(8,128)} fusion(bf16[336,12,512]{2,1,0:T(8,128)(2,1)} %all-gather.7.cloned.1.call-done, bf16[512,512]{1,0:T(8,128)(2,1)S(1)} %copy-done.16), kind=kOutput, calls=%fused_computation.52 | convolution fusion | flops 2113929216 | bytes 12910592 | tf_op jit(solution)/shard_map/psd,df->psf/dot_general | solution.py:93
  236.4 31.7 %all-gather.9.cloned.1.call-done = bf16[336,12,512]{2,1,0:T(8,128)(2,1)} async-done(((bf16[84,12,512]{2,1,0:T(8,128)(2,1)}), bf16[336,12,512]{2,1,0:T(8,128)(2,1)}) %all-gather.9.cloned.1.call-update) | async-done | bytes 4128784 | tf_op jit(solution)/shard_map/all_gather | solution.py:109
  268.1 14.3 %convert_reduce_fusion = (f32[512]{0:T(512)S(1)}, bf16[336,12,512]{2,0,1:T(8,128)(2,1)S(1)}) fusion(f32[336,12,512]{2,0,1:T(8,128)} %fusion.32, f32[512]{0:T(512)S(1)} %copy-done.26, bf16[512,512]{1,0:T(8,128)(2,1)S(1)} %copy-done, bf16[336,12,512]{2,1,0:T(8,128)(2,1)} %all-gather.9.cloned.1.call-done), kind=kOutput, calls=%fused_computation.17 | convolution fusion | flops 2161409536 | bytes 17043456 | tf_op jit(solution)/shard_map/psd,fd->psf/dot_general | solution.py:111
  282.4 1.9 copy-done.29
  284.3 4.5 convolution_convert_fusion.1
  288.9 84.5 %all-reduce.14.cloned.1.call-done = bf16[336,12,512]{2,0,1:T(8,128)(2,1)} async-done(((bf16[336,12,512]{2,0,1:T(8,128)(2,1)}), bf16[336,12,512]{2,0,1:T(8,128)(2,1)}) %all-reduce.14.cloned.1.call-update) | async-done | bytes 4128784
  373.4 1.6 constant_dynamic-slice_fusion.1
  375.0 4.8 fusion.51
  379.8 5.5 convert_reduce_fusion.5
  385.4 8.7 %convolution_convert_fusion.2 = bf16[336,12,512]{2,0,1:T(8,128)(2,1)} fusion(bf16[512,512]{1,0:T(8,128)(2,1)S(1)} %copy-done, f32[336,12,512]{2,0,1:T(8,128)} %fusion.32, f32[512]{0:T(512)S(1)} %copy-done.26), kind=kOutput, calls=%fused_computation.82 | convolution fusion | flops 2136637440 | bytes 12912640 | tf_op jit(solution)/shard_map/psf,fd->psd/dot_general | solution.py:98
  394.2 33.4 %all-gather.11.cloned.1.call-done = bf16[336,12,512]{2,1,0:T(8,128)(2,1)} async-done(((bf16[84,12,512]{2,1,0:T(8,128)(2,1)}), bf16[336,12,512]{2,1,0:T(8,128)(2,1)}) %all-gather.11.cloned.1.call-update) | async-done | bytes 4128784 | tf_op jit(solution)/shard_map/all_gather | solution.py:130
  427.5 8.2 %fusion.61 = bf16[336,12,128]{2,0,1:T(8,128)(2,1)} fusion(bf16[336,12,512]{2,1,0:T(8,128)(2,1)} %all-gather.11.cloned.1.call-done, bf16[128,512]{1,0:T(8,128)(2,1)S(1)} %copy-done.20), kind=kOutput, calls=%fused_computation.90 | convolution fusion | flops 528998400 | bytes 5292032 | tf_op jit(solution)/shard_map/psd,ed->pse/dot_general | solution.py:134
  435.7 2.6 copy.68
  438.3 7.0 fusion.66
  445.4 9.4 %multiply_reduce_fusion = (f32[12,2,336]{2,1,0:T(2,128)S(1)}, f32[12,2,336,336]{2,3,1,0:T(8,128)}) fusion(f32[12,2,336,336]{2,3,1,0:T(8,128)} %copy-done.2, f32[12,2,336]{2,1,0:T(2,128)S(1)} %bitcast.110, bf16[336,12,2,64]{0,3,2,1:T(8,128)(2,1)S(1)} %bitcast.106, bf16[336,12,2,3,64]{0,4,3,2,1:T(8,128)(2,1)S(1)} %bitcast.100), kind=kOutput, calls=%fused_computation.1 | convolution fusion | flops 354936960 | bytes 24104448 | tf_op jit(solution)/shard_map/pshe,qshe->shpq/dot_general | solution.py:140
  454.8 6.3 multiply_convert_fusion
  461.1 2.0 fusion.65
  463.1 1.2 fusion.64
  464.3 0.8 pad_maximum_fusion
  465.1 0.5 copy.72
  465.7 1.8 copy-done.7
  467.5 4.8 convolution_convert_fusion
  472.3 0.4 all-reduce.16.cloned.1.call-start
  472.8 13.4 %fusion.69 = f32[512,512]{1,0:T(8,128)} fusion(bf16[336,12,512]{2,0,1:T(8,128)(2,1)} %copy-done.29, bf16[336,12,512]{2,1,0:T(8,128)(2,1)} %all-gather.7.cloned.1.call-done), kind=kOutput, calls=%fused_computation.94 | convolution fusion | flops 2113929216 | bytes 9306112 | tf_op jit(solution)/shard_map/psd,psf->df/dot_general | solution.py:115
  486.2 13.6 %fusion.72 = f32[512,512]{1,0:T(8,128)} fusion(bf16[336,12,512]{2,1,0:T(8,128)(2,1)} %all-gather.9.cloned.1.call-done, f32[336,12,512]{2,0,1:T(8,128)} %fusion.32, f32[512]{0:T(512)S(1)} %copy-done.26), kind=kOutput, calls=%fused_computation.95 | convolution fusion | flops 2134573056 | bytes 13436928 | tf_op jit(solution)/shard_map/psf,psd->fd/dot_general | solution.py:110
  499.8 5.3 fusion.78
  505.1 9.6 %fusion.75 = f32[512,384]{1,0:T(8,128)} fusion(bf16[336,12,384]{0,2,1:T(8,128)(2,1)S(1)} %bitcast.104, bf16[336,12,512]{2,1,0:T(8,128)(2,1)S(1)} %bitcast.115), kind=kOutput, calls=%fused_computation.96 | convolution fusion | flops 1585446912 | bytes 8011776 | tf_op jit(solution)/shard_map/psd,pse->de/dot_general | solution.py:157
  514.8 21.9 %psum.81 = f32[512]{0:T(512)} all-reduce(f32[512]{0:T(512)S(1)} %get-tuple-element.56), channel_id=1, replica_groups=mesh['dp'=8,'tensor'=4] {'dp'}, use_global_device_ids=true, to_apply=%region_20.21 | all-reduce | flops 512 | bytes 4096 | tf_op jit(solution)/shard_map/psum | solution.py:190
  536.7 86.9 %all-reduce.18.cloned.1.call-done = (bf16[336,12,512]{2,0,1:T(8,128)(2,1)}, bf16[336,12,512]{2,0,1:T(8,128)(2,1)}) async-done(((bf16[336,12,512]{2,0,1:T(8,128)(2,1)}, bf16[336,12,512]{2,0,1:T(8,128)(2,1)}), (bf16[336,12,512]{2,0,1:T(8,128)(2,1)}, bf16[336,12,512]{2,0,1:T(8,128)(2,1)})) %all-reduce.18.cloned.1.call-update) | async-done | bytes 8257552
  623.6 1.5 constant_dynamic-slice_fusion.2
  625.1 1.7 constant_dynamic-slice_fusion
  626.9 3.6 fusion.52
  630.6 7.3 fusion.43
  637.9 1.6 copy.82
  639.4 1.5 copy.81
  641.0 42.2 %all-reduce.4 = (f32[512]{0:T(512)}, f32[512]{0:T(512)}, f32[512]{0:T(512)}, f32[512]{0:T(512)}, f32[512]{0:T(512)}, /*index=5*/f32[512]{0:T(512)}) all-reduce(f32[512]{0:T(512)S(1)} %get-tuple-element.48, f32[512]{0:T(512)S(1)} %get-tuple-element.46, ...), channel_id=1, replica_groups=mesh['dp'=8,'tensor'=4] {'dp','tensor'}, use_global_device_ids=true, to_apply=%region_22.23 | all-reduce | flops 3072 | bytes 24576 | tf_op jit(solution)/shard_map/psum | solution.py:179
  683.1 77.2 %all-reduce.16.cloned.1.call-done = (f32[512,384]{1,0:T(8,128)}, f32[128,512]{1,0:T(8,128)}, f32[512,512]{1,0:T(8,128)}, f32[512,512]{1,0:T(8,128)}) async-done(((f32[512,384]{1,0:T(8,128)}, f32[128,512]{1,0:T(8,128)}, f32[512,512]{1,0:T(8,128)}, f32[512,512]{1,0:T(8,128)}), (f32[512,384]{1,0:T(8,128)}, f32[128,512]{1,0:T(8,128)}, f32[512,512]{1,0:T(8,128)}, ...) | async-done | bytes 3145744 | tf_op jit(solution)/shard_map/psum | solution.py:190
  760.3 2.2 copy.211
  762.5 1.7 copy.212
  764.2 1.0 copy.213
  765.2 1.0 copy.214
  (99 shorter events, 0.8 us)
Async XLA Ops:
  7.2 260.9 %copy-start = (bf16[512,512]{1,0:T(8,128)(2,1)S(1)}, bf16[512,512]{1,0:T(8,128)(2,1)}, u32[]{:S(2)}) copy-start(bf16[512,512]{1,0:T(8,128)(2,1)} %param.27) | copy-start | bytes 1572868
  7.2 3.8 copy-start.3
  7.2 51.2 %all-gather.5.cloned.1.call-start = ((), (), s32[]{:S(2)}) async-start(), calls=%async_computation | async-start | bytes 6881280 | tf_op jit(solution)/shard_map/all_gather | solution.py:55
  9.0 4.7 copy-start.27
  11.0 47.4 %copy-start.17 = (bf16[512,384]{1,0:T(8,128)(2,1)S(1)}, bf16[512,384]{1,0:T(8,128)(2,1)}, u32[]{:S(2)}) copy-start(bf16[512,384]{1,0:T(8,128)(2,1)} %param.20) | copy-start | bytes 1179652
  13.6 162.2 %all-reduce.12.cloned.1.call-start = ((), (), s32[]{:S(2)}) async-start(), calls=%async_computation.4 | async-start | bytes 8257536
  78.6 4.5 copy-start.2
  83.1 4.8 copy-start.19
  86.9 1.1 copy-start.12
  91.2 0.7 copy-start.28
  91.2 86.1 %copy-start.21 = (f32[512]{0:T(512)S(1)}, f32[512]{0:T(512)}, u32[]{:S(2)}) copy-start(f32[512]{0:T(512)} %param.22) | copy-start | bytes 6148
  91.2 133.5 %all-gather.7.cloned.1.call-start = ((), (), s32[]{:S(2)}) async-start(), calls=%async_computation.1 | async-start | bytes 6881280 | tf_op jit(solution)/shard_map/all_gather | solution.py:91
  177.3 1.9 copy-start.22
  177.3 1.9 copy-start.24
  182.4 42.2 %copy-start.16 = (bf16[512,512]{1,0:T(8,128)(2,1)S(1)}, bf16[512,512]{1,0:T(8,128)(2,1)}, u32[]{:S(2)}) copy-start(bf16[512,512]{1,0:T(8,128)(2,1)} %param.25) | copy-start | bytes 1572868
  182.4 85.7 %all-gather.9.cloned.1.call-start = ((), (), s32[]{:S(2)}) async-start(), calls=%async_computation.2 | async-start | bytes 6881280 | tf_op jit(solution)/shard_map/all_gather | solution.py:109
  186.4 81.7 %copy-start.26 = (f32[512]{0:T(512)S(1)}, f32[512]{0:T(512)}, u32[]{:S(2)}) copy-start(f32[512]{0:T(512)} %param.26) | copy-start | bytes 6148
  186.5 186.9 %all-reduce.14.cloned.1.call-start = ((), (), s32[]{:S(2)}) async-start(), calls=%async_computation.5 | async-start | bytes 8257536
  282.4 1.9 copy-start.29
  288.8 138.7 %all-gather.11.cloned.1.call-start = ((), (), s32[]{:S(2)}) async-start(), calls=%async_computation.3 | async-start | bytes 6881280 | tf_op jit(solution)/shard_map/all_gather | solution.py:130
  373.4 6.4 copy-start.10
  375.0 10.3 %copy-start.5 = (bf16[84,12,512]{2,0,1:T(8,128)(2,1)}, bf16[84,12,512]{2,0,1:T(8,128)(2,1)S(1)}, u32[]{:S(2)}) copy-start(bf16[84,12,512]{2,0,1:T(8,128)(2,1)S(1)} %constant_dynamic-slice_fusion.1) | copy-start | bytes 3096580
  385.3 238.2 %all-reduce.18.cloned.1.call-start = ((), (), s32[]{:S(2)}) async-start(), calls=%async_computation.7 | async-start | bytes 16515072
  385.4 42.1 %copy-start.20 = (bf16[128,512]{1,0:T(8,128)(2,1)S(1)}, bf16[128,512]{1,0:T(8,128)(2,1)}, u32[]{:S(2)}) copy-start(bf16[128,512]{1,0:T(8,128)(2,1)} %param.21) | copy-start | bytes 393220
  438.3 7.0 copy-start.4
  438.3 7.0 copy-start.9
  438.3 16.4 %slice-start = ((s8[12386304]{0:T(1024)(128)(4,1)}), s8[4194304]{0:T(1024)(128)(4,1)S(1)}, s32[]{:S(2)}) async-start(s8[12386304]{0:T(1024)(128)(4,1)} %bitcast.96), calls=%async_computation.8 | async-start | bytes 8388608
  438.3 16.4 %slice-start.1 = ((s8[12386304]{0:T(1024)(128)(4,1)}), s8[4194304]{0:T(1024)(128)(4,1)S(1)}, s32[]{:S(2)}) async-start(s8[12386304]{0:T(1024)(128)(4,1)} %bitcast.96), calls=%async_computation.9 | async-start | bytes 8388608
  445.3 9.4 %slice-start.2 = ((s8[12386304]{0:T(1024)(128)(4,1)}), s8[3997696]{0:T(1024)(128)(4,1)S(1)}, s32[]{:S(2)}) async-start(s8[12386304]{0:T(1024)(128)(4,1)} %bitcast.96), calls=%async_computation.10 | async-start | bytes 7995392
  465.1 2.3 copy-start.18
  465.7 1.8 copy-start.7
  472.3 288.0 %all-reduce.16.cloned.1.call-start = ((), (), s32[]{:S(2)}) async-start(), calls=%async_computation.6 | async-start | bytes 6291456 | tf_op jit(solution)/shard_map/psum | solution.py:190
  472.8 27.0 %slice-start.5 = ((s8[5505024]{0:T(1024)(128)(4,1)}), s8[4194304]{0:T(1024)(128)(4,1)S(1)}, s32[]{:S(2)}) async-start(s8[5505024]{0:T(1024)(128)(4,1)} %bitcast.116), calls=%async_computation.13 | async-start | bytes 8388608
  472.8 32.4 %slice-start.3 = ((s8[5505024]{0:T(1024)(128)(4,1)}), s8[4194304]{0:T(1024)(128)(4,1)S(1)}, s32[]{:S(2)}) async-start(s8[5505024]{0:T(1024)(128)(4,1)} %bitcast.114), calls=%async_computation.11 | async-start | bytes 8388608
  486.1 13.6 %copy-start.13 = (bf16[12,2,64,336]{3,2,1,0:T(8,128)(2,1)S(1)}, bf16[12,2,64,336]{3,2,1,0:T(8,128)(2,1)}, u32[]{:S(2)}) copy-start(bf16[12,2,64,336]{3,2,1,0:T(8,128)(2,1)} %copy-done.12) | copy-start | bytes 3096580
  486.2 13.6 %slice-start.6 = ((s8[5505024]{0:T(1024)(128)(4,1)}), s8[1310720]{0:T(1024)(128)(4,1)S(1)}, s32[]{:S(2)}) async-start(s8[5505024]{0:T(1024)(128)(4,1)} %bitcast.116), calls=%async_computation.14 | async-start | bytes 2621440
  486.2 19.0 %slice-start.4 = ((s8[5505024]{0:T(1024)(128)(4,1)}), s8[1310720]{0:T(1024)(128)(4,1)S(1)}, s32[]{:S(2)}) async-start(s8[5505024]{0:T(1024)(128)(4,1)} %bitcast.114), calls=%async_computation.12 | async-start | bytes 2621440
  499.8 5.4 copy-start.8
  514.8 112.1 %copy-start.23 = (f32[512]{0:T(512)S(1)}, f32[512]{0:T(512)}, u32[]{:S(2)}) copy-start(f32[512]{0:T(512)} %param.18) | copy-start | bytes 6148
  625.1 5.4 copy-start.6
  625.1 5.4 copy-start.11
  625.1 5.4 copy-start.25
  760.3 3.9 copy-start.15
  760.3 4.9 copy-start.14
  760.3 5.8 copy-start.1
Sparse Core Ops, SparseCore 0:
  13.7 44.6 all-gather.4
  91.3 84.4 all-reduce.11
  182.6 42.0 all-gather.6
  226.2 41.9 all-gather.8
  288.9 84.4 all-reduce.13
  385.4 42.0 all-gather.10
  472.4 151.1 all-reduce.17
  628.5 131.7 all-reduce.15
where the time goes:
time: 780 us; the launch traced here: 773 us
  waiting for transfers between devices  477 us (61%)
  matrix products  135 us (17%)
  blocking collectives  64.1 us (8%)
  other arithmetic  47.2 us (6%)
  local copies, waits for them, and re-layouts  32.9 us (4%)
  between operations  16.3 us (2%)
    unnamed x11, waiting for transfers between devices  254 us
    psum x1, waiting for transfers between devices, shards(): lax.psum((qkv_weight_grad, out_weight_grad, up_weight_grad, down_weight_g...  77.2 us
    psum x1, blocking collectives, shards(): lax.psum((norm1_gain_grad, norm1_bias_grad, norm2_gain_grad, norm2_bias_g...  42.2 us
    all_gather x1, waiting for transfers between devices, shards(): a_one = lax.all_gather(a_one, 'tensor', axis=0, tiled=True)  42.1 us
    all_gather x1, waiting for transfers between devices, shards(): a_two = lax.all_gather(a_two, 'tensor', axis=0, tiled=True)  38.2 us
    all_gather x1, waiting for transfers between devices, shards(): d_attn = lax.all_gather(grad_attn, 'tensor', axis=0, tiled=True)  33.4 us
    all_gather x1, waiting for transfers between devices, shards(): d_mlp = lax.all_gather(grad_mlp, 'tensor', axis=0, tiled=True)  31.7 us
    unnamed x85, local copies, waits for them, and re-layouts  23.8 us
  transfers between devices with their start and end apart: 8, of which 8 were waited for; matrix products, arithmetic and copies ran while one was open for 11% of the time, Pallas kernels for 0%

commit v1 on v0

v1 whole, which is shorter than its diff:
```python
import functools
import math

import jax
import jax.numpy as jnp
from jax import lax
from jax.experimental import pallas as pl
from jax.experimental.pallas import tpu as pltpu
from jax.sharding import PartitionSpec as P

HD = 64
FRAME_TOK = 56
BF16 = jnp.bfloat16
F32 = jnp.float32
NN = (((1,), (0,)), ((), ()))
NT = (((1,), (1,)), ((), ()))
TN = (((0,), (0,)), ((), ()))
GELU_A = 0.7978845608
GELU_B = 0.044715
VMEM_LIMIT = 56 << 20


def dot(a, b, dims=NN):
    return lax.dot_general(a, b, dims, preferred_element_type=F32)


def stats(x):
    c = x - jnp.mean(x, axis=-1, keepdims=True)
    inv = lax.rsqrt(jnp.mean(c * c, axis=-1, keepdims=True) + 1e-5)
    return c * inv, inv


def norm_back(d, hat, inv, gain):
    e = d * gain
    return inv * (
        e - jnp.mean(e, axis=-1, keepdims=True) - hat * jnp.mean(e * hat, axis=-1, keepdims=True)
    )


def full(a):
    return pl.BlockSpec(a.shape, lambda *_: (0,) * len(a.shape))


def struct(shape, dtype):
    return jax.ShapeDtypeStruct(shape, dtype)


def call(kernel, scalars, args, out_shape, grid=(1,), in_specs=None, out_specs=None, scratch=(), flops=0, name=None, aliases=None):
    in_specs = [full(a) for a in args] if in_specs is None else in_specs
    out_specs = [full(o) for o in out_shape] if out_specs is None else out_specs
    moved = sum(math.prod(a.shape) * a.dtype.itemsize for a in (*args, *out_shape))
    return pl.pallas_call(
        kernel,
        grid_spec=pltpu.PrefetchScalarGridSpec(
            num_scalar_prefetch=len(scalars),
            grid=grid,
            in_specs=in_specs,
            out_specs=out_specs,
            scratch_shapes=list(scratch),
        ),
        out_shape=list(out_shape),
        compiler_params=pltpu.CompilerParams(vmem_limit_bytes=VMEM_LIMIT),
        cost_estimate=pl.CostEstimate(flops=flops, bytes_accessed=moved, transcendentals=0),
        name=name,
        input_output_aliases=aliases or {},
    )(*scalars, *args)


def pack_kernel(wqkv_ref, wout_ref, ub_ref, w_ref):
    d = wout_ref.shape[1]
    half = d // 2
    ub = ub_ref[...]
    high = ub.astype(BF16).astype(F32)
    row = lax.broadcasted_iota(jnp.int32, (16, d), 0)
    ub = jnp.where(row == 0, high, jnp.where(row == 1, ub - high, 0.0)).astype(BF16)
    side = wout_ref.shape[0]
    for h in range(2):
        here = pl.ds(h * half, half)
        a, b, c = (wqkv_ref[here, pl.ds(128 * j, 128)].astype(F32) for j in range(3))
        low = lax.broadcasted_iota(jnp.int32, a.shape, 1) < HD
        w_ref[h, 0:half, 0:128] = jnp.where(low, a, b).astype(BF16)
        w_ref[h, 0:half, 128:256] = pltpu.roll(jnp.where(low, c, a), HD, 1).astype(BF16)
        w_ref[h, 0:half, 256:384] = jnp.where(low, b, c).astype(BF16)
        for j in range(half // side):
            w_ref[h, pl.ds(j * side, side), 384:512] = wout_ref[:, pl.ds(h * half + 128 * j, 128)]
        w_ref[h, half:half + 16, :] = ub


def pack(wqkv, wout, ub):
    d = wqkv.shape[0]
    return call(pack_kernel, (), (wqkv, wout, ub), [struct((2, d // 2 + 16, d), BF16)], name="pack_weights")[0]


def place_kernel(me_ref, b0, b1, b2, b3, out_ref):
    each = b0.shape[0]
    for k, b in enumerate((b0, b1, b2, b3)):
        out_ref[pl.ds((me_ref[0] ^ k) * each, each)] = b[...]


def place(me, blocks):
    each, rows, d = blocks[0].shape
    return call(place_kernel, (me,), blocks, [struct((4 * each, rows, d), BF16)], name="place")[0]


def attn_fwd_kernel(me_ref, bit_ref, ff_ref, t0, t1, t2, t3, w0, w1, w2a, w2b, w3a, w3b,
                    g1_ref, b1_ref, bo_ref, g2_ref, b2_ref,
                    qkv_ref, p_ref, o_ref, x_ref, y1_ref, a1_ref, a2_ref, wq_ref, wo_ref, ub_ref,
                    blk_sc, bias_sc):
    s = pl.program_id(0)
    _, rows, d = t0.shape
    length = 4 * rows
    me = me_ref[0]

    @pl.when(s == 0)
    def _():
        bit = bit_ref[0]
        half = d // 2
        for k, parts in enumerate((
            ((0, w0.at[0]), (half, w0.at[1])),
            ((0, w1.at[0]), (half, w1.at[1])),
            ((pl.multiple_of(bit * half, half), w2a), (pl.multiple_of((1 - bit) * half, half), w2b)),
            ((pl.multiple_of(bit * half, half), w3a), (pl.multiple_of((1 - bit) * half, half), w3b)),
        )):
            for at, w in parts:
                wq_ref[pl.ds(at, half), pl.ds(384 * k, 384)] = w[0:half, 0:384]
                for j in range(half // 128):
                    lane = pl.multiple_of(at + 128 * j, 128)
                    wo_ref[pl.ds(128 * k, 128), pl.ds(lane, 128)] = w[pl.ds(128 * j, 128), 384:512]
            ub = parts[0][1][half:half + 16, :].astype(F32)
            ub_ref[k] = jnp.broadcast_to(ub[0:1] + ub[1:2], ub_ref.shape[1:])

    for k, t in enumerate((t0, t1, t2, t3)):
        blk_sc[me ^ k] = t[0].astype(F32)
    for i in range(4):
        x_ref[0, pl.ds(i * rows, rows), :] = blk_sc[i]
    hat, _ = stats(x_ref[0])
    a1 = (hat * g1_ref[...] + b1_ref[...]).astype(BF16)
    a1_ref[0] = a1
    qkv_ref[0] = dot(a1, wq_ref[...]).astype(BF16)
    start = ff_ref[me * pl.num_programs(0) + s] * FRAME_TOK
    jj = lax.broadcasted_iota(jnp.int32, (length, length), 0)
    ii = lax.broadcasted_iota(jnp.int32, (length, length), 1)
    bias_sc[...] = jnp.where((jj <= ii) & ((jj >= start) | (jj == ii)), 0.0, -1e30)
    lane = lax.broadcasted_iota(jnp.int32, (length, 128), 1)
    for p in range(4):
        q = qkv_ref[0, :, pl.ds(p * 384, 128)]
        k = qkv_ref[0, :, pl.ds(p * 384 + 128, 128)]
        v = qkv_ref[0, :, pl.ds(p * 384 + 256, 128)]
        acc = None
        for h in range(2):
            mine = (lane < HD) if h == 0 else (lane >= HD)
            kh = jnp.where(mine, k, jnp.zeros_like(k))
            vh = jnp.where(mine, v, jnp.zeros_like(v))
            st = dot(kh, q, NT) * (HD ** -0.5) + bias_sc[...]
            e = jnp.exp(st - jnp.max(st, axis=0, keepdims=True))
            prob = (e * (1.0 / jnp.sum(e, axis=0, keepdims=True))).astype(BF16)
            p_ref[0, 2 * p + h] = prob
            part = dot(prob, vh, TN)
            acc = part if acc is None else acc + part
        o_ref[0, :, pl.ds(p * 128, 128)] = acc.astype(BF16)
    y1 = x_ref[0] + dot(o_ref[0], wo_ref[...]) + bo_ref[...]
    y1_ref[0] = y1
    hat, _ = stats(y1)
    a2_ref[0] = (hat * g2_ref[...] + b2_ref[...]).astype(BF16)


def per_seq(a):
    return pl.BlockSpec((1, *a.shape[1:]), lambda s, *_: (s,) + (0,) * (len(a.shape) - 1))


def attn_fwd(me, bit, ff, t, w, g1, b1, bo, g2, b2):
    seqs, rows, d = t[0].shape
    length = 4 * rows
    small = (g1, b1, bo, g2, b2)
    outs = [
        struct((seqs, length, 3 * d), BF16),
        struct((seqs, 8, length, length), BF16),
        struct((seqs, length, d), BF16),
        struct((seqs, length, d), F32),
        struct((seqs, length, d), F32),
        struct((seqs, length, d), BF16),
        struct((seqs, length, d), BF16),
    ]
    weights = [struct((d, 3 * d), BF16), struct((d, d), BF16), struct((4, 8, d), F32)]
    return call(
        attn_fwd_kernel, (me, bit, ff), (*t, *w, *small), outs + weights, grid=(seqs,),
        in_specs=[per_seq(a) for a in t] + [full(a) for a in (*w, *small)],
        out_specs=[per_seq(o) for o in outs] + [full(o) for o in weights],
        scratch=[pltpu.VMEM((4, rows, d), F32), pltpu.VMEM((length, length), F32)],
        flops=2 * seqs * length * (4 * d * d + 2 * d * length), name="attention_forward")


def ff_kernel(first, me_ref, bit_ref, live_ref, *refs):
    blocks = (3, 1) if first else (2, 0)
    refs = list(refs)
    take = lambda n: [refs.pop(0) for _ in range(n)]
    weights = take(4)
    ub_ref, a2_ref = take(2)
    if first:
        cots = take(4)
    else:
        gm_ref, recv_ref = take(2)
    take(1)
    hm_ref, du_ref, g_ref, w_ref = take(4)
    if first:
        (gm_ref,) = take(1)
    wbuf, sems = take(2)
    c = pl.program_id(0)
    seqs, length, d = a2_ref.shape
    total = seqs * length
    rows = length // 4
    bit = bit_ref[0]
    copies = []
    for n, k in enumerate(blocks):
        at = (bit, 1 - bit) if k >= 2 else (0, 1)
        copies.append([
            pltpu.make_async_copy(weights[2 * n + m], wbuf.at[n, at[m]], sems.at[n, m]) for m in range(2)])
    out_copy = pltpu.make_async_copy(wbuf, w_ref, sems.at[0, 0])

    @pl.when(c == 0)
    def _():
        for group in copies:
            for cp in group:
                cp.start()
        if first:
            blk_sc, gy_sc = refs
            for s in range(seqs):
                live = live_ref[s] > 0
                for k, cot in enumerate(cots):
                    blk_sc[me_ref[0] ^ k] = jnp.where(live, cot[s].astype(F32), 0.0)
                for i in range(4):
                    gy_sc[pl.ds(i * rows, rows), :] = blk_sc[i]
                gm_ref[s] = gy_sc[...].astype(BF16)

    for n, group in enumerate(copies):
        @pl.when(c == n)
        def _():
            for cp in group:
                cp.wait()

    @pl.when(c == 1)
    def _():
        out_copy.start()

    up = wbuf[c, 0]
    dn = wbuf[c, 1]
    ub = ub_ref[jnp.where(c == 0, blocks[0], blocks[1]), 0:1]
    ubg = jnp.zeros((8, d), F32)
    for s in range(seqs):
        here = pl.ds(s * length, length)
        pre = dot(a2_ref[s], up) + ub
        dh = dot(gm_ref[s], dn, NT)
        sq = pre * pre
        t = jnp.tanh(pre * (GELU_A + (GELU_A * GELU_B) * sq))
        ht = 0.5 * t + 0.5
        slope = ht + (ht - ht * ht) * (pre * ((2 * GELU_A) + (6.0 * GELU_A * GELU_B) * sq))
        hm_ref[here, :] = (pre * ht).astype(BF16)
        du = (dh * slope).astype(BF16)
        du_ref[here, :] = du
        ubg += jnp.sum(du.astype(F32).reshape(length // 8, 8, d), axis=0)
    upg = dot(a2_ref[...].reshape(total, d), du_ref[...], TN)
    dng = dot(gm_ref[...].reshape(total, d), hm_ref[...], TN)
    ubg = jnp.sum(ubg, axis=0, keepdims=True)
    extra = jnp.where(lax.broadcasted_iota(jnp.int32, (64, d), 0) == 0, ubg, 0.0)
    if not first:
        upg += recv_ref[0, 0:d].astype(F32)
        dng += recv_ref[0, d:2 * d].astype(F32)
        extra += recv_ref[0, 2 * d:2 * d + 64].astype(F32)
    g_ref[0, 0:d, :] = upg.astype(BF16)
    g_ref[0, d:2 * d, :] = dng.astype(BF16)
    g_ref[0, 2 * d:2 * d + 64, :] = extra.astype(BF16)

    @pl.when(c == 1)
    def _():
        out_copy.wait()


def ff(first, me, bit, live, w, ub, a2, rest, after):
    seqs, length, d = a2.shape
    total = seqs * length
    anys = pl.BlockSpec(memory_space=pl.ANY)
    swap = lambda c, *_: (1 - c, 0, 0)
    g = pl.BlockSpec((1, 2 * d + 64, d), swap)
    outs = [struct((total, 2 * d), BF16)] * 2 + [struct((2, 2 * d + 64, d), BF16), struct((2, 2, d, d), BF16)]
    out_specs = [pl.BlockSpec((total, d), lambda c, *_: (0, c))] * 2 + [g, anys]
    scratch = [pltpu.VMEM((2, 2, d, d), BF16), pltpu.SemaphoreType.DMA((2, 2))]
    if first:
        rest_specs = [full(a) for a in rest]
        outs.append(struct((seqs, length, d), BF16))
        out_specs.append(full(outs[-1]))
        scratch += [pltpu.VMEM((4, length // 4, d), F32), pltpu.VMEM((length, d), F32)]
    else:
        rest_specs = [full(rest[0]), g]
    return call(
        functools.partial(ff_kernel, first), (me, bit, live), (*w, ub, a2, *rest, after), outs, grid=(2,),
        in_specs=[anys] * 4 + [full(ub), full(a2)] + rest_specs + [anys],
        out_specs=out_specs, scratch=scratch, flops=8 * total * d * d, name="feed_forward")


def attn_bwd_kernel(last, me_ref, *refs):
    refs = list(refs)
    take = lambda n: [refs.pop(0) for _ in range(n)]
    dua_ref, dub_ref, gm_ref, y1_ref, x_ref, g1_ref, g2_ref, wa_ref, wb_ref, wq_ref, wo_ref, qkv_ref, p_ref, small_in = take(14)
    if last:
        a1_ref, o_ref, dqkv_old, ga_old = take(4)
        take(4)
    take(1)
    dxs = take(4)
    if last:
        send_ref, keep_ref = take(2)
    else:
        dqkv_ref, ga_ref, small_ref = take(3)
    do_sc, full_sc, blk_sc = take(3)
    if last:
        dqkv_ref, small_ref, ga_sc, dqkv_sc = take(4)
    s = pl.program_id(0)
    _, length, d = gm_ref.shape

    @pl.when(s == 0)
    def _():
        small_ref[...] = small_in[...]

    da2 = None
    for du_ref, w_ref in ((dua_ref, wa_ref), (dub_ref, wb_ref)):
        for k in range(2):
            part = dot(du_ref[:, pl.ds(k * d, d)], w_ref[k, 0], NT)
            da2 = part if da2 is None else da2 + part
    hat, inv = stats(y1_ref[0])
    gy = gm_ref[0].astype(F32)
    dy1 = gy + norm_back(da2, hat, inv, g2_ref[...])
    full_sc[...] = dy1
    ga = dy1.astype(BF16)
    if not last:
        ga_ref[0] = ga
    sums = [jnp.sum(v, axis=0, keepdims=True) for v in (da2 * hat, da2, ga.astype(F32), gy)]
    do_sc[...] = dot(ga, wo_ref[...], NT).astype(BF16)
    lane = lax.broadcasted_iota(jnp.int32, (length, 128), 1)
    scale = HD ** -0.5
    for p in range(4):
        q = qkv_ref[0, :, pl.ds(p * 384, 128)]
        k = qkv_ref[0, :, pl.ds(p * 384 + 128, 128)]
        v = qkv_ref[0, :, pl.ds(p * 384 + 256, 128)]
        do = do_sc[:, pl.ds(p * 128, 128)]
        dq = dk = dv = None
        for h in range(2):
            mine = (lane < HD) if h == 0 else (lane >= HD)
            zero = jnp.zeros_like(q)
            qh, kh, vh, doh = (jnp.where(mine, a, zero) for a in (q, k, v, do))
            prob = p_ref[0, 2 * p + h]
            dp = dot(vh, do, NT)
            probs = prob.astype(F32)
            pd = probs * dp
            ds = (pd - probs * jnp.sum(pd, axis=0, keepdims=True)).astype(BF16)
            parts = dot(ds, kh, TN), dot(ds, qh), dot(prob, doh)
            dq, dk, dv = parts if dq is None else (dq + parts[0], dk + parts[1], dv + parts[2])
        dqkv_ref[0, :, pl.ds(p * 384, 128)] = (dq * scale).astype(BF16)
        dqkv_ref[0, :, pl.ds(p * 384 + 128, 128)] = (dk * scale).astype(BF16)
        dqkv_ref[0, :, pl.ds(p * 384 + 256, 128)] = dv.astype(BF16)

    da1 = dot(dqkv_ref[0], wq_ref[...], NT)
    hat, inv = stats(x_ref[0])
    sums += [jnp.sum(v, axis=0, keepdims=True) for v in (da1 * hat, da1)]
    full_sc[...] += norm_back(da1, hat, inv, g1_ref[...])
    spread(dxs, me_ref[0], full_sc, blk_sc)
    row = lax.broadcasted_iota(jnp.int32, (8, d), 0)
    small = jnp.zeros((8, d), F32)
    for n, v in enumerate(sums):
        small = jnp.where(row == n, v, small)
    small_ref[...] += small

    if last:
        before = dqkv_old.shape[0] * length
        for n in range(dqkv_old.shape[0]):
            dqkv_sc[pl.ds(n * length, length), :] = dqkv_old[n]
            ga_sc[pl.ds(n * length, length), :] = ga_old[n]
        dqkv_sc[pl.ds(before, length), :] = dqkv_ref[0]
        ga_sc[pl.ds(before, length), :] = ga
        total = before + length
        extra = jnp.concatenate([small_ref[...], jnp.zeros((56, d), F32)], axis=0).astype(BF16)
        for k in range(4):
            ref = send_ref if k % 2 else keep_ref
            ref[k // 2, 0:384] = dot(dqkv_sc[:, pl.ds(384 * k, 384)], a1_ref[...].reshape(total, d), TN).astype(BF16)
            ref[k // 2, 384:512] = dot(o_ref[:, :, pl.ds(128 * k, 128)].reshape(total, 128), ga_sc[...], TN).astype(BF16)
            ref[k // 2, 512:576] = extra


def attn_bwd(me, after, du, gm, y1, x, g1, g2, w, wq, wo, qkv, p, small, old=None, a1=None, o=None):
    seqs, length, d = gm.shape
    last = old is not None
    first, count = (seqs - 1, 1) if last else (0, seqs - 1)
    per = lambda a: pl.BlockSpec((1, *a.shape[1:]), lambda s, *_: (s + first,) + (0,) * (len(a.shape) - 1))
    anys = pl.BlockSpec(memory_space=pl.ANY)
    g = struct((2, 576, d), BF16)
    dx = struct((seqs, length // 4, d), BF16)
    outs = [dx] * 4
    args = [*du, gm, y1, x, g1, g2, *w, wq, wo, qkv, p, small]
    up = pl.BlockSpec((2, 1, d, d), lambda s, *_: (0, 0, 0, 0))
    in_specs = [pl.BlockSpec((length, 2 * d), lambda s, *_: (s + first, 0))] * 2 + [
        per(gm), per(y1), per(x), full(g1), full(g2), up, up, full(wq), full(wo), per(qkv), per(p), full(small)]
    out_specs = [per(a) for a in outs]
    scratch = [pltpu.VMEM((length, d), BF16), pltpu.VMEM((length, d), F32), pltpu.VMEM((4, length // 4, d), F32)]
    aliases = {}
    if last:
        dxs, dqkv, ga = old
        args += [a1, o, dqkv, ga, *dxs]
        in_specs += [full(a1), full(o), full(dqkv), full(ga), *[anys] * 4]
        aliases = {19 + k: k for k in range(4)}
        outs += [g, g]
        out_specs += [full(g), full(g)]
        scratch += [pltpu.VMEM((1, length, 3 * d), BF16), pltpu.VMEM((8, d), F32), pltpu.VMEM((seqs * length, d), BF16),
                    pltpu.VMEM((seqs * length, 3 * d), BF16)]
    else:
        extra = [struct((count, length, 3 * d), BF16), struct((count, length, d), BF16), struct((8, d), F32)]
        outs += extra
        out_specs += [per(extra[0]), per(extra[1]), full(extra[2])]
    args.append(after)
    in_specs.append(anys)
    return call(functools.partial(attn_bwd_kernel, last), (me,), args, outs, grid=(count,), in_specs=in_specs,
                out_specs=out_specs, scratch=scratch, aliases=aliases,
                flops=4 * count * length * (4 * d * d + 2 * d * length), name="attention_backward")


def spread(refs, me, full_sc, blk_sc):
    rows = blk_sc.shape[1]
    for i in range(4):
        blk_sc[i] = full_sc[pl.ds(i * rows, rows), :]
    for k, out in enumerate(refs):
        out[0] = blk_sc[me ^ k].astype(BF16)


def finish_out_kernel(me_ref, live_ref, hma_ref, hmb_ref, wa_ref, wb_ref, y1_ref, db_ref, after_ref,
                      o0, o1, o2, o3, full_sc, blk_sc):
    s = pl.program_id(0)
    d = y1_ref.shape[2]
    mlp = None
    for hm_ref, w_ref in ((hma_ref, wa_ref), (hmb_ref, wb_ref)):
        for k in range(2):
            part = dot(hm_ref[:, pl.ds(k * d, d)], w_ref[k, 0])
            mlp = part if mlp is None else mlp + part
    full_sc[...] = jnp.where(live_ref[s] > 0, y1_ref[0] + mlp + db_ref[...], 0.0)
    spread((o0, o1, o2, o3), me_ref[0], full_sc, blk_sc)


def finish_out(me, live, after, hm, w, y1, db):
    seqs, length, d = y1.shape
    outs = [struct((seqs, length // 4, d), BF16)] * 4
    down = pl.BlockSpec((2, 1, d, d), lambda s, *_: (0, 1, 0, 0))
    return call(
        finish_out_kernel, (me, live), (*hm, *w, y1, db, after), outs, grid=(seqs,),
        in_specs=[pl.BlockSpec((length, 2 * d), lambda s, *_: (s, 0))] * 2 + [
            down, down, per_seq(y1), full(db), pl.BlockSpec(memory_space=pl.ANY)],
        out_specs=[per_seq(outs[0])] * 4,
        scratch=[pltpu.VMEM((length, d), F32), pltpu.VMEM((4, length // 4, d), F32)],
        flops=2 * seqs * length * 4 * d * d, name="block_output")


def hop(value, axis, bit):
    n = lax.axis_size(axis)
    return lax.ppermute(value, axis, [(i, i ^ bit) for i in range(n)])


def split(rows, me):
    rows = rows.transpose(1, 0, 2)
    each = rows.shape[0] // 4
    return [lax.dynamic_slice_in_dim(rows, (me ^ k) * each, each) for k in range(4)]


def scatter(blocks):
    return [blocks[0]] + [hop(blocks[k], "tensor", k) for k in (1, 2, 3)]


def halves(a, side, axis=0):
    n = a.shape[axis] // 2
    return (lax.dynamic_slice_in_dim(a, side * n, n, axis), lax.dynamic_slice_in_dim(a, (1 - side) * n, n, axis))


def join(mine, other, side, axis=0):
    return jnp.where(side == 0, jnp.concatenate([mine, other], axis), jnp.concatenate([other, mine], axis))


def tie(value, *others):
    return lax.optimization_barrier((value, *others))[0]


def plus(a, b):
    return (a.astype(F32) + b.astype(F32)).astype(BF16)


class Sum:
    def __init__(self):
        self.n = lax.axis_size("dp")
        me = lax.axis_index("dp")
        self.y, self.z = me % 2, (me // 2) % 2

    def step1(self, pair):
        self.middle = middle = pair.shape[1] // 2
        self.a = pair[0, :middle]
        self.b, b_other = halves(pair[:, middle:], self.y, 1)
        self.a_got = hop(pair[1, :middle], "tensor", 2)
        self.b_got = hop(b_other, "dp", 1)
        return b_other

    def step2(self, after=()):
        a = plus(self.a, tie(self.a_got, *after))
        self.a, a_other = halves(a, self.y)
        self.a_got = hop(a_other, "dp", 1)
        self.b = plus(self.b, tie(self.b_got, *after))
        self.b_got = hop(self.b[1], "tensor", 2)
        return a_other

    def step3(self, after=()):
        a = plus(self.a, tie(self.a_got, *after))
        b = plus(self.b[0], tie(self.b_got, *after))
        self.part, other = halves(jnp.concatenate([a, b]), self.z)
        self.got = hop(other, "dp", 2)
        return other

    def step4(self, after=()):
        self.part = plus(self.part, tie(self.got, *after))
        for bit in range(2, self.n.bit_length() - 2):
            self.part = plus(self.part, hop(self.part, "dp", 1 << bit))
        self.got = hop(self.part, "dp", 1 << (self.n.bit_length() - 2))
        return self.part

    def step5(self, after=()):
        self.part = plus(self.part, tie(self.got, *after))
        self.got = hop(self.part, "dp", 2)
        return self.part

    def step6(self, after=()):
        part = join(self.part, tie(self.got, *after), self.z)
        self.part = part.reshape(2, self.middle // 2, -1)
        self.got = hop(self.part, "dp", 1)
        return self.part

    def result(self):
        return join(self.part, self.got, self.y, 1).reshape(2 * self.middle, -1)


def shards(
    tokens,
    seq_counts,
    first_frame,
    norm1_gain,
    norm1_bias,
    qkv_weight,
    out_weight,
    out_bias,
    norm2_gain,
    norm2_bias,
    up_weight,
    up_bias,
    down_weight,
    down_bias,
    out_cotangent,
):
    d = tokens.shape[2]
    seqs = tokens.shape[1] // 4
    mine = lax.axis_index("tensor").astype(jnp.int32)
    me = mine.reshape(1)
    y = lax.axis_index("dp").astype(jnp.int32) % 2
    bit = y.reshape(1)
    live = ((mine * seqs + jnp.arange(seqs, dtype=jnp.int32)) < seq_counts[0]).astype(jnp.int32)
    row = lambda a: a.reshape(1, -1)
    g1, b1, bo, g2, b2, db = map(row, (norm1_gain, norm1_bias, out_bias, norm2_gain, norm2_bias, down_bias))

    packed = pack(qkv_weight, out_weight, row(up_bias))
    far = lax.dynamic_index_in_dim(packed, y, 0, keepdims=False)
    far_a = hop(far, "tensor", 2)
    up, down = tie((up_weight, down_weight), far)
    far2_a = hop(jnp.where(y == 0, up, down), "tensor", 2)
    near = hop(packed, "tensor", 1)
    t = scatter(split(tie(tokens, far), mine))
    far_b = hop(far_a, "dp", 1)
    w1 = (packed, near, far_a, far_b, hop(far_a, "tensor", 1), hop(far_b, "tensor", 1))
    far2_b = hop(far2_a, "dp", 1)
    wa = (hop(far2_a, "tensor", 1), hop(far2_b, "tensor", 1), hop(tie(up, far_a), "tensor", 1), hop(tie(down, far_a), "tensor", 1))
    wb = (far2_a, far2_b, up_weight, down_weight)
    cot = scatter(split(tie(out_cotangent, t[2]), mine))

    qkv, p, o, x, y1, a1, a2, wq, wo, ub = attn_fwd(me, bit, first_frame, t, w1, g1, b1, bo, g2, b2)
    hma, dua, send, wa, gm = ff(True, me, bit, live, wa, ub, a2, cot, a2)
    hmb, dub, pair, wb = ff(False, me, bit, live, wb, ub, a2, (gm, hop(send, "tensor", 1)), a2)
    du, hm, w2 = (dua, dub), (hma, hmb), (wa, wb)

    mlp_sum, attn_sum = Sum(), Sum()
    ready = mlp_sum.step1(pair)
    *dx, dqkv, ga, small = attn_bwd(me, ready, du, gm, y1, x, g1, g2, w2, wq, wo, qkv, p, jnp.zeros((8, d), F32))
    ready = mlp_sum.step2((small,))
    *dx, send, keep = attn_bwd(me, ready, du, gm, y1, x, g1, g2, w2, wq, wo, qkv, p, small, (dx, dqkv, ga), a1, o)
    got = hop(send, "tensor", 1)
    ready = mlp_sum.step3((send,))
    ready = attn_sum.step1(plus(keep, tie(got, ready)))
    out = finish_out(me, live, ready, hm, w2, y1, db)
    ready = mlp_sum.step4((out[0],))
    ready = attn_sum.step2((ready,))
    dx = scatter(tie(dx, ready))
    ready = attn_sum.step3((ready,))
    ready = mlp_sum.step5((ready,))
    ready = attn_sum.step4((ready,))
    out = scatter(tie(out, dx[2], ready))
    ready = mlp_sum.step6((ready,))
    ready = attn_sum.step5((ready,))
    input_grad = place(me, tie(dx, ready)).transpose(1, 0, 2)
    ready = attn_sum.step6((ready,))
    mlp_grad = mlp_sum.result()
    attn_grad = attn_sum.result()
    block_output = place(me, out).transpose(1, 0, 2)

    mlp_grad = mlp_grad.astype(F32)
    attn_grad = attn_grad.astype(F32)
    heads = attn_grad[:384].reshape(3, 2, HD, d).transpose(1, 0, 2, 3).reshape(384, d)
    norm2_g, norm2_b, out_b, down_b, norm1_g, norm1_b = (attn_grad[512 + i] for i in range(6))
    return (
        block_output,
        input_grad,
        heads.T,
        attn_grad[384:512],
        mlp_grad[:d],
        mlp_grad[d:2 * d].T,
        mlp_grad[2 * d],
        out_b,
        down_b,
        norm1_g,
        norm1_b,
        norm2_g,
        norm2_b,
    )


def solution(mesh):
    return jax.shard_map(
        shards,
        mesh=mesh,
        in_specs=(
            P("tensor", "dp", None),
            P("dp"),
            P("dp"),
            P(),
            P(),
            P(None, "tensor"),
            P("tensor", None),
            P(),
            P(),
            P(),
            P(None, "tensor"),
            P("tensor"),
            P("tensor", None),
            P(),
            P("tensor", "dp", None),
        ),
        out_specs=(
            P("tensor", "dp", None),
            P("tensor", "dp", None),
            P(None, "tensor"),
            P("tensor", None),
            P(None, "tensor"),
            P("tensor", None),
            P("tensor"),
            P(),
            P(),
            P(),
            P(),
            P(),
            P(),
        ),
        check_vma=False,
    )
```

time: 780 us -> 229 us (0.29)
  waiting for transfers between devices: 477 us -> 83.7 us
  matrix products: 135 us -> 0 us
  Pallas kernels: 0 us -> 84.2 us
  blocking collectives: 64.1 us -> 0 us
  other arithmetic: 47.2 us -> 7.4 us
  starting transfers between devices: 1.14 us -> 34.7 us
  local copies, waits for them, and re-layouts: 32.9 us -> 16.5 us
  between operations: 16.3 us -> 1.9 us
    unnamed x11 -> x0, waiting for transfers between devices: 254 us -> none
    all_gather x4 -> x0, waiting for transfers between devices: 145 us -> none  [the longest x1 42.1 us: shards(): a_one = lax.all_gather(a_one, 'tensor', axis=0, tiled=True)]
    dot_general x18 -> x0, matrix products: 135 us -> none  [the longest x1 14.3 us: shards(): jnp.einsum('psd,fd->psf', d_mlp, down_weight, preferred_element_type=jnp....]
    pallas_call x0 -> x9, Pallas kernels: none -> 84.2 us  [call(): pl.pallas_call(kernel, grid_spec=pltpu.PrefetchScalarGridSpec(num_scalar_...]
    ppermute x0 -> x41, waiting for transfers between devices: none -> 83.7 us  [hop(): return lax.ppermute(value, axis, [(i, i ^ bit) for i in range(n)])]
    psum x1 -> x0, waiting for transfers between devices: 77.2 us -> none  [shards(): lax.psum((qkv_weight_grad, out_weight_grad, up_weight_grad, down_weight_g...]
    psum x2 -> x0, blocking collectives: 64.1 us -> none  [the longest x1 42.2 us: shards(): lax.psum((norm1_gain_grad, norm1_bias_grad, norm2_gain_grad, norm2_bias_g...]
    ppermute x0 -> x41, starting transfers between devices: none -> 34.7 us  [hop(): return lax.ppermute(value, axis, [(i, i ^ bit) for i in range(n)])]
  transfers between devices with their start and end apart: 8 -> 41, of which waited for: 8 -> 19; matrix products, arithmetic and copies ran while one was open for 11% -> 5% of each run, Pallas kernels for 0% -> 20%
where the time goes in v1:
time: 229 us; the launch traced here: 228 us
  Pallas kernels  84.2 us (37%)
  waiting for transfers between devices  83.7 us (37%)
  starting transfers between devices  34.7 us (15%)
  local copies, waits for them, and re-layouts  16.5 us (7%)
  other arithmetic  7.4 us (3%)
    pallas_call x9, Pallas kernels, call(): pl.pallas_call(kernel, grid_spec=pltpu.PrefetchScalarGridSpec(num_scalar_...  84.2 us
    ppermute x41, waiting for transfers between devices, hop(): return lax.ppermute(value, axis, [(i, i ^ bit) for i in range(n)])  83.7 us
    ppermute x41, starting transfers between devices, hop(): return lax.ppermute(value, axis, [(i, i ^ bit) for i in range(n)])  34.7 us
    unnamed x76, local copies, waits for them, and re-layouts  6.65 us
  transfers between devices with their start and end apart: 41, of which 19 were waited for; matrix products, arithmetic and copies ran while one was open for 5% of the time, Pallas kernels for 20%

profile of v1, /device:TPU:0, one launch (start us, length us, event | category | flops | bytes accessed | tf_op | source)
XLA Modules:
  0.0 228.3 jit_solution(6432853346359799368)
XLA Ops:
  0.7 2.1 pack_weights.1.w0
  2.8 1.1 dynamic-slice_bitcast_fusion
  3.9 0.9 broadcast_select_fusion
  4.7 2.9 %collective-permute-start = (bf16[512,512]{1,0:T(8,128)(2,1)}, bf16[512,512]{1,0:T(8,128)(2,1)}, u32[]{:S(2)}, u32[]{:S(2)}) collective-permute-start(bf16[512,512]{1,0:T(8,128)(2,1)} %broadcast_select_fusion), channel_id=1, source_target_pairs={{0,2},{1,3},{2,0},{3,1},{4,6},{5,7},{6,4},{7,5},{8,10},{9,11},{10,... | collective-permute-start | bytes 1572872 | tf_op jit(solution)/shard_map/ppermute | solution.py:459
  7.7 0.8 dynamic-slice_bitcast_fusion.5
  8.5 0.9 collective-permute-start.9
  9.4 1.2 collective-permute-start.4
  10.6 15.8 %collective-permute-done.8.t2 = bf16[3,84,512]{2,1,0:T(8,128)(2,1)S(1)} collective-permute-done((bf16[3,84,512]{2,1,0:T(8,128)(2,1)S(1)}, bf16[3,84,512]{2,1,0:T(8,128)(2,1)S(1)}, u32[]{:S(2)}, u32[]{:S(2)}) %collective-permute-start.8) | collective-permute-done | bytes 258080 | tf_op jit(solution)/shard_map/ppermute | solution.py:459
  26.4 2.2 collective-permute-start.2
  28.6 0.8 dynamic-slice_bitcast_fusion.1
  29.4 2.4 %collective-permute-done.9.t3 = bf16[3,84,512]{2,1,0:T(8,128)(2,1)S(1)} collective-permute-done((bf16[3,84,512]{2,1,0:T(8,128)(2,1)S(1)}, bf16[3,84,512]{2,1,0:T(8,128)(2,1)S(1)}, u32[]{:S(2)}, u32[]{:S(2)}) %collective-permute-start.9) | collective-permute-done | bytes 258080 | tf_op jit(solution)/shard_map/ppermute | solution.py:459
  31.8 2.2 collective-permute-start.16
  34.0 4.2 %collective-permute-done.4.w2a = bf16[272,512]{1,0:T(8,128)(2,1)S(1)} collective-permute-done((bf16[272,512]{1,0:T(8,128)(2,1)S(1)}, bf16[272,512]{1,0:T(8,128)(2,1)S(1)}, u32[]{:S(2)}, u32[]{:S(2)}) %collective-permute-start.4) | collective-permute-done | bytes 278560 | tf_op jit(solution)/shard_map/ppermute | solution.py:459
  38.2 2.1 collective-permute-start.11
  40.3 2.1 collective-permute-done.16.refs_9_
  42.4 1.3 collective-permute-start.15
  43.7 3.6 %collective-permute-done.11.w2b = bf16[272,512]{1,0:T(8,128)(2,1)S(1)} collective-permute-done((bf16[272,512]{1,0:T(8,128)(2,1)S(1)}, bf16[272,512]{1,0:T(8,128)(2,1)S(1)}, u32[]{:S(2)}, u32[]{:S(2)}) %collective-permute-start.11) | collective-permute-done | bytes 278560 | tf_op jit(solution)/shard_map/ppermute | solution.py:459
  47.3 4.4 %collective-permute-done.15.refs_8_ = bf16[3,84,512]{2,1,0:T(8,128)(2,1)S(1)} collective-permute-done((bf16[3,84,512]{2,1,0:T(8,128)(2,1)S(1)}, bf16[3,84,512]{2,1,0:T(8,128)(2,1)S(1)}, u32[]{:S(2)}, u32[]{:S(2)}) %collective-permute-start.15) | collective-permute-done | bytes 258080 | tf_op jit(solution)/shard_map/ppermute | solution.py:459
  54.6 16.1 %attention_forward.1 = (bf16[3,336,1536]{2,1,0:T(8,128)(2,1)}, bf16[3,8,336,336]{3,2,1,0:T(8,128)(2,1)}, bf16[3,336,512]{2,1,0:T(8,128)(2,1)}, f32[3,336,512]{2,...) custom-call(s32[1]{0:T(128)} %bitcast.me_ref, ...), custom_call_target="tpu_custom_call" | custom-call | flops 2807562240 | bytes 21174272 | tf_op jit(solution)/shard_map/attention_forward/pallas_call | solution.py:52
  70.9 0.6 copy-done.36
  72.2 11.2 %feed_forward.2 = (bf16[1008,1024]{1,0:T(8,128)(2,1)}, bf16[1008,1024]{1,0:T(8,128)(2,1)}, bf16[2,1088,512]{2,1,0:T(8,128)(2,1)}, bf16[2,2,512,512]{3,2,1,0:T(8,128)(2,1)}, bf16[3,336,512]{2,1,0:T(8,128)(2,1)}) custom-call(s32[1]{0:T(128)} %bitcast.me_ref, s32[1]{0:T(128)} %bitcast.2.bit_ref, s32[3]{0:T(128)} %compare_convert_fusion.live_ref, ...), custom_call_target="tpu_custom_call" | custom-call | flops 2113929216 | bytes 14745600 | tf_op jit(solution)/shard_map/feed_forward/pallas_call | solution.py:52
  83.7 4.4 %collective-permute-done.17.refs_7_ = bf16[2,1088,512]{2,1,0:T(8,128)(2,1)S(1)} collective-permute-done((bf16[2,1088,512]{2,1,0:T(8,128)(2,1)}, bf16[2,1088,512]{2,1,0:T(8,128)(2,1)S(1)}, u32[]{:S(2)}, u32[]{:S(2)}) %collective-permute-start.17) | collective-permute-done | bytes 2228256 | tf_op jit(solution)/shard_map/ppermute | solution.py:459
  88.1 1.3 copy-done.19
  89.4 11.3 %feed_forward.3 = (bf16[1008,1024]{1,0:T(8,128)(2,1)}, bf16[1008,1024]{1,0:T(8,128)(2,1)}, bf16[2,1088,512]{2,1,0:T(8,128)(2,1)}, bf16[2,2,512,512]{3,2,1,0:T(8,128)(2,1)}) custom-call(s32[1]{0:T(128)} %bitcast.me_ref, s32[1]{0:T(128)} %bitcast.2.bit_ref, s32[3]{0:T(128)} %compare_convert_fusion.live_ref, bf16[512,512]{1,0:T(8,128)(2,1)} %collective-permute-done.refs_0_, ...), custom_call_target="tpu_custom_call" | custom-call | flops 2113929216 | bytes 15941632 | tf_op jit(solution)/shard_map/feed_forward/pallas_call | solution.py:52
  100.8 1.3 slice.63
  102.2 1.6 collective-permute-start.21
  103.8 1.1 slice_bitcast_fusion.1
  104.9 1.2 collective-permute-start.18
  106.7 17.4 %attention_backward.2 = (bf16[3,84,512]{2,1,0:T(8,128)(2,1)}, bf16[3,84,512]{2,1,0:T(8,128)(2,1)}, bf16[3,84,512]{2,1,0:T(8,128)(2,1)}, bf16[3,84,512]{2,1,0:T(8...) custom-call(s32[1]{0:T(128)} %bitcast.me_ref, ...), custom_call_target="tpu_custom_call" | custom-call | flops 3743416320 | bytes 28475392 | tf_op jit(solution)/shard_map/attention_backward/pallas_call | solution.py:52
  124.1 1.4 fusion
  125.5 0.7 constant_dynamic-slice_fusion.2.refs_22_
  126.2 14.5 %attention_backward.3 = (bf16[3,84,512]{2,1,0:T(8,128)(2,1)}, bf16[3,84,512]{2,1,0:T(8,128)(2,1)}, bf16[3,84,512]{2,1,0:T(8,128)(2,1)}, bf16[3,84,512]{2,1,0:T(8...) custom-call(s32[1]{0:T(128)} %bitcast.me_ref, ...), custom_call_target="tpu_custom_call", output_to_operand_aliasing={{0}: (19, {}), {1}: (20, {}), {2}: (21, {}), {3}: (22, {})} | custom-call | flops 1871708160 | bytes 33636352 | tf_op jit(solution)/shard_map/attention_backward/pallas_call | solution.py:52
  140.8 1.2 add_convert_fusion.1
  142.0 0.9 collective-permute-start.22
  143.5 7.6 %collective-permute-done.22 = bf16[272,512]{1,0:T(8,128)(2,1)S(1)} collective-permute-done((bf16[272,512]{1,0:T(8,128)(2,1)S(1)}, bf16[272,512]{1,0:T(8,128)(2,1)S(1)}, u32[]{:S(2)}, u32[]{:S(2)}) %collective-permute-start.22) | collective-permute-done | bytes 278560 | tf_op jit(solution)/shard_map/ppermute | solution.py:459
  151.1 0.8 collective-permute-done.20
  152.5 1.6 collective-permute-start.24
  154.5 1.2 collective-permute-start.23
  156.5 7.1 %block_output.1 = (bf16[3,84,512]{2,1,0:T(8,128)(2,1)}, bf16[3,84,512]{2,1,0:T(8,128)(2,1)}, bf16[3,84,512]{2,1,0:T(8,128)(2,1)}, bf16[3,84,512]{2,1,0:T(8,128)(2,1)}) custom-call(s32[1]{0:T(128)} %bitcast.me_ref, s32[3]{0:T(128)} %compare_convert_fusion.live_ref, bf16[1008,1024]{1,0:T(8,128)(2,1)} %get-tuple-element.90.hma_ref, ...), custom_call_target="tpu_custom_call" | custom-call | flops 2113929216 | bytes 11716608 | tf_op jit(solution)/shard_map/block_output/pallas_call | solution.py:52
  164.1 1.5 collective-permute-start.26
  165.7 0.9 collective-permute-start.28
  166.6 2.6 %collective-permute-start.30 = (bf16[272,512]{1,0:T(8,128)(2,1)S(1)}, bf16[272,512]{1,0:T(8,128)(2,1)S(1)}, u32[]{:S(2)}, u32[]{:S(2)}) collective-permute-start(bf16[272,512]{1,0:T(8,128)(2,1)S(1)} %add_convert_fusion.4), channel_id=1, source_target_pairs={{0,16},{4,20},{8,24},{12,28},{16,0},{20,4},{24,8},{28,12},{1,17},{... | collective-permute-start | bytes 835592 | tf_op jit(solution)/shard_map/ppermute | solution.py:459
  169.3 1.6 collective-permute-done.28
  171.6 8.4 %collective-permute-done.30 = bf16[272,512]{1,0:T(8,128)(2,1)S(1)} collective-permute-done((bf16[272,512]{1,0:T(8,128)(2,1)S(1)}, bf16[272,512]{1,0:T(8,128)(2,1)S(1)}, u32[]{:S(2)}, u32[]{:S(2)}) %collective-permute-start.30) | collective-permute-done | bytes 278560 | tf_op jit(solution)/shard_map/ppermute | solution.py:459
  180.2 1.3 collective-permute-done.29
  181.7 1.8 collective-permute-start.36
  183.4 8.4 %collective-permute-done.37 = bf16[272,512]{1,0:T(8,128)(2,1)S(1)} collective-permute-done((bf16[272,512]{1,0:T(8,128)(2,1)S(1)}, bf16[272,512]{1,0:T(8,128)(2,1)S(1)}, u32[]{:S(2)}, u32[]{:S(2)}) %collective-permute-start.37) | collective-permute-done | bytes 278560 | tf_op jit(solution)/shard_map/ppermute | solution.py:459
  192.2 1.2 collective-permute-start.25
  193.4 3.9 %collective-permute-done.38 = bf16[144,512]{1,0:T(8,128)(2,1)S(1)} collective-permute-done((bf16[144,512]{1,0:T(8,128)(2,1)S(1)}, bf16[144,512]{1,0:T(8,128)(2,1)S(1)}, u32[]{:S(2)}, u32[]{:S(2)}) %collective-permute-start.38) | collective-permute-done | bytes 147488 | tf_op jit(solution)/shard_map/ppermute | solution.py:459
  197.4 1.0 collective-permute-start.39
  198.4 1.4 collective-permute-done.25.b2
  199.8 1.1 collective-permute-start.32
  200.9 0.8 collective-permute-start.33
  201.7 5.5 %collective-permute-done.35.b3 = bf16[3,84,512]{2,1,0:T(8,128)(2,1)S(1)} collective-permute-done((bf16[3,84,512]{2,1,0:T(8,128)(2,1)S(1)}, bf16[3,84,512]{2,1,0:T(8,128)(2,1)S(1)}, u32[]{:S(2)}, u32[]{:S(2)}) %collective-permute-start.35) | collective-permute-done | bytes 258080 | tf_op jit(solution)/shard_map/ppermute | solution.py:459
  207.2 1.1 collective-permute-start.40
  208.3 2.2 place.3
  210.6 1.8 collective-permute-done.32.b2
  212.4 6.1 %collective-permute-done.33.b3 = bf16[3,84,512]{2,1,0:T(8,128)(2,1)S(1)} collective-permute-done((bf16[3,84,512]{2,1,0:T(8,128)(2,1)S(1)}, bf16[3,84,512]{2,1,0:T(8,128)(2,1)S(1)}, u32[]{:S(2)}, u32[]{:S(2)}) %collective-permute-start.33) | collective-permute-done | bytes 258080 | tf_op jit(solution)/shard_map/ppermute | solution.py:459
  218.5 0.7 copy-done.18
  219.2 2.2 place.2
  221.8 0.7 slice.92
  222.7 1.2 copy.38
  225.9 1.1 slice_bitcast_fusion
  227.0 1.3 copy.39
  (146 shorter events, 11.1 us)
Async XLA Ops:
  2.8 4.9 %copy-start.4 = (bf16[84,12,512]{2,0,1:T(8,128)(2,1)S(1)}, bf16[84,12,512]{2,0,1:T(8,128)(2,1)}, u32[]{:S(2)}) copy-start(bf16[84,12,512]{2,0,1:T(8,128)(2,1)} %param.15) | copy-start | bytes 3096580
  4.7 5.8 %copy-start.1 = (bf16[2,272,512]{2,1,0:T(8,128)(2,1)S(1)}, bf16[2,272,512]{2,1,0:T(8,128)(2,1)}, u32[]{:S(2)}) copy-start(bf16[2,272,512]{2,1,0:T(8,128)(2,1)} %pack_weights.1.w0) | copy-start | bytes 1671172
  4.7 23.9 %copy-start.5 = (bf16[84,12,512]{2,0,1:T(8,128)(2,1)S(1)}, bf16[84,12,512]{2,0,1:T(8,128)(2,1)}, u32[]{:S(2)}) copy-start(bf16[84,12,512]{2,0,1:T(8,128)(2,1)} %param.29) | copy-start | bytes 3096580
  4.7 21.7 %collective-permute-start = (bf16[512,512]{1,0:T(8,128)(2,1)}, bf16[512,512]{1,0:T(8,128)(2,1)}, u32[]{:S(2)}, u32[]{:S(2)}) collective-permute-start(bf16[512,512]{1,0:T(8,128)(2,1)} %broadcast_select_fusion), channel_id=1, source_target_pairs={{0,2},{1,3},{2,0},{3,1},{4,6},{5,7},{6,4},{7,5},{8,10},{9,11},{10,... | collective-permute-start | bytes 1572872 | tf_op jit(solution)/shard_map/ppermute | solution.py:459
  8.5 43.2 %copy-start.9 = (bf16[512,512]{1,0:T(8,128)(2,1)S(1)}, bf16[512,512]{1,0:T(8,128)(2,1)}, u32[]{:S(2)}) copy-start(bf16[512,512]{1,0:T(8,128)(2,1)} %refs_3_.1) | copy-start | bytes 1572868
  8.5 17.9 %collective-permute-start.8 = (bf16[3,84,512]{2,1,0:T(8,128)(2,1)S(1)}, bf16[3,84,512]{2,1,0:T(8,128)(2,1)S(1)}, u32[]{:S(2)}, u32[]{:S(2)}) collective-permute-start(bf16[3,84,512]{2,1,0:T(8,128)(2,1)S(1)} %get-tuple-element.203), channel_id=1, source_target_pairs={{0,2},{1,3},{2,0},{3,1},{4,6},{5,7},{6,4},{7,5},{8,10},{9,11},{10,... | collective-permute-start | bytes 774152 | tf_op jit(solution)/shard_map/ppermute | solution.py:459
  8.5 23.3 %collective-permute-start.9 = (bf16[3,84,512]{2,1,0:T(8,128)(2,1)S(1)}, bf16[3,84,512]{2,1,0:T(8,128)(2,1)S(1)}, u32[]{:S(2)}, u32[]{:S(2)}) collective-permute-start(bf16[3,84,512]{2,1,0:T(8,128)(2,1)S(1)} %get-tuple-element.202), channel_id=1, source_target_pairs={{0,3},{1,2},{2,1},{3,0},{4,7},{5,6},{6,5},{7,4},{8,11},{9,10},{10,... | collective-permute-start | bytes 774152 | tf_op jit(solution)/shard_map/ppermute | solution.py:459
  9.4 28.8 %collective-permute-start.4 = (bf16[272,512]{1,0:T(8,128)(2,1)S(1)}, bf16[272,512]{1,0:T(8,128)(2,1)S(1)}, u32[]{:S(2)}, u32[]{:S(2)}) collective-permute-start(bf16[272,512]{1,0:T(8,128)(2,1)S(1)} %dynamic-slice_bitcast_fusion), channel_id=1, source_target_pairs={{0,2},{1,3},{2,0},{3,1},{4,6},{5,7},{6,4},{7,5},{8,10},{9,11},{10,... | collective-permute-start | bytes 835592 | tf_op jit(solution)/shard_map/ppermute | solution.py:459
  10.6 41.7 %collective-permute-start.10 = (bf16[2,272,512]{2,1,0:T(8,128)(2,1)S(1)}, bf16[2,272,512]{2,1,0:T(8,128)(2,1)S(1)}, u32[]{:S(2)}, u32[]{:S(2)}) collective-permute-start(bf16[2,272,512]{2,1,0:T(8,128)(2,1)S(1)} %copy-done.1), channel_id=1, source_target_pairs={{0,1},{1,0},{2,3},{3,2},{4,5},{5,4},{6,7},{7,6},{8,9},{9,8},{10,11... | collective-permute-start | bytes 1671176 | tf_op jit(solution)/shard_map/ppermute | solution.py:459
  26.4 27.6 %copy-start.31 = (bf16[3,84,512]{2,1,0:T(8,128)(2,1)}, bf16[3,84,512]{2,1,0:T(8,128)(2,1)S(1)}, u32[]{:S(2)}) copy-start(bf16[3,84,512]{2,1,0:T(8,128)(2,1)S(1)} %collective-permute-done.8.t2) | copy-start | bytes 774148
  26.4 13.9 %collective-permute-start.7 = (bf16[3,84,512]{2,1,0:T(8,128)(2,1)S(1)}, bf16[3,84,512]{2,1,0:T(8,128)(2,1)S(1)}, u32[]{:S(2)}, u32[]{:S(2)}) collective-permute-start(bf16[3,84,512]{2,1,0:T(8,128)(2,1)S(1)} %get-tuple-element.204), channel_id=1, source_target_pairs={{0,1},{1,0},{2,3},{3,2},{4,5},{5,4},{6,7},{7,6},{8,9},{9,8},{10,11... | collective-permute-start | bytes 774152 | tf_op jit(solution)/shard_map/ppermute | solution.py:459
  26.4 25.9 %collective-permute-start.2 = (bf16[512,512]{1,0:T(8,128)(2,1)}, bf16[512,512]{1,0:T(8,128)(2,1)S(1)}, u32[]{:S(2)}, u32[]{:S(2)}) collective-permute-start(bf16[512,512]{1,0:T(8,128)(2,1)} %collective-permute-done.refs_0_), channel_id=1, source_target_pairs={{0,4},{4,0},{8,12},{12,8},{16,20},{20,16},{24,28},{28,24},{1,5},{5... | collective-permute-start | bytes 1572872 | tf_op jit(solution)/shard_map/ppermute | solution.py:459
  31.8 22.3 %copy-start.32 = (bf16[3,84,512]{2,1,0:T(8,128)(2,1)}, bf16[3,84,512]{2,1,0:T(8,128)(2,1)S(1)}, u32[]{:S(2)}) copy-start(bf16[3,84,512]{2,1,0:T(8,128)(2,1)S(1)} %collective-permute-done.9.t3) | copy-start | bytes 774148
  31.8 10.6 %collective-permute-start.16 = (bf16[3,84,512]{2,1,0:T(8,128)(2,1)S(1)}, bf16[3,84,512]{2,1,0:T(8,128)(2,1)S(1)}, u32[]{:S(2)}, u32[]{:S(2)}) collective-permute-start(bf16[3,84,512]{2,1,0:T(8,128)(2,1)S(1)} %get-tuple-element.198), channel_id=1, source_target_pairs={{0,3},{1,2},{2,1},{3,0},{4,7},{5,6},{6,5},{7,4},{8,11},{9,10},{10,... | collective-permute-start | bytes 774152 | tf_op jit(solution)/shard_map/ppermute | solution.py:459
  38.2 15.9 %copy-start.26 = (bf16[272,512]{1,0:T(8,128)(2,1)}, bf16[272,512]{1,0:T(8,128)(2,1)S(1)}, u32[]{:S(2)}) copy-start(bf16[272,512]{1,0:T(8,128)(2,1)S(1)} %collective-permute-done.4.w2a) | copy-start | bytes 835588
  38.2 9.1 %collective-permute-start.11 = (bf16[272,512]{1,0:T(8,128)(2,1)S(1)}, bf16[272,512]{1,0:T(8,128)(2,1)S(1)}, u32[]{:S(2)}, u32[]{:S(2)}) collective-permute-start(bf16[272,512]{1,0:T(8,128)(2,1)S(1)} %collective-permute-done.4.w2a), channel_id=1, source_target_pairs={{0,4},{4,0},{8,12},{12,8},{16,20},{20,16},{24,28},{28,24},{1,5},{5... | collective-permute-start | bytes 835592 | tf_op jit(solution)/shard_map/ppermute | solution.py:459
  40.3 13.8 %copy-start.34 = (bf16[3,84,512]{2,1,0:T(8,128)(2,1)}, bf16[3,84,512]{2,1,0:T(8,128)(2,1)S(1)}, u32[]{:S(2)}) copy-start(bf16[3,84,512]{2,1,0:T(8,128)(2,1)S(1)} %collective-permute-done.7.t1) | copy-start | bytes 774148
  40.3 11.4 %collective-permute-start.12 = (bf16[272,512]{1,0:T(8,128)(2,1)S(1)}, bf16[272,512]{1,0:T(8,128)(2,1)S(1)}, u32[]{:S(2)}, u32[]{:S(2)}) collective-permute-start(bf16[272,512]{1,0:T(8,128)(2,1)S(1)} %collective-permute-done.4.w2a), channel_id=1, source_target_pairs={{0,1},{1,0},{2,3},{3,2},{4,5},{5,4},{6,7},{7,6},{8,9},{9,8},{10,11... | collective-permute-start | bytes 835592 | tf_op jit(solution)/shard_map/ppermute | solution.py:459
  42.4 28.4 %copy-start.33 = (bf16[3,84,512]{2,1,0:T(8,128)(2,1)}, bf16[3,84,512]{2,1,0:T(8,128)(2,1)S(1)}, u32[]{:S(2)}) copy-start(bf16[3,84,512]{2,1,0:T(8,128)(2,1)S(1)} %collective-permute-done.16.refs_9_) | copy-start | bytes 774148
  42.4 9.2 %collective-permute-start.15 = (bf16[3,84,512]{2,1,0:T(8,128)(2,1)S(1)}, bf16[3,84,512]{2,1,0:T(8,128)(2,1)S(1)}, u32[]{:S(2)}, u32[]{:S(2)}) collective-permute-start(bf16[3,84,512]{2,1,0:T(8,128)(2,1)S(1)} %get-tuple-element.199), channel_id=1, source_target_pairs={{0,2},{1,3},{2,0},{3,1},{4,6},{5,7},{6,4},{7,5},{8,10},{9,11},{10,... | collective-permute-start | bytes 774152 | tf_op jit(solution)/shard_map/ppermute | solution.py:459
  47.3 6.8 %copy-start.27 = (bf16[272,512]{1,0:T(8,128)(2,1)}, bf16[272,512]{1,0:T(8,128)(2,1)S(1)}, u32[]{:S(2)}) copy-start(bf16[272,512]{1,0:T(8,128)(2,1)S(1)} %collective-permute-done.11.w2b) | copy-start | bytes 835588
  47.3 6.6 %collective-permute-start.13 = (bf16[272,512]{1,0:T(8,128)(2,1)S(1)}, bf16[272,512]{1,0:T(8,128)(2,1)S(1)}, u32[]{:S(2)}, u32[]{:S(2)}) collective-permute-start(bf16[272,512]{1,0:T(8,128)(2,1)S(1)} %collective-permute-done.11.w2b), channel_id=1, source_target_pairs={{0,1},{1,0},{2,3},{3,2},{4,5},{5,4},{6,7},{7,6},{8,9},{9,8},{10,11... | collective-permute-start | bytes 835592 | tf_op jit(solution)/shard_map/ppermute | solution.py:459
  51.7 19.1 %copy-start.35 = (bf16[3,84,512]{2,1,0:T(8,128)(2,1)}, bf16[3,84,512]{2,1,0:T(8,128)(2,1)S(1)}, u32[]{:S(2)}) copy-start(bf16[3,84,512]{2,1,0:T(8,128)(2,1)S(1)} %collective-permute-done.15.refs_8_) | copy-start | bytes 774148
  51.7 19.2 %collective-permute-start.5 = (bf16[512,512]{1,0:T(8,128)(2,1)S(1)}, bf16[512,512]{1,0:T(8,128)(2,1)S(1)}, u32[]{:S(2)}, u32[]{:S(2)}) collective-permute-start(bf16[512,512]{1,0:T(8,128)(2,1)S(1)} %copy-done.7), channel_id=1, source_target_pairs={{0,1},{1,0},{2,3},{3,2},{4,5},{5,4},{6,7},{7,6},{8,9},{9,8},{10,11... | collective-permute-start | bytes 1572872 | tf_op jit(solution)/shard_map/ppermute | solution.py:459
  51.7 19.2 %collective-permute-start.6 = (bf16[512,512]{1,0:T(8,128)(2,1)S(1)}, bf16[512,512]{1,0:T(8,128)(2,1)S(1)}, u32[]{:S(2)}, u32[]{:S(2)}) collective-permute-start(bf16[512,512]{1,0:T(8,128)(2,1)S(1)} %copy-done.9), channel_id=1, source_target_pairs={{0,1},{1,0},{2,3},{3,2},{4,5},{5,4},{6,7},{7,6},{8,9},{9,8},{10,11... | collective-permute-start | bytes 1572872 | tf_op jit(solution)/shard_map/ppermute | solution.py:459
  52.2 18.6 %collective-permute-start.1 = (bf16[512,512]{1,0:T(8,128)(2,1)}, bf16[512,512]{1,0:T(8,128)(2,1)S(1)}, u32[]{:S(2)}, u32[]{:S(2)}) collective-permute-start(bf16[512,512]{1,0:T(8,128)(2,1)} %collective-permute-done.refs_0_), channel_id=1, source_target_pairs={{0,1},{1,0},{2,3},{3,2},{4,5},{5,4},{6,7},{7,6},{8,9},{9,8},{10,11... | collective-permute-start | bytes 1572872 | tf_op jit(solution)/shard_map/ppermute | solution.py:459
  52.3 18.4 %copy-start.21 = (bf16[512,512]{1,0:T(8,128)(2,1)}, bf16[512,512]{1,0:T(8,128)(2,1)S(1)}, u32[]{:S(2)}) copy-start(bf16[512,512]{1,0:T(8,128)(2,1)S(1)} %collective-permute-done.2.refs_1_) | copy-start | bytes 1572868
  52.3 18.5 %collective-permute-start.3 = (bf16[512,512]{1,0:T(8,128)(2,1)S(1)}, bf16[512,512]{1,0:T(8,128)(2,1)S(1)}, u32[]{:S(2)}, u32[]{:S(2)}) collective-permute-start(bf16[512,512]{1,0:T(8,128)(2,1)S(1)} %collective-permute-done.2.refs_1_), channel_id=1, source_target_pairs={{0,1},{1,0},{2,3},{3,2},{4,5},{5,4},{6,7},{7,6},{8,9},{9,8},{10,11... | collective-permute-start | bytes 1572872 | tf_op jit(solution)/shard_map/ppermute | solution.py:459
  53.9 16.9 %collective-permute-start.14 = (bf16[3,84,512]{2,1,0:T(8,128)(2,1)S(1)}, bf16[3,84,512]{2,1,0:T(8,128)(2,1)S(1)}, u32[]{:S(2)}, u32[]{:S(2)}) collective-permute-start(bf16[3,84,512]{2,1,0:T(8,128)(2,1)S(1)} %get-tuple-element.200), channel_id=1, source_target_pairs={{0,1},{1,0},{2,3},{3,2},{4,5},{5,4},{6,7},{7,6},{8,9},{9,8},{10,11... | collective-permute-start | bytes 774152 | tf_op jit(solution)/shard_map/ppermute | solution.py:459
  83.5 4.6 %collective-permute-start.17 = (bf16[2,1088,512]{2,1,0:T(8,128)(2,1)}, bf16[2,1088,512]{2,1,0:T(8,128)(2,1)S(1)}, u32[]{:S(2)}, u32[]{:S(2)}) collective-permute-start(bf16[2,1088,512]{2,1,0:T(8,128)(2,1)} %get-tuple-element.92), channel_id=1, source_target_pairs={{0,1},{1,0},{2,3},{3,2},{4,5},{5,4},{6,7},{7,6},{8,9},{9,8},{10,11... | collective-permute-start | bytes 6684680 | tf_op jit(solution)/shard_map/ppermute | solution.py:459
  102.2 4.5 %copy-start = (bf16[2,272,512]{2,1,0:T(8,128)(2,1)}, bf16[2,272,512]{2,1,0:T(8,128)(2,1)S(1)}, u32[]{:S(2)}) copy-start(bf16[2,272,512]{2,1,0:T(8,128)(2,1)S(1)} %constant_dynamic-slice_fusion.3.refs_14_) | copy-start | bytes 1671172
  102.2 21.8 %collective-permute-start.21 = (bf16[2,272,512]{2,1,0:T(8,128)(2,1)S(1)}, bf16[2,272,512]{2,1,0:T(8,128)(2,1)S(1)}, u32[]{:S(2)}, u32[]{:S(2)}) collective-permute-start(bf16[2,272,512]{2,1,0:T(8,128)(2,1)S(1)} %constant_dynamic-slice_fusion.3.refs_14_), channel_id=1, source_target_pairs={{0,4},{4,0},{8,12},{12,8},{16,20},{20,16},{24,28},{28,24},{1,5},{5... | collective-permute-start | bytes 1671176 | tf_op jit(solution)/shard_map/ppermute | solution.py:459
  104.9 19.2 %collective-permute-start.18 = (bf16[544,512]{1,0:T(8,128)(2,1)S(1)}, bf16[544,512]{1,0:T(8,128)(2,1)S(1)}, u32[]{:S(2)}, u32[]{:S(2)}) collective-permute-start(bf16[544,512]{1,0:T(8,128)(2,1)S(1)} %slice_bitcast_fusion.1), channel_id=1, source_target_pairs={{0,2},{1,3},{2,0},{3,1},{4,6},{5,7},{6,4},{7,5},{8,10},{9,11},{10,... | collective-permute-start | bytes 1671176 | tf_op jit(solution)/shard_map/ppermute | solution.py:459
  124.0 16.7 %copy-start.6 = (bf16[2,272,512]{2,1,0:T(8,128)(2,1)}, bf16[2,272,512]{2,1,0:T(8,128)(2,1)S(1)}, u32[]{:S(2)}) copy-start(bf16[2,272,512]{2,1,0:T(8,128)(2,1)S(1)} %collective-permute-done.21) | copy-start | bytes 1671172
  140.7 13.4 %collective-permute-start.19 = (bf16[2,576,512]{2,1,0:T(8,128)(2,1)}, bf16[2,576,512]{2,1,0:T(8,128)(2,1)S(1)}, u32[]{:S(2)}, u32[]{:S(2)}) collective-permute-start(bf16[2,576,512]{2,1,0:T(8,128)(2,1)} %get-tuple-element.116), channel_id=1, source_target_pairs={{0,1},{1,0},{2,3},{3,2},{4,5},{5,4},{6,7},{7,6},{8,9},{9,8},{10,11... | collective-permute-start | bytes 3538952 | tf_op jit(solution)/shard_map/ppermute | solution.py:459
  142.0 9.1 %collective-permute-start.22 = (bf16[272,512]{1,0:T(8,128)(2,1)S(1)}, bf16[272,512]{1,0:T(8,128)(2,1)S(1)}, u32[]{:S(2)}, u32[]{:S(2)}) collective-permute-start(bf16[272,512]{1,0:T(8,128)(2,1)S(1)} %slice_bitcast_fusion.4), channel_id=1, source_target_pairs={{0,2},{1,3},{2,0},{3,1},{4,6},{5,7},{6,4},{7,5},{8,10},{9,11},{10,... | collective-permute-start | bytes 835592 | tf_op jit(solution)/shard_map/ppermute | solution.py:459
  143.0 9.0 %collective-permute-start.20 = (bf16[272,512]{1,0:T(8,128)(2,1)}, bf16[272,512]{1,0:T(8,128)(2,1)S(1)}, u32[]{:S(2)}, u32[]{:S(2)}) collective-permute-start(bf16[272,512]{1,0:T(8,128)(2,1)} %constant_dynamic-slice_fusion.2.refs_22_), channel_id=1, source_target_pairs={{0,4},{4,0},{8,12},{12,8},{16,20},{20,16},{24,28},{28,24},{1,5},{5... | collective-permute-start | bytes 835592 | tf_op jit(solution)/shard_map/ppermute | solution.py:459
  143.5 10.6 %copy-start.3 = (bf16[2,576,512]{2,1,0:T(8,128)(2,1)S(1)}, bf16[2,576,512]{2,1,0:T(8,128)(2,1)}, u32[]{:S(2)}) copy-start(bf16[2,576,512]{2,1,0:T(8,128)(2,1)} %get-tuple-element.115) | copy-start | bytes 3538948
  152.5 11.1 %collective-permute-start.24 = (bf16[272,512]{1,0:T(8,128)(2,1)S(1)}, bf16[272,512]{1,0:T(8,128)(2,1)S(1)}, u32[]{:S(2)}, u32[]{:S(2)}) collective-permute-start(bf16[272,512]{1,0:T(8,128)(2,1)S(1)} %fusion.5), channel_id=1, source_target_pairs={{0,8},{4,12},{8,0},{12,4},{16,24},{20,28},{24,16},{28,20},{1,9},{5... | collective-permute-start | bytes 835592 | tf_op jit(solution)/shard_map/ppermute | solution.py:459
  154.5 9.4 %collective-permute-start.23 = (bf16[288,512]{1,0:T(8,128)(2,1)S(1)}, bf16[288,512]{1,0:T(8,128)(2,1)S(1)}, u32[]{:S(2)}, u32[]{:S(2)}) collective-permute-start(bf16[288,512]{1,0:T(8,128)(2,1)S(1)} %slice_bitcast_fusion.2), channel_id=1, source_target_pairs={{0,2},{1,3},{2,0},{3,1},{4,6},{5,7},{6,4},{7,5},{8,10},{9,11},{10,... | collective-permute-start | bytes 884744 | tf_op jit(solution)/shard_map/ppermute | solution.py:459
  155.8 9.7 %collective-permute-start.27 = (bf16[2,144,512]{2,1,0:T(8,128)(2,1)S(1)}, bf16[2,144,512]{2,1,0:T(8,128)(2,1)S(1)}, u32[]{:S(2)}, u32[]{:S(2)}) collective-permute-start(bf16[2,144,512]{2,1,0:T(8,128)(2,1)S(1)} %constant_dynamic-slice_fusion.1.after_ref), channel_id=1, source_target_pairs={{0,4},{4,0},{8,12},{12,8},{16,20},{20,16},{24,28},{28,24},{1,5},{5... | collective-permute-start | bytes 884744 | tf_op jit(solution)/shard_map/ppermute | solution.py:459
  164.1 5.2 %collective-permute-start.26 = (bf16[144,512]{1,0:T(8,128)(2,1)S(1)}, bf16[144,512]{1,0:T(8,128)(2,1)S(1)}, u32[]{:S(2)}, u32[]{:S(2)}) collective-permute-start(bf16[144,512]{1,0:T(8,128)(2,1)S(1)} %constant_dynamic-slice_fusion), channel_id=1, source_target_pairs={{0,4},{4,0},{8,12},{12,8},{16,20},{20,16},{24,28},{28,24},{1,5},{5... | collective-permute-start | bytes 442376 | tf_op jit(solution)/shard_map/ppermute | solution.py:459
  165.7 5.2 %collective-permute-start.28 = (bf16[144,512]{1,0:T(8,128)(2,1)S(1)}, bf16[144,512]{1,0:T(8,128)(2,1)S(1)}, u32[]{:S(2)}, u32[]{:S(2)}) collective-permute-start(bf16[144,512]{1,0:T(8,128)(2,1)S(1)} %slice_bitcast_fusion.6), channel_id=1, source_target_pairs={{0,2},{1,3},{2,0},{3,1},{4,6},{5,7},{6,4},{7,5},{8,10},{9,11},{10,... | collective-permute-start | bytes 442376 | tf_op jit(solution)/shard_map/ppermute | solution.py:459
  166.6 13.4 %collective-permute-start.30 = (bf16[272,512]{1,0:T(8,128)(2,1)S(1)}, bf16[272,512]{1,0:T(8,128)(2,1)S(1)}, u32[]{:S(2)}, u32[]{:S(2)}) collective-permute-start(bf16[272,512]{1,0:T(8,128)(2,1)S(1)} %add_convert_fusion.4), channel_id=1, source_target_pairs={{0,16},{4,20},{8,24},{12,28},{16,0},{20,4},{24,8},{28,12},{1,17},{... | collective-permute-start | bytes 835592 | tf_op jit(solution)/shard_map/ppermute | solution.py:459
  171.1 10.4 %collective-permute-start.29 = (bf16[144,512]{1,0:T(8,128)(2,1)S(1)}, bf16[144,512]{1,0:T(8,128)(2,1)S(1)}, u32[]{:S(2)}, u32[]{:S(2)}) collective-permute-start(bf16[144,512]{1,0:T(8,128)(2,1)S(1)} %fusion.6), channel_id=1, source_target_pairs={{0,8},{4,12},{8,0},{12,4},{16,24},{20,28},{24,16},{28,20},{1,9},{5... | collective-permute-start | bytes 442376 | tf_op jit(solution)/shard_map/ppermute | solution.py:459
  180.1 12.1 %copy-start.11 = (bf16[3,84,512]{2,1,0:T(8,128)(2,1)S(1)}, bf16[3,84,512]{2,1,0:T(8,128)(2,1)}, u32[]{:S(2)}) copy-start(bf16[3,84,512]{2,1,0:T(8,128)(2,1)} %get-tuple-element.131) | copy-start | bytes 774148
  180.1 13.3 %copy-start.10 = (bf16[3,84,512]{2,1,0:T(8,128)(2,1)S(1)}, bf16[3,84,512]{2,1,0:T(8,128)(2,1)}, u32[]{:S(2)}) copy-start(bf16[3,84,512]{2,1,0:T(8,128)(2,1)} %get-tuple-element.142) | copy-start | bytes 774148
  180.1 11.7 %collective-permute-start.37 = (bf16[272,512]{1,0:T(8,128)(2,1)S(1)}, bf16[272,512]{1,0:T(8,128)(2,1)S(1)}, u32[]{:S(2)}, u32[]{:S(2)}) collective-permute-start(bf16[272,512]{1,0:T(8,128)(2,1)S(1)} %add_convert_fusion.3), channel_id=1, source_target_pairs={{0,8},{4,12},{8,0},{12,4},{16,24},{20,28},{24,16},{28,20},{1,9},{5... | collective-permute-start | bytes 835592 | tf_op jit(solution)/shard_map/ppermute | solution.py:459
  181.6 16.8 %copy-start.12 = (bf16[3,84,512]{2,1,0:T(8,128)(2,1)S(1)}, bf16[3,84,512]{2,1,0:T(8,128)(2,1)}, u32[]{:S(2)}) copy-start(bf16[3,84,512]{2,1,0:T(8,128)(2,1)} %get-tuple-element.143) | copy-start | bytes 774148
  181.7 19.3 %copy-start.30 = (bf16[3,84,512]{2,1,0:T(8,128)(2,1)S(1)}, bf16[3,84,512]{2,1,0:T(8,128)(2,1)}, u32[]{:S(2)}) copy-start(bf16[3,84,512]{2,1,0:T(8,128)(2,1)} %get-tuple-element.140) | copy-start | bytes 774148
  181.7 10.4 %collective-permute-start.36 = (bf16[144,512]{1,0:T(8,128)(2,1)S(1)}, bf16[144,512]{1,0:T(8,128)(2,1)S(1)}, u32[]{:S(2)}, u32[]{:S(2)}) collective-permute-start(bf16[144,512]{1,0:T(8,128)(2,1)S(1)} %add_convert_fusion.7), channel_id=1, source_target_pairs={{0,16},{4,20},{8,24},{12,28},{16,0},{20,4},{24,8},{28,12},{1,17},{... | collective-permute-start | bytes 442376 | tf_op jit(solution)/shard_map/ppermute | solution.py:459
  192.1 5.2 %collective-permute-start.38 = (bf16[144,512]{1,0:T(8,128)(2,1)S(1)}, bf16[144,512]{1,0:T(8,128)(2,1)S(1)}, u32[]{:S(2)}, u32[]{:S(2)}) collective-permute-start(bf16[144,512]{1,0:T(8,128)(2,1)S(1)} %add_convert_fusion.6), channel_id=1, source_target_pairs={{0,8},{4,12},{8,0},{12,4},{16,24},{20,28},{24,16},{28,20},{1,9},{5... | collective-permute-start | bytes 442376 | tf_op jit(solution)/shard_map/ppermute | solution.py:459
  192.2 7.6 %collective-permute-start.25 = (bf16[3,84,512]{2,1,0:T(8,128)(2,1)S(1)}, bf16[3,84,512]{2,1,0:T(8,128)(2,1)S(1)}, u32[]{:S(2)}, u32[]{:S(2)}) collective-permute-start(bf16[3,84,512]{2,1,0:T(8,128)(2,1)S(1)} %copy-done.11), channel_id=1, source_target_pairs={{0,2},{1,3},{2,0},{3,1},{4,6},{5,7},{6,4},{7,5},{8,10},{9,11},{10,... | collective-permute-start | bytes 774152 | tf_op jit(solution)/shard_map/ppermute | solution.py:459
  193.4 7.5 %collective-permute-start.34 = (bf16[3,84,512]{2,1,0:T(8,128)(2,1)S(1)}, bf16[3,84,512]{2,1,0:T(8,128)(2,1)S(1)}, u32[]{:S(2)}, u32[]{:S(2)}) collective-permute-start(bf16[3,84,512]{2,1,0:T(8,128)(2,1)S(1)} %copy-done.10), channel_id=1, source_target_pairs={{0,1},{1,0},{2,3},{3,2},{4,5},{5,4},{6,7},{7,6},{8,9},{9,8},{10,11... | collective-permute-start | bytes 774152 | tf_op jit(solution)/shard_map/ppermute | solution.py:459
  197.4 24.0 %collective-permute-start.39 = (bf16[2,144,512]{2,1,0:T(8,128)(2,1)S(1)}, bf16[2,144,512]{2,1,0:T(8,128)(2,1)S(1)}, u32[]{:S(2)}, u32[]{:S(2)}) collective-permute-start(bf16[2,144,512]{2,1,0:T(8,128)(2,1)S(1)} %bitcast.84), channel_id=1, source_target_pairs={{0,4},{4,0},{8,12},{12,8},{16,20},{20,16},{24,28},{28,24},{1,5},{5... | collective-permute-start | bytes 884744 | tf_op jit(solution)/shard_map/ppermute | solution.py:459
  198.4 8.8 %collective-permute-start.35 = (bf16[3,84,512]{2,1,0:T(8,128)(2,1)S(1)}, bf16[3,84,512]{2,1,0:T(8,128)(2,1)S(1)}, u32[]{:S(2)}, u32[]{:S(2)}) collective-permute-start(bf16[3,84,512]{2,1,0:T(8,128)(2,1)S(1)} %copy-done.12), channel_id=1, source_target_pairs={{0,3},{1,2},{2,1},{3,0},{4,7},{5,6},{6,5},{7,4},{8,11},{9,10},{10,... | collective-permute-start | bytes 774152 | tf_op jit(solution)/shard_map/ppermute | solution.py:459
  199.8 8.5 %copy-start.13 = (bf16[3,84,512]{2,1,0:T(8,128)(2,1)}, bf16[3,84,512]{2,1,0:T(8,128)(2,1)S(1)}, u32[]{:S(2)}) copy-start(bf16[3,84,512]{2,1,0:T(8,128)(2,1)S(1)} %collective-permute-done.25.b2) | copy-start | bytes 774148
  199.8 10.8 %collective-permute-start.31 = (bf16[3,84,512]{2,1,0:T(8,128)(2,1)}, bf16[3,84,512]{2,1,0:T(8,128)(2,1)S(1)}, u32[]{:S(2)}, u32[]{:S(2)}) collective-permute-start(bf16[3,84,512]{2,1,0:T(8,128)(2,1)} %get-tuple-element.138), channel_id=1, source_target_pairs={{0,1},{1,0},{2,3},{3,2},{4,5},{5,4},{6,7},{7,6},{8,9},{9,8},{10,11... | collective-permute-start | bytes 774152 | tf_op jit(solution)/shard_map/ppermute | solution.py:459
  199.8 12.6 %collective-permute-start.32 = (bf16[3,84,512]{2,1,0:T(8,128)(2,1)}, bf16[3,84,512]{2,1,0:T(8,128)(2,1)S(1)}, u32[]{:S(2)}, u32[]{:S(2)}) collective-permute-start(bf16[3,84,512]{2,1,0:T(8,128)(2,1)} %get-tuple-element.139), channel_id=1, source_target_pairs={{0,2},{1,3},{2,0},{3,1},{4,6},{5,7},{6,4},{7,5},{8,10},{9,11},{10,... | collective-permute-start | bytes 774152 | tf_op jit(solution)/shard_map/ppermute | solution.py:459
  200.9 7.4 %copy-start.14 = (bf16[3,84,512]{2,1,0:T(8,128)(2,1)}, bf16[3,84,512]{2,1,0:T(8,128)(2,1)S(1)}, u32[]{:S(2)}) copy-start(bf16[3,84,512]{2,1,0:T(8,128)(2,1)S(1)} %collective-permute-done.34.b1) | copy-start | bytes 774148
  200.9 17.5 %collective-permute-start.33 = (bf16[3,84,512]{2,1,0:T(8,128)(2,1)S(1)}, bf16[3,84,512]{2,1,0:T(8,128)(2,1)S(1)}, u32[]{:S(2)}, u32[]{:S(2)}) collective-permute-start(bf16[3,84,512]{2,1,0:T(8,128)(2,1)S(1)} %copy-done.30), channel_id=1, source_target_pairs={{0,3},{1,2},{2,1},{3,0},{4,7},{5,6},{6,5},{7,4},{8,11},{9,10},{10,... | collective-permute-start | bytes 774152 | tf_op jit(solution)/shard_map/ppermute | solution.py:459
  207.2 17.3 %collective-permute-start.40 = (bf16[2,272,512]{2,1,0:T(8,128)(2,1)S(1)}, bf16[2,272,512]{2,1,0:T(8,128)(2,1)S(1)}, u32[]{:S(2)}, u32[]{:S(2)}) collective-permute-start(bf16[2,272,512]{2,1,0:T(8,128)(2,1)S(1)} %bitcast.82), channel_id=1, source_target_pairs={{0,4},{4,0},{8,12},{12,8},{16,20},{20,16},{24,28},{28,24},{1,5},{5... | collective-permute-start | bytes 1671176 | tf_op jit(solution)/shard_map/ppermute | solution.py:459
  210.6 7.9 %copy-start.15 = (bf16[3,84,512]{2,1,0:T(8,128)(2,1)}, bf16[3,84,512]{2,1,0:T(8,128)(2,1)S(1)}, u32[]{:S(2)}) copy-start(bf16[3,84,512]{2,1,0:T(8,128)(2,1)S(1)} %collective-permute-done.31.b1) | copy-start | bytes 774148
  212.4 6.1 %copy-start.16 = (bf16[3,84,512]{2,1,0:T(8,128)(2,1)}, bf16[3,84,512]{2,1,0:T(8,128)(2,1)S(1)}, u32[]{:S(2)}) copy-start(bf16[3,84,512]{2,1,0:T(8,128)(2,1)S(1)} %collective-permute-done.32.b2) | copy-start | bytes 774148
  (14 other events, 20.5 us)

commit v2 on v1

v2 whole, which is shorter than its diff:
```python
import functools
import math

import jax
import jax.numpy as jnp
from jax import lax
from jax.experimental import pallas as pl
from jax.experimental.pallas import tpu as pltpu
from jax.sharding import PartitionSpec as P

HD = 64
FRAME_TOK = 56
BF16 = jnp.bfloat16
F32 = jnp.float32
NN = (((1,), (0,)), ((), ()))
NT = (((1,), (1,)), ((), ()))
TN = (((0,), (0,)), ((), ()))
GELU_A = 0.7978845608
GELU_B = 0.044715
VMEM_LIMIT = 40 << 20


def dot(a, b, dims=NN):
    return lax.dot_general(a, b, dims, preferred_element_type=F32)


def stats(x):
    c = x - jnp.mean(x, axis=-1, keepdims=True)
    inv = lax.rsqrt(jnp.mean(c * c, axis=-1, keepdims=True) + 1e-5)
    return c * inv, inv


def norm_back(d, hat, inv, gain):
    e = d * gain
    return inv * (
        e - jnp.mean(e, axis=-1, keepdims=True) - hat * jnp.mean(e * hat, axis=-1, keepdims=True)
    )


def full(a):
    return pl.BlockSpec(a.shape, lambda *_: (0,) * len(a.shape))


def once(shape, at=None):
    return pl.BlockSpec(shape, lambda *_: at or (0,) * len(shape), pipeline_mode=pl.Buffered(1))


def struct(shape, dtype):
    return jax.ShapeDtypeStruct(shape, dtype)


def call(kernel, scalars, args, out_shape, grid=(1,), in_specs=None, out_specs=None, scratch=(), flops=0, name=None, aliases=None, vmem=VMEM_LIMIT):
    in_specs = [full(a) for a in args] if in_specs is None else in_specs
    out_specs = [full(o) for o in out_shape] if out_specs is None else out_specs
    moved = sum(math.prod(a.shape) * a.dtype.itemsize for a in (*args, *out_shape))
    return pl.pallas_call(
        kernel,
        grid_spec=pltpu.PrefetchScalarGridSpec(
            num_scalar_prefetch=len(scalars),
            grid=grid,
            in_specs=in_specs,
            out_specs=out_specs,
            scratch_shapes=list(scratch),
        ),
        out_shape=list(out_shape),
        compiler_params=pltpu.CompilerParams(vmem_limit_bytes=vmem),
        cost_estimate=pl.CostEstimate(flops=flops, bytes_accessed=moved, transcendentals=0),
        name=name,
        input_output_aliases=aliases or {},
    )(*scalars, *args)


def pack_kernel(y_ref, z_ref, wqkv_ref, wout_ref, ub_ref, up_ref, down_ref, own_ref, far_ref):
    d = wout_ref.shape[1]
    half = d // 2
    pitch = half + 16
    ub = ub_ref[...]
    high = ub.astype(BF16).astype(F32)
    row = lax.broadcasted_iota(jnp.int32, (16, d), 0)
    ub = jnp.where(row == 0, high, jnp.where(row == 1, ub - high, 0.0)).astype(BF16)
    side = wout_ref.shape[0]
    for h in range(2):
        here = pl.ds(h * half, half)
        there = pl.ds(h * pitch, half)
        a, b, c = (wqkv_ref[here, pl.ds(128 * j, 128)].astype(F32) for j in range(3))
        low = lax.broadcasted_iota(jnp.int32, a.shape, 1) < HD
        own_ref[there, 0:128] = jnp.where(low, a, b).astype(BF16)
        own_ref[there, 128:256] = pltpu.roll(jnp.where(low, c, a), HD, 1).astype(BF16)
        own_ref[there, 256:384] = jnp.where(low, b, c).astype(BF16)
        for j in range(half // side):
            own_ref[pl.ds(h * pitch + j * side, side), 384:512] = wout_ref[:, pl.ds(h * half + 128 * j, 128)]
        own_ref[pl.ds(h * pitch + half, 16), :] = ub
    own_ref[2 * pitch:2 * pitch + d] = up_ref[...]
    own_ref[2 * pitch + d:2 * pitch + 2 * d] = down_ref[...]
    far_ref[0:2 * pitch] = own_ref[0:2 * pitch]
    at = 2 * pitch + y_ref[0] * d + z_ref[0] * half
    far_ref[2 * pitch:] = own_ref[pl.ds(pl.multiple_of(at, 16), half)]


def pack(y, z, wqkv, wout, ub, up, down):
    d = wqkv.shape[0]
    half = d // 2
    return call(pack_kernel, (y, z), (wqkv, wout, ub, up, down),
                [struct((3 * d + 32, d), BF16), struct((d + half + 32, d), BF16)], name="pack_weights")


def place_kernel(me_ref, b0, b1, b2, b3, out_ref):
    each = b0.shape[0]
    for k, b in enumerate((b0, b1, b2, b3)):
        out_ref[pl.ds((me_ref[0] ^ k) * each, each)] = b[...]


def place(me, blocks):
    each, rows, d = blocks[0].shape
    return call(place_kernel, (me,), blocks, [struct((4 * each, rows, d), BF16)], name="place")[0]


def attn_fwd_kernel(me_ref, ff_ref, t0, t1, t2, t3, w0, w1, w2, w3,
                    g1_ref, b1_ref, bo_ref, g2_ref, b2_ref,
                    qkv_ref, p_ref, o_ref, x_ref, y1_ref, a1_ref, a2_ref, wq_ref, wo_ref, ub_ref,
                    blk_sc, bias_sc, x_sc):
    s = pl.program_id(0)
    _, rows, d = t0.shape
    length = 4 * rows
    me = me_ref[0]

    @pl.when(s == 0)
    def _():
        half = d // 2
        pitch = half + 16
        for k, w in enumerate((w0, w1, w2, w3)):
            for h in range(2):
                wq_ref[pl.ds(h * half, half), pl.ds(384 * k, 384)] = w[pl.ds(h * pitch, half), 0:384]
                for j in range(half // 128):
                    wo_ref[pl.ds(128 * k, 128), pl.ds(h * half + 128 * j, 128)] = w[pl.ds(h * pitch + 128 * j, 128), 384:512]
            ub = w[half:pitch, :].astype(F32)
            ub_ref[k] = jnp.broadcast_to(ub[0:1] + ub[1:2], ub_ref.shape[1:])

    for k, t in enumerate((t0, t1, t2, t3)):
        blk_sc[me ^ k] = t[0].astype(F32)
    for i in range(4):
        x_sc[pl.ds(i * rows, rows), :] = blk_sc[i]
    x_ref[0] = x_sc[...].astype(BF16)
    hat, _ = stats(x_sc[...])
    a1 = (hat * g1_ref[...] + b1_ref[...]).astype(BF16)
    a1_ref[0] = a1
    qkv_ref[0] = dot(a1, wq_ref[...]).astype(BF16)
    start = ff_ref[me * pl.num_programs(0) + s] * FRAME_TOK
    jj = lax.broadcasted_iota(jnp.int32, (length, length), 0)
    ii = lax.broadcasted_iota(jnp.int32, (length, length), 1)
    bias_sc[...] = jnp.where((jj <= ii) & ((jj >= start) | (jj == ii)), 0.0, -1e30)
    lane = lax.broadcasted_iota(jnp.int32, (length, 128), 1)
    for p in range(4):
        q = qkv_ref[0, :, pl.ds(p * 384, 128)]
        k = qkv_ref[0, :, pl.ds(p * 384 + 128, 128)]
        v = qkv_ref[0, :, pl.ds(p * 384 + 256, 128)]
        acc = None
        for h in range(2):
            mine = (lane < HD) if h == 0 else (lane >= HD)
            kh = jnp.where(mine, k, jnp.zeros_like(k))
            vh = jnp.where(mine, v, jnp.zeros_like(v))
            st = dot(kh, q, NT) * (HD ** -0.5) + bias_sc[...]
            e = jnp.exp(st - jnp.max(st, axis=0, keepdims=True))
            prob = (e * (1.0 / jnp.sum(e, axis=0, keepdims=True))).astype(BF16)
            p_ref[0, 2 * p + h] = prob
            part = dot(prob, vh, TN)
            acc = part if acc is None else acc + part
        o_ref[0, :, pl.ds(p * 128, 128)] = acc.astype(BF16)
    y1 = x_sc[...] + dot(o_ref[0], wo_ref[...]) + bo_ref[...]
    y1_ref[0] = y1
    hat, _ = stats(y1)
    a2_ref[0] = (hat * g2_ref[...] + b2_ref[...]).astype(BF16)


def per_seq(a):
    return pl.BlockSpec((1, *a.shape[1:]), lambda s, *_: (s,) + (0,) * (len(a.shape) - 1))


def attn_fwd(me, ff, t, w, g1, b1, bo, g2, b2):
    seqs, rows, d = t[0].shape
    length = 4 * rows
    small = (g1, b1, bo, g2, b2)
    outs = [
        struct((seqs, length, 3 * d), BF16),
        struct((seqs, 8, length, length), BF16),
        struct((seqs, length, d), BF16),
        struct((seqs, length, d), BF16),
        struct((seqs, length, d), F32),
        struct((seqs, length, d), BF16),
        struct((seqs, length, d), BF16),
    ]
    weights = [struct((d, 3 * d), BF16), struct((d, d), BF16), struct((4, 8, d), F32)]
    return call(
        attn_fwd_kernel, (me, ff), (*t, *w, *small), outs + weights, grid=(seqs,),
        in_specs=[per_seq(a) for a in t] + [pl.BlockSpec((d + 32, d), lambda *_: (0, 0))] * 4 + [full(a) for a in small],
        out_specs=[per_seq(o) for o in outs] + [full(o) for o in weights],
        scratch=[pltpu.VMEM((4, rows, d), F32), pltpu.VMEM((length, length), F32), pltpu.VMEM((length, d), F32)],
        flops=2 * seqs * length * (4 * d * d + 2 * d * length), name="attention_forward", vmem=56 << 20)


def ff_kernel(me_ref, y_ref, z_ref, live_ref, w0, w1, a2_, b2_, c2_, a3_, b3_, c3_, ub_ref, a2_ref, c0, c1, c2, c3,
              hm_ref, du_ref, gm_ref, send_ref, keep_ref, w_ref, wbuf, sems, out_sems, blk_sc, row_sc):
    c = pl.program_id(0)
    seqs, length, d = a2_ref.shape
    total = seqs * length
    y, z = y_ref[0], z_ref[0]
    half = d // 2
    pitch = half + 16
    quarter = lambda k, at, side: wbuf.at[k, at, pl.ds(pl.multiple_of(side * half, half), half)]
    copies = [
        [pltpu.make_async_copy(w.at[pl.ds(2 * pitch + n * d, d)], wbuf.at[k, n], sems.at[k, n]) for n in range(2)]
        for k, w in enumerate((w0, w1))
    ] + [
        [pltpu.make_async_copy(a.at[pl.ds(2 * pitch, half)], quarter(k, y, z), sems.at[k, 0]),
         pltpu.make_async_copy(b, quarter(k, y, 1 - z), sems.at[k, 1]),
         pltpu.make_async_copy(c.at[0:half], quarter(k, 1 - y, z), sems.at[k, 2]),
         pltpu.make_async_copy(c.at[half:d], quarter(k, 1 - y, 1 - z), sems.at[k, 3])]
        for k, (a, b, c) in ((2, (a2_, b2_, c2_)), (3, (a3_, b3_, c3_)))
    ]
    out_copies = [pltpu.make_async_copy(wbuf.at[k], w_ref.at[k], out_sems.at[k]) for k in range(4)]
    order = (3, 1, 2, 0)

    @pl.when(c == 0)
    def _():
        for k in order:
            for cp in copies[k]:
                cp.start()
        rows = length // 4
        for s in range(seqs):
            live = live_ref[s] > 0
            for k, cot in enumerate((c0, c1, c2, c3)):
                blk_sc[me_ref[0] ^ k] = jnp.where(live, cot[s].astype(F32), 0.0)
            for i in range(4):
                row_sc[pl.ds(i * rows, rows), :] = blk_sc[i]
            gm_ref[s] = row_sc[...].astype(BF16)

    for n, k in enumerate(order):
        @pl.when(c == n)
        def _():
            for cp in copies[k]:
                cp.wait()
            out_copies[k].start()

    blk = jnp.where(c == 0, 3, jnp.where(c == 1, 1, jnp.where(c == 2, 2, 0)))
    up = wbuf[blk, 0]
    dn = wbuf[blk, 1]
    ub = ub_ref[blk, 0:1]
    ubg = jnp.zeros((8, d), F32)
    for s in range(seqs):
        here = pl.ds(s * length, length)
        pre = dot(a2_ref[s], up) + ub
        dh = dot(gm_ref[s], dn, NT)
        sq = pre * pre
        t = jnp.tanh(pre * (GELU_A + (GELU_A * GELU_B) * sq))
        ht = 0.5 * t + 0.5
        slope = ht + (ht - ht * ht) * (pre * ((2 * GELU_A) + (6.0 * GELU_A * GELU_B) * sq))
        hm_ref[here, :] = (pre * ht).astype(BF16)
        du = (dh * slope).astype(BF16)
        du_ref[here, :] = du
        ubg += jnp.sum(du.astype(F32).reshape(length // 8, 8, d), axis=0)
    upg = dot(a2_ref[...].reshape(total, d), du_ref[...], TN).astype(BF16)
    dng = dot(hm_ref[...], gm_ref[...].reshape(total, d), TN).astype(BF16)
    ubg = jnp.sum(ubg, axis=0, keepdims=True)
    extra = jnp.where(lax.broadcasted_iota(jnp.int32, (64, d), 0) == 0, ubg, 0.0).astype(BF16)

    @pl.when(c < 2)
    def _():
        send_ref[0, 0:d, :] = upg
        send_ref[0, d:2 * d, :] = dng
        send_ref[0, 2 * d:2 * d + 64, :] = extra

    @pl.when(c >= 2)
    def _():
        keep_ref[0, 0:d, :] = upg
        keep_ref[0, d:2 * d, :] = dng
        keep_ref[0, 2 * d:2 * d + 64, :] = extra

    @pl.when(c == 3)
    def _():
        for cp in out_copies:
            cp.wait()


def ff(me, y, z, live, w, ub, a2, cots):
    seqs, length, d = a2.shape
    total = seqs * length
    anys = pl.BlockSpec(memory_space=pl.ANY)
    column = lambda c, *_: (0, jnp.where(c == 0, 3, jnp.where(c == 1, 1, jnp.where(c == 2, 2, 0))))
    outs = [struct((total, 4 * d), BF16)] * 2 + [struct((seqs, length, d), BF16)] + [
        struct((2, 2 * d + 64, d), BF16)] * 2 + [struct((4, 2, d, d), BF16)]
    return call(
        ff_kernel, (me, y, z, live), (*w, ub, a2, *cots), outs, grid=(4,),
        in_specs=[anys] * 8 + [full(a) for a in (ub, a2, *cots)],
        out_specs=[pl.BlockSpec((total, d), column)] * 2 + [
            full(outs[2]),
            pl.BlockSpec((1, 2 * d + 64, d), lambda c, *_: (1 - jnp.minimum(c, 1), 0, 0)),
            pl.BlockSpec((1, 2 * d + 64, d), lambda c, *_: (1 - jnp.maximum(c - 2, 0), 0, 0)),
            anys],
        scratch=[pltpu.VMEM((4, 2, d, d), BF16), pltpu.SemaphoreType.DMA((4, 4)), pltpu.SemaphoreType.DMA((4,)),
                 pltpu.VMEM((4, length // 4, d), F32), pltpu.VMEM((length, d), F32)],
        flops=16 * total * d * d, name="feed_forward", vmem=44 << 20)


def attn_bwd_kernel(me_ref, du_ref, gm_ref, y1_ref, x_ref, g1_ref, g2_ref, w_ref, wq_ref, wo_ref, qkv_ref, p_ref,
                    a1_ref, o_ref, after_ref, d0, d1, d2, d3, send_ref, keep_ref,
                    do_sc, full_sc, blk_sc, small_ref, dqkv_ref, dqkv_sc, ga_sc):
    dxs = (d0, d1, d2, d3)
    s = pl.program_id(0)
    _, length, d = gm_ref.shape
    here = pl.ds(pl.multiple_of(s * length, 16), length)

    @pl.when(s == 0)
    def _():
        small_ref[...] = jnp.zeros_like(small_ref)

    da2 = None
    for k in range(4):
        part = dot(du_ref[:, pl.ds(k * d, d)], w_ref[k, 0], NT)
        da2 = part if da2 is None else da2 + part
    hat, inv = stats(y1_ref[0])
    gy = gm_ref[0].astype(F32)
    dy1 = gy + norm_back(da2, hat, inv, g2_ref[...])
    full_sc[...] = dy1
    ga = dy1.astype(BF16)
    ga_sc[here, :] = ga
    sums = [jnp.sum(v, axis=0, keepdims=True) for v in (da2 * hat, da2, ga.astype(F32), gy)]
    do_sc[...] = dot(ga, wo_ref[...], NT).astype(BF16)
    lane = lax.broadcasted_iota(jnp.int32, (length, 128), 1)
    scale = HD ** -0.5
    for p in range(4):
        q = qkv_ref[0, :, pl.ds(p * 384, 128)]
        k = qkv_ref[0, :, pl.ds(p * 384 + 128, 128)]
        v = qkv_ref[0, :, pl.ds(p * 384 + 256, 128)]
        do = do_sc[:, pl.ds(p * 128, 128)]
        dq = dk = dv = None
        for h in range(2):
            mine = (lane < HD) if h == 0 else (lane >= HD)
            zero = jnp.zeros_like(q)
            qh, kh, vh, doh = (jnp.where(mine, a, zero) for a in (q, k, v, do))
            prob = p_ref[0, 2 * p + h]
            dp = dot(vh, do, NT)
            probs = prob.astype(F32)
            pd = probs * dp
            ds = (pd - probs * jnp.sum(pd, axis=0, keepdims=True)).astype(BF16)
            parts = dot(ds, kh, TN), dot(ds, qh), dot(prob, doh)
            dq, dk, dv = parts if dq is None else (dq + parts[0], dk + parts[1], dv + parts[2])
        dqkv_ref[0, :, pl.ds(p * 384, 128)] = (dq * scale).astype(BF16)
        dqkv_ref[0, :, pl.ds(p * 384 + 128, 128)] = (dk * scale).astype(BF16)
        dqkv_ref[0, :, pl.ds(p * 384 + 256, 128)] = dv.astype(BF16)

    da1 = dot(dqkv_ref[0], wq_ref[...], NT)
    hat, inv = stats(x_ref[0].astype(F32))
    sums += [jnp.sum(v, axis=0, keepdims=True) for v in (da1 * hat, da1)]
    full_sc[...] += norm_back(da1, hat, inv, g1_ref[...])
    spread(dxs, me_ref[0], full_sc, blk_sc)
    row = lax.broadcasted_iota(jnp.int32, (8, d), 0)
    small = jnp.zeros((8, d), F32)
    for n, v in enumerate(sums):
        small = jnp.where(row == n, v, small)
    small_ref[...] += small


    dqkv_sc[here, :] = dqkv_ref[0]

    @pl.when(s == pl.num_programs(0) - 1)
    def _():
        total = dqkv_sc.shape[0]
        extra = jnp.concatenate([small_ref[...], jnp.zeros((56, d), F32)], axis=0).astype(BF16)
        for k in range(4):
            ref = send_ref if k % 2 else keep_ref
            ref[k // 2, 0:384] = dot(dqkv_sc[:, pl.ds(384 * k, 384)], a1_ref[...].reshape(total, d), TN).astype(BF16)
            ref[k // 2, 384:512] = dot(o_ref[:, :, pl.ds(128 * k, 128)].reshape(total, 128), ga_sc[...], TN).astype(BF16)
            ref[k // 2, 512:576] = extra


def attn_bwd(me, after, du, gm, y1, x, g1, g2, w, wq, wo, qkv, p, a1, o):
    seqs, length, d = gm.shape
    total = seqs * length
    anys = pl.BlockSpec(memory_space=pl.ANY)
    outs = [struct((seqs, length // 4, d), BF16)] * 4 + [struct((2, 576, d), BF16)] * 2
    args = [du, gm, y1, x, g1, g2, w, wq, wo, qkv, p, a1, o, after]
    in_specs = [pl.BlockSpec((length, 4 * d), lambda s, *_: (s, 0)), per_seq(gm), per_seq(y1), per_seq(x), full(g1), full(g2),
                once((4, 1, d, d)), once(wq.shape), once(wo.shape), per_seq(qkv), per_seq(p), once(a1.shape), once(o.shape), anys]
    scratch = [pltpu.VMEM((length, d), BF16), pltpu.VMEM((length, d), F32), pltpu.VMEM((4, length // 4, d), F32),
               pltpu.VMEM((8, d), F32), pltpu.VMEM((1, length, 3 * d), BF16), pltpu.VMEM((total, 3 * d), BF16),
               pltpu.VMEM((total, d), BF16)]
    return call(attn_bwd_kernel, (me,), args, outs, grid=(seqs,), in_specs=in_specs,
                out_specs=[per_seq(a) for a in outs[:4]] + [once(a.shape) for a in outs[4:]], scratch=scratch,
                flops=6 * total * (4 * d * d + 2 * d * length), name="attention_backward", vmem=40 << 20)


def spread(refs, me, full_sc, blk_sc):
    rows = blk_sc.shape[1]
    for i in range(4):
        blk_sc[i] = full_sc[pl.ds(i * rows, rows), :]
    for k, out in enumerate(refs):
        out[0] = blk_sc[me ^ k].astype(BF16)


def finish_out_kernel(me_ref, live_ref, hm_ref, w_ref, y1_ref, db_ref, after_ref, o0, o1, o2, o3, full_sc, blk_sc):
    s = pl.program_id(0)
    d = y1_ref.shape[2]
    mlp = None
    for k in range(4):
        part = dot(hm_ref[:, pl.ds(k * d, d)], w_ref[k, 0])
        mlp = part if mlp is None else mlp + part
    full_sc[...] = jnp.where(live_ref[s] > 0, y1_ref[0] + mlp + db_ref[...], 0.0)
    spread((o0, o1, o2, o3), me_ref[0], full_sc, blk_sc)


def finish_out(me, live, after, hm, w, y1, db):
    seqs, length, d = y1.shape
    outs = [struct((seqs, length // 4, d), BF16)] * 4
    return call(
        finish_out_kernel, (me, live), (hm, w, y1, db, after), outs, grid=(seqs,),
        in_specs=[pl.BlockSpec((length, 4 * d), lambda s, *_: (s, 0)),
                  pl.BlockSpec((4, 1, d, d), lambda s, *_: (0, 1, 0, 0)), per_seq(y1), full(db),
                  pl.BlockSpec(memory_space=pl.ANY)],
        out_specs=[per_seq(outs[0])] * 4,
        scratch=[pltpu.VMEM((length, d), F32), pltpu.VMEM((4, length // 4, d), F32)],
        flops=2 * seqs * length * 4 * d * d, name="block_output", vmem=56 << 20)


def hop(value, axis, bit):
    n = lax.axis_size(axis)
    return lax.ppermute(value, axis, [(i, i ^ bit) for i in range(n)])


def split(rows, me):
    rows = rows.transpose(1, 0, 2)
    each = rows.shape[0] // 4
    return [lax.dynamic_slice_in_dim(rows, (me ^ k) * each, each) for k in range(4)]


def scatter(blocks):
    return [blocks[0]] + [hop(blocks[k], "tensor", k) for k in (1, 2, 3)]


def halves(a, side, axis=0):
    n = a.shape[axis] // 2
    return (lax.dynamic_slice_in_dim(a, side * n, n, axis), lax.dynamic_slice_in_dim(a, (1 - side) * n, n, axis))


def join(mine, other, side, axis=0):
    return jnp.where(side == 0, jnp.concatenate([mine, other], axis), jnp.concatenate([other, mine], axis))


def tie(value, *others):
    return lax.optimization_barrier((value, *others))[0]


def plus(a, b):
    return (a.astype(F32) + b.astype(F32)).astype(BF16)


def wait(after, *groups):
    sizes = [len(g) for g in groups]
    flat = lax.optimization_barrier((*[a for g in groups for a in g], *after))
    out = []
    for n in sizes:
        out.append(list(flat[:n]))
        flat = flat[n:]
    return out


class Sum:
    def __init__(self, one, two):
        self.n = lax.axis_size("dp")
        me = lax.axis_index("dp")
        self.one, self.two = one, two
        self.y, self.z = (me // one) % 2, (me // two) % 2

    def step1(self, pair):
        self.middle = middle = pair.shape[1] // 2
        self.a = pair[0, :middle]
        a_other = pair[1, :middle]
        self.b, b_other = halves(pair[:, middle:], self.y, 1)
        self.got = [hop(a_other, "tensor", 2), hop(b_other, "dp", self.one)]
        return [a_other, b_other]

    def step2(self):
        self.a, a_other = halves(plus(self.a, self.got[0]), self.y)
        b = plus(self.b, self.got[1])
        self.b, b_other = b[0], b[1]
        self.got = [hop(a_other, "dp", self.one), hop(b_other, "tensor", 2)]
        return [a_other, b_other]

    def step3(self):
        both = jnp.concatenate([plus(self.a, self.got[0]), plus(self.b, self.got[1])])
        self.part, other = halves(both, self.z)
        self.got = [hop(other, "dp", self.two)]
        return [other]

    def step4(self):
        self.part = plus(self.part, self.got[0])
        top = self.n.bit_length() - 2
        for bit in range(2, top):
            self.part = plus(self.part, hop(self.part, "dp", 1 << bit))
        self.got = [hop(self.part, "dp", 1 << top)]
        return [self.part]

    def step5(self):
        part = plus(self.part, self.got[0])
        n = part.shape[0] // 2
        self.h1, self.h2 = part[:n], part[n:]
        self.got = [hop(self.h1, "dp", self.two), hop(self.h2, "dp", self.one)]
        return [self.h1, self.h2]

    def step6(self):
        pick = lambda mine, other, side: jnp.where(side == 0, jnp.stack([mine, other]), jnp.stack([other, mine]))
        self.h1 = pick(self.h1, self.got[0], self.z)
        self.h2 = pick(self.h2, self.got[1], self.y)
        self.got = [hop(self.h1, "dp", self.one), hop(self.h2, "dp", self.two)]
        return [self.h1, self.h2]

    def result(self):
        pick = lambda mine, other, side, axis: jnp.where(
            side == 0, jnp.stack([mine, other], axis), jnp.stack([other, mine], axis))
        h1 = pick(self.h1, self.got[0], self.y, 1)
        h2 = pick(self.h2, self.got[1], self.z, 0)
        return jnp.concatenate([h1, h2], axis=2).reshape(2 * self.middle, -1)


def shards(
    tokens,
    seq_counts,
    first_frame,
    norm1_gain,
    norm1_bias,
    qkv_weight,
    out_weight,
    out_bias,
    norm2_gain,
    norm2_bias,
    up_weight,
    up_bias,
    down_weight,
    down_bias,
    out_cotangent,
):
    d = tokens.shape[2]
    seqs = tokens.shape[1] // 4
    mine = lax.axis_index("tensor").astype(jnp.int32)
    me = mine.reshape(1)
    y = lax.axis_index("dp").astype(jnp.int32) % 2
    bit = y.reshape(1)
    live = ((mine * seqs + jnp.arange(seqs, dtype=jnp.int32)) < seq_counts[0]).astype(jnp.int32)
    row = lambda a: a.reshape(1, -1)
    g1, b1, bo, g2, b2, db = map(row, (norm1_gain, norm1_bias, out_bias, norm2_gain, norm2_bias, down_bias))

    z = (lax.axis_index("dp").astype(jnp.int32) // 2) % 2
    zbit = z.reshape(1)
    own, far = pack(bit, zbit, qkv_weight, out_weight, row(up_bias), up_weight, down_weight)
    far_a = hop(far, "tensor", 2)
    near = hop(own, "tensor", 1)
    t = split(tie(tokens, near), mine)
    t = [t[0]] + [hop(t[k], "tensor", k) for k in (1, 2, 3)]
    far_2 = far_a[d + 32:]
    far_b = hop(far_2, "dp", 2)
    diag_a, diag_b = hop(tie(far_a, t[1]), "tensor", 1), hop(far_b, "tensor", 1)
    far_c = hop(tie(jnp.concatenate([far_2, far_b]), diag_a, t[1], t[2], t[3]), "dp", 1)
    w1 = (own, near, far_a, diag_a)
    cot = scatter(split(tie(out_cotangent, t[1], t[2]), mine))

    qkv, p, o, x, y1, a1, a2, wq, wo, ub = attn_fwd(me, first_frame, t, w1, g1, b1, bo, g2, b2)
    w2 = (own, near, far_a, far_b, far_c, diag_a, diag_b, hop(tie(far_c, a2, *cot), "tensor", 1))
    hm, du, gm, send, keep, w2 = ff(me, bit, zbit, live, w2, ub, a2, cot)

    m, a = Sum(1, 2), Sum(2, 1)
    got = hop(send, "tensor", 1)
    out = finish_out(me, live, a2, hm, w2, y1, db)
    ((got,),) = wait(out, [got])
    sent = m.step1(plus(keep, got))
    out = scatter(tie(out, *sent))
    *dx, send, keep = attn_bwd(me, tie(*sent), du, gm, y1, x, g1, g2, w2, wq, wo, qkv, p, a1, o)
    m.got, out = wait([send], m.got, out)
    sent = m.step2()
    got = hop(tie(send, *sent), "tensor", 1)
    ((got,),) = wait(sent, [got])
    sent = a.step1(plus(keep, got))
    block_output = place(me, tie(out, *sent)).transpose(1, 0, 2)
    (m.got,) = wait([block_output], m.got)
    sent = m.step3()
    (a.got,) = wait(sent, a.got)
    sent = a.step2()
    dx = scatter(tie(dx, *sent))
    (m.got,) = wait(sent, m.got)
    sent = m.step4()
    (a.got,) = wait(sent, a.got)
    sent = a.step3()
    a.got, dx = wait(sent, a.got, dx)
    sent = a.step4()
    input_grad = place(me, tie(dx, *sent)).transpose(1, 0, 2)
    (m.got,) = wait([input_grad], m.got)
    sent = m.step5()
    (a.got,) = wait(sent, a.got)
    sent = a.step5()
    (m.got,) = wait(sent, m.got)
    sent = m.step6()
    (a.got,) = wait(sent, a.got)
    sent = a.step6()
    (m.got,) = wait(sent, m.got)
    mlp_grad = m.result()
    (a.got,) = wait([mlp_grad], a.got)
    attn_grads = a.result()

    mlp_grad = mlp_grad.astype(F32)
    attn_grads = attn_grads.astype(F32)
    heads = attn_grads[:384].reshape(3, 2, HD, d).transpose(1, 0, 2, 3).reshape(384, d)
    norm2_g, norm2_b, out_b, down_b, norm1_g, norm1_b = (attn_grads[512 + i] for i in range(6))
    return (
        block_output,
        input_grad,
        heads.T,
        attn_grads[384:512],
        mlp_grad[:d],
        mlp_grad[d:2 * d],
        mlp_grad[2 * d],
        out_b,
        down_b,
        norm1_g,
        norm1_b,
        norm2_g,
        norm2_b,
    )


def solution(mesh):
    return jax.shard_map(
        shards,
        mesh=mesh,
        in_specs=(
            P("tensor", "dp", None),
            P("dp"),
            P("dp"),
            P(),
            P(),
            P(None, "tensor"),
            P("tensor", None),
            P(),
            P(),
            P(),
            P(None, "tensor"),
            P("tensor"),
            P("tensor", None),
            P(),
            P("tensor", "dp", None),
        ),
        out_specs=(
            P("tensor", "dp", None),
            P("tensor", "dp", None),
            P(None, "tensor"),
            P("tensor", None),
            P(None, "tensor"),
            P("tensor", None),
            P("tensor"),
            P(),
            P(),
            P(),
            P(),
            P(),
            P(),
        ),
        check_vma=False,
    )
```

time: 229 us -> 192 us (0.84)
  waiting for transfers between devices: 83.7 us -> 64.1 us
  Pallas kernels: 84.2 us -> 65.8 us
    ppermute x41, waiting for transfers between devices: 83.7 us -> 64.1 us  [hop(): return lax.ppermute(value, axis, [(i, i ^ bit) for i in range(n)])]
    pallas_call x9 -> x7, Pallas kernels: 84.2 us -> 65.8 us  [call(): pl.pallas_call(kernel, grid_spec=pltpu.PrefetchScalarGridSpec(num_scalar_...]
    unnamed x76 -> x87, local copies, waits for them, and re-layouts: 6.65 us -> 10.2 us
  transfers between devices with their start and end apart: 41 -> 41, of which waited for: 19 -> 19; matrix products, arithmetic and copies ran while one was open for 5% -> 4% of each run, Pallas kernels for 20% -> 26%
where the time goes in v2:
time: 192 us
  Pallas kernels  65.8 us (34%)
  waiting for transfers between devices  64.1 us (33%)
  starting transfers between devices  35.7 us (19%)
  local copies, waits for them, and re-layouts  17.8 us (9%)
  other arithmetic  6.28 us (3%)
  between operations  2.16 us (1%)
    pallas_call x7, Pallas kernels, call(): pl.pallas_call(kernel, grid_spec=pltpu.PrefetchScalarGridSpec(num_scalar_...  65.8 us
    ppermute x41, waiting for transfers between devices, hop(): return lax.ppermute(value, axis, [(i, i ^ bit) for i in range(n)])  64.1 us
    ppermute x41, starting transfers between devices, hop(): return lax.ppermute(value, axis, [(i, i ^ bit) for i in range(n)])  35.7 us
    unnamed x87, local copies, waits for them, and re-layouts  10.2 us
  transfers between devices with their start and end apart: 41, of which 19 were waited for; matrix products, arithmetic and copies ran while one was open for 4% of the time, Pallas kernels for 26%

profile of v2, /device:TPU:0, one launch (start us, length us, event | category | flops | bytes accessed | tf_op | source)
XLA Modules:
  0.0 191.8 jit_solution(1446646375333354049)
XLA Ops:
  0.7 1.0 copy-done.2
  1.7 1.0 copy-done.3
  2.8 1.0 copy-done.4
  3.8 0.9 copy-done.6
  4.7 0.7 copy-done.9
  6.2 2.6 %collective-permute-start.1 = (bf16[800,512]{1,0:T(8,128)(2,1)S(1)}, bf16[800,512]{1,0:T(8,128)(2,1)S(1)}, u32[]{:S(2)}, u32[]{:S(2)}) collective-permute-start(bf16[800,512]{1,0:T(8,128)(2,1)S(1)} %get-tuple-element.95), channel_id=1, source_target_pairs={{0,2},{1,3},{2,0},{3,1},{4,6},{5,7},{6,4},{7,5},{8,10},{9,11},{10,... | collective-permute-start | bytes 2457608 | tf_op jit(solution)/shard_map/ppermute | solution.py:426
  8.7 0.6 collective-permute-done.w1
  9.4 2.0 %dynamic-slice_bitcast_fusion.4 = (bf16[3,84,512]{2,1,0:T(8,128)(2,1)}, bf16[3,84,512]{2,1,0:T(8,128)(2,1)S(1)}, bf16[3,84,512]{2,1,0:T(8,128)(2,1)S(1)}, bf16[3,84,512]{2,1,0:T(8,128)(2,1)S(1)}) fusion(bf16[84,12,512]{2,0,1:T(8,128)(2,1)} %param.15, s32[]{:T(128)S(6)} %select_n.177, s32[]{:T(128)S(6)} %select_n.176, s32[]{:T(128)S(6)} %select_n.175, ...), kind=kLoop, calls=%fused_computation.50 | loop fusion | bytes 2064400 | tf_op jit(solution)/shard_map/dynamic_slice | solution.py:432
  11.7 15.8 %collective-permute-done.1.w2.a2_ = bf16[800,512]{1,0:T(8,128)(2,1)S(1)} collective-permute-done((bf16[800,512]{1,0:T(8,128)(2,1)S(1)}, bf16[800,512]{1,0:T(8,128)(2,1)S(1)}, u32[]{:S(2)}, u32[]{:S(2)}) %collective-permute-start.1) | collective-permute-done | bytes 819232 | tf_op jit(solution)/shard_map/ppermute | solution.py:426
  27.7 1.9 collective-permute-start.2
  29.6 1.5 collective-permute-start.5
  31.2 5.4 %collective-permute-done.2.b2_ = bf16[256,512]{1,0:T(8,128)(2,1)S(1)} collective-permute-done((bf16[256,512]{1,0:T(8,128)(2,1)S(1)}, bf16[256,512]{1,0:T(8,128)(2,1)S(1)}, u32[]{:S(2)}, u32[]{:S(2)}) %collective-permute-start.2) | collective-permute-done | bytes 262176 | tf_op jit(solution)/shard_map/ppermute | solution.py:426
  36.6 2.3 %collective-permute-done.5.t2 = bf16[3,84,512]{2,1,0:T(8,128)(2,1)S(1)} collective-permute-done((bf16[3,84,512]{2,1,0:T(8,128)(2,1)S(1)}, bf16[3,84,512]{2,1,0:T(8,128)(2,1)S(1)}, u32[]{:S(2)}, u32[]{:S(2)}) %collective-permute-start.5) | collective-permute-done | bytes 258080 | tf_op jit(solution)/shard_map/ppermute | solution.py:426
  38.9 4.3 %collective-permute-done.6.t3 = bf16[3,84,512]{2,1,0:T(8,128)(2,1)S(1)} collective-permute-done((bf16[3,84,512]{2,1,0:T(8,128)(2,1)S(1)}, bf16[3,84,512]{2,1,0:T(8,128)(2,1)S(1)}, u32[]{:S(2)}, u32[]{:S(2)}) %collective-permute-start.6) | collective-permute-done | bytes 258080 | tf_op jit(solution)/shard_map/ppermute | solution.py:426
  43.3 1.6 collective-permute-start.7
  44.9 1.6 collective-permute-start.10
  47.2 16.3 %attention_forward.1 = (bf16[3,336,1536]{2,1,0:T(8,128)(2,1)}, bf16[3,8,336,336]{3,2,1,0:T(8,128)(2,1)}, bf16[3,336,512]{2,1,0:T(8,128)(2,1)}, bf16[3,336,512]{2...) custom-call(s32[1]{0:T(128)} %bitcast.me_ref, ...), custom_call_target="tpu_custom_call" | custom-call | flops 2807562240 | bytes 22763520 | tf_op jit(solution)/shard_map/attention_forward/pallas_call | solution.py:56
  64.8 1.1 collective-permute-done.8.b3_
  65.9 1.2 copy-done.1
  67.1 1.1 copy-done.14
  68.3 0.8 copy-done.30
  69.1 15.4 %feed_forward.1 = (bf16[1008,2048]{1,0:T(8,128)(2,1)}, bf16[1008,2048]{1,0:T(8,128)(2,1)}, bf16[3,336,512]{2,1,0:T(8,128)(2,1)S(1)}, bf16[2,1088,512]{2,1,0:T(8,...) custom-call(s32[1]{0:T(128)} %bitcast.me_ref, s32[1]{0:T(128)} %bitcast.1.y_ref, ...), custom_call_target="tpu_custom_call" | custom-call | flops 4227858432 | bytes 26492928 | tf_op jit(solution)/shard_map/feed_forward/pallas_call | solution.py:56
  84.6 1.0 copy-done.27
  85.7 7.3 %block_output.1 = (bf16[3,84,512]{2,1,0:T(8,128)(2,1)}, bf16[3,84,512]{2,1,0:T(8,128)(2,1)}, bf16[3,84,512]{2,1,0:T(8,128)(2,1)}, bf16[3,84,512]{2,1,0:T(8,128)(2,1)}) custom-call(s32[1]{0:T(128)} %bitcast.me_ref, s32[3]{0:T(128)} %copy-done.10, bf16[1008,2048]{1,0:T(8,128)(2,1)} %get-tuple-element.105.hm_ref, ...), custom_call_target="tpu_custom_call" | custom-call | flops 2113929216 | bytes 12453888 | tf_op jit(solution)/shard_map/block_output/pallas_call | solution.py:56
  93.1 0.6 add_convert_fusion
  94.0 0.6 collective-permute-start.15
  94.6 1.5 collective-permute-start.14
  96.1 0.6 collective-permute-start.17
  96.7 1.3 collective-permute-start.18
  98.0 24.4 %attention_backward.1 = (bf16[3,84,512]{2,1,0:T(8,128)(2,1)S(1)}, bf16[3,84,512]{2,1,0:T(8,128)(2,1)S(1)}, bf16[3,84,512]{2,1,0:T(8,128)(2,1)S(1)}, bf16[3,84,51...) custom-call(s32[1]{0:T(128)} %bitcast.me_ref, ...), custom_call_target="tpu_custom_call" | custom-call | flops 8422686720 | bytes 29081600 | tf_op jit(solution)/shard_map/attention_backward/pallas_call | solution.py:56
  122.6 0.8 slice_bitcast_fusion.5
  123.6 0.8 constant_dynamic-slice_fusion.2
  125.4 1.5 collective-permute-start.22
  126.9 0.6 collective-permute-done.19
  127.5 1.6 add_convert_fusion.1
  129.8 1.0 collective-permute-start.20
  130.8 1.1 place.2
  131.8 2.8 %collective-permute-done.23 = bf16[272,512]{1,0:T(8,128)(2,1)S(1)} collective-permute-done((bf16[272,512]{1,0:T(8,128)(2,1)}, bf16[272,512]{1,0:T(8,128)(2,1)S(1)}, u32[]{:S(2)}, u32[]{:S(2)}) %collective-permute-start.23) | collective-permute-done | bytes 278560 | tf_op jit(solution)/shard_map/ppermute | solution.py:426
  135.3 3.8 %collective-permute-done.21 = bf16[2,144,512]{2,1,0:T(8,128)(2,1)S(1)} collective-permute-done((bf16[2,144,512]{2,1,0:T(8,128)(2,1)S(1)}, bf16[2,144,512]{2,1,0:T(8,128)(2,1)S(1)}, u32[]{:S(2)}, u32[]{:S(2)}) %collective-permute-start.21) | collective-permute-done | bytes 294944 | tf_op jit(solution)/shard_map/ppermute | solution.py:426
  139.1 1.0 collective-permute-done.20
  140.2 0.6 collective-permute-start.25
  140.9 0.6 collective-permute-start.24
  141.6 1.5 collective-permute-start.29
  143.0 2.1 %collective-permute-done.26 = bf16[272,512]{1,0:T(8,128)(2,1)S(1)} collective-permute-done((bf16[272,512]{1,0:T(8,128)(2,1)S(1)}, bf16[272,512]{1,0:T(8,128)(2,1)S(1)}, u32[]{:S(2)}, u32[]{:S(2)}) %collective-permute-start.26) | collective-permute-done | bytes 278560 | tf_op jit(solution)/shard_map/ppermute | solution.py:426
  145.5 0.8 collective-permute-done.25
  146.3 1.4 collective-permute-done.24
  147.9 1.6 collective-permute-start.27
  149.5 2.6 %collective-permute-start.32 = (bf16[272,512]{1,0:T(8,128)(2,1)S(1)}, bf16[272,512]{1,0:T(8,128)(2,1)S(1)}, u32[]{:S(2)}, u32[]{:S(2)}) collective-permute-start(bf16[272,512]{1,0:T(8,128)(2,1)S(1)} %add_convert_fusion.5), channel_id=1, source_target_pairs={{0,16},{4,20},{8,24},{12,28},{16,0},{20,4},{24,8},{28,12},{1,17},{... | collective-permute-start | bytes 835592 | tf_op jit(solution)/shard_map/ppermute | solution.py:426
  152.1 4.1 %collective-permute-done.30.b3 = bf16[3,84,512]{2,1,0:T(8,128)(2,1)S(1)} collective-permute-done((bf16[3,84,512]{2,1,0:T(8,128)(2,1)S(1)}, bf16[3,84,512]{2,1,0:T(8,128)(2,1)S(1)}, u32[]{:S(2)}, u32[]{:S(2)}) %collective-permute-start.30) | collective-permute-done | bytes 258080 | tf_op jit(solution)/shard_map/ppermute | solution.py:426
  156.4 2.6 %collective-permute-start.31 = (bf16[144,512]{1,0:T(8,128)(2,1)S(1)}, bf16[144,512]{1,0:T(8,128)(2,1)S(1)}, u32[]{:S(2)}, u32[]{:S(2)}) collective-permute-start(bf16[144,512]{1,0:T(8,128)(2,1)S(1)} %add_convert_fusion.8), channel_id=1, source_target_pairs={{0,16},{4,20},{8,24},{12,28},{16,0},{20,4},{24,8},{28,12},{1,17},{... | collective-permute-start | bytes 442376 | tf_op jit(solution)/shard_map/ppermute | solution.py:426
  158.9 1.1 place.3
  160.0 7.4 %collective-permute-done.32 = bf16[272,512]{1,0:T(8,128)(2,1)S(1)} collective-permute-done((bf16[272,512]{1,0:T(8,128)(2,1)S(1)}, bf16[272,512]{1,0:T(8,128)(2,1)S(1)}, u32[]{:S(2)}, u32[]{:S(2)}) %collective-permute-start.32) | collective-permute-done | bytes 278560 | tf_op jit(solution)/shard_map/ppermute | solution.py:426
  167.5 0.9 collective-permute-start.35
  168.9 1.5 collective-permute-done.31
  171.1 0.7 collective-permute-start.34
  171.7 1.6 collective-permute-done.35
  173.7 1.9 %collective-permute-start.40 = (bf16[2,136,512]{2,1,0:T(8,128)(2,1)S(1)}, bf16[2,136,512]{2,1,0:T(8,128)(2,1)S(1)}, u32[]{:S(2)}, u32[]{:S(2)}) collective-permute-start(bf16[2,136,512]{2,1,0:T(8,128)(2,1)S(1)} %maximum_select_fusion.5), channel_id=1, source_target_pairs={{0,8},{4,12},{8,0},{12,4},{16,24},{20,28},{24,16},{28,20},{1,9},{5... | collective-permute-start | bytes 835592 | tf_op jit(solution)/shard_map/ppermute | solution.py:426
  176.4 1.6 collective-permute-start.38
  178.3 6.9 %collective-permute-done.38 = bf16[2,72,512]{2,1,0:T(8,128)(2,1)S(1)} collective-permute-done((bf16[2,72,512]{2,1,0:T(8,128)(2,1)S(1)}, bf16[2,72,512]{2,1,0:T(8,128)(2,1)S(1)}, u32[]{:S(2)}, u32[]{:S(2)}) %collective-permute-start.38) | collective-permute-done | bytes 147488 | tf_op jit(solution)/shard_map/ppermute | solution.py:426
  185.6 0.7 slice.120
  186.3 1.1 copy.31
  187.5 0.6 fusion.9
  188.1 1.1 maximum_select_fusion
  189.8 1.5 fusion.8
  (166 shorter events, 10.6 us)
Async XLA Ops:
  5.6 22.0 %copy-start.11 = (bf16[1568,512]{1,0:T(8,128)(2,1)}, bf16[1568,512]{1,0:T(8,128)(2,1)S(1)}, u32[]{:S(2)}) copy-start(bf16[1568,512]{1,0:T(8,128)(2,1)S(1)} %get-tuple-element.94.w0) | copy-start | bytes 4816900
  5.6 3.7 %collective-permute-start = (bf16[1568,512]{1,0:T(8,128)(2,1)S(1)}, bf16[1568,512]{1,0:T(8,128)(2,1)}, u32[]{:S(2)}, u32[]{:S(2)}) collective-permute-start(bf16[1568,512]{1,0:T(8,128)(2,1)S(1)} %get-tuple-element.94.w0), channel_id=1, source_target_pairs={{0,1},{1,0},{2,3},{3,2},{4,5},{5,4},{6,7},{7,6},{8,9},{9,8},{10,11... | collective-permute-start | bytes 4816904 | tf_op jit(solution)/shard_map/ppermute | solution.py:426
  6.2 21.4 %collective-permute-start.1 = (bf16[800,512]{1,0:T(8,128)(2,1)S(1)}, bf16[800,512]{1,0:T(8,128)(2,1)S(1)}, u32[]{:S(2)}, u32[]{:S(2)}) collective-permute-start(bf16[800,512]{1,0:T(8,128)(2,1)S(1)} %get-tuple-element.95), channel_id=1, source_target_pairs={{0,2},{1,3},{2,0},{3,1},{4,6},{5,7},{6,4},{7,5},{8,10},{9,11},{10,... | collective-permute-start | bytes 2457608 | tf_op jit(solution)/shard_map/ppermute | solution.py:426
  11.4 33.5 %copy-start.36 = (bf16[84,12,512]{2,0,1:T(8,128)(2,1)S(1)}, bf16[84,12,512]{2,0,1:T(8,128)(2,1)}, u32[]{:S(2)}) copy-start(bf16[84,12,512]{2,0,1:T(8,128)(2,1)} %param.29) | copy-start | bytes 3096580
  11.4 16.2 %collective-permute-start.3 = (bf16[3,84,512]{2,1,0:T(8,128)(2,1)S(1)}, bf16[3,84,512]{2,1,0:T(8,128)(2,1)S(1)}, u32[]{:S(2)}, u32[]{:S(2)}) collective-permute-start(bf16[3,84,512]{2,1,0:T(8,128)(2,1)S(1)} %get-tuple-element.216), channel_id=1, source_target_pairs={{0,1},{1,0},{2,3},{3,2},{4,5},{5,4},{6,7},{7,6},{8,9},{9,8},{10,11... | collective-permute-start | bytes 774152 | tf_op jit(solution)/shard_map/ppermute | solution.py:426
  27.6 17.4 %copy-start.7 = (bf16[800,512]{1,0:T(8,128)(2,1)}, bf16[800,512]{1,0:T(8,128)(2,1)S(1)}, u32[]{:S(2)}) copy-start(bf16[800,512]{1,0:T(8,128)(2,1)S(1)} %collective-permute-done.1.w2.a2_) | copy-start | bytes 2457604
  27.6 17.4 %copy-start.37 = (bf16[3,84,512]{2,1,0:T(8,128)(2,1)}, bf16[3,84,512]{2,1,0:T(8,128)(2,1)S(1)}, u32[]{:S(2)}) copy-start(bf16[3,84,512]{2,1,0:T(8,128)(2,1)S(1)} %collective-permute-done.3.t1) | copy-start | bytes 774148
  27.6 15.7 %collective-permute-start.4 = (bf16[800,512]{1,0:T(8,128)(2,1)S(1)}, bf16[800,512]{1,0:T(8,128)(2,1)S(1)}, u32[]{:S(2)}, u32[]{:S(2)}) collective-permute-start(bf16[800,512]{1,0:T(8,128)(2,1)S(1)} %collective-permute-done.1.w2.a2_), channel_id=1, source_target_pairs={{0,1},{1,0},{2,3},{3,2},{4,5},{5,4},{6,7},{7,6},{8,9},{9,8},{10,11... | collective-permute-start | bytes 2457608 | tf_op jit(solution)/shard_map/ppermute | solution.py:426
  27.7 8.9 %collective-permute-start.2 = (bf16[256,512]{1,0:T(8,128)(2,1)S(1)}, bf16[256,512]{1,0:T(8,128)(2,1)S(1)}, u32[]{:S(2)}, u32[]{:S(2)}) collective-permute-start(bf16[256,512]{1,0:T(8,128)(2,1)S(1)} %slice.104), channel_id=1, source_target_pairs={{0,8},{4,12},{8,0},{12,4},{16,24},{20,28},{24,16},{28,20},{1,9},{5... | collective-permute-start | bytes 786440 | tf_op jit(solution)/shard_map/ppermute | solution.py:426
  29.6 9.3 %collective-permute-start.5 = (bf16[3,84,512]{2,1,0:T(8,128)(2,1)S(1)}, bf16[3,84,512]{2,1,0:T(8,128)(2,1)S(1)}, u32[]{:S(2)}, u32[]{:S(2)}) collective-permute-start(bf16[3,84,512]{2,1,0:T(8,128)(2,1)S(1)} %get-tuple-element.215), channel_id=1, source_target_pairs={{0,2},{1,3},{2,0},{3,1},{4,6},{5,7},{6,4},{7,5},{8,10},{9,11},{10,... | collective-permute-start | bytes 774152 | tf_op jit(solution)/shard_map/ppermute | solution.py:426
  31.1 12.2 %collective-permute-start.6 = (bf16[3,84,512]{2,1,0:T(8,128)(2,1)S(1)}, bf16[3,84,512]{2,1,0:T(8,128)(2,1)S(1)}, u32[]{:S(2)}, u32[]{:S(2)}) collective-permute-start(bf16[3,84,512]{2,1,0:T(8,128)(2,1)S(1)} %get-tuple-element.214), channel_id=1, source_target_pairs={{0,3},{1,2},{2,1},{3,0},{4,7},{5,6},{6,5},{7,4},{8,11},{9,10},{10,... | collective-permute-start | bytes 774152 | tf_op jit(solution)/shard_map/ppermute | solution.py:426
  38.9 8.2 %copy-start.40 = (bf16[3,84,512]{2,1,0:T(8,128)(2,1)}, bf16[3,84,512]{2,1,0:T(8,128)(2,1)S(1)}, u32[]{:S(2)}) copy-start(bf16[3,84,512]{2,1,0:T(8,128)(2,1)S(1)} %collective-permute-done.5.t2) | copy-start | bytes 774148
  43.3 20.3 %collective-permute-start.7 = (bf16[512,512]{1,0:T(8,128)(2,1)S(1)}, bf16[512,512]{1,0:T(8,128)(2,1)S(1)}, u32[]{:S(2)}, u32[]{:S(2)}) collective-permute-start(bf16[512,512]{1,0:T(8,128)(2,1)S(1)} %pad_maximum_fusion.2), channel_id=1, source_target_pairs={{0,4},{4,0},{8,12},{12,8},{16,20},{20,16},{24,28},{28,24},{1,5},{5... | collective-permute-start | bytes 1572872 | tf_op jit(solution)/shard_map/ppermute | solution.py:426
  44.9 18.6 %collective-permute-start.10 = (bf16[3,84,512]{2,1,0:T(8,128)(2,1)S(1)}, bf16[3,84,512]{2,1,0:T(8,128)(2,1)S(1)}, u32[]{:S(2)}, u32[]{:S(2)}) collective-permute-start(bf16[3,84,512]{2,1,0:T(8,128)(2,1)S(1)} %get-tuple-element.210), channel_id=1, source_target_pairs={{0,2},{1,3},{2,0},{3,1},{4,6},{5,7},{6,4},{7,5},{8,10},{9,11},{10,... | collective-permute-start | bytes 774152 | tf_op jit(solution)/shard_map/ppermute | solution.py:426
  46.5 17.0 %collective-permute-start.11 = (bf16[3,84,512]{2,1,0:T(8,128)(2,1)S(1)}, bf16[3,84,512]{2,1,0:T(8,128)(2,1)S(1)}, u32[]{:S(2)}, u32[]{:S(2)}) collective-permute-start(bf16[3,84,512]{2,1,0:T(8,128)(2,1)S(1)} %get-tuple-element.209), channel_id=1, source_target_pairs={{0,3},{1,2},{2,1},{3,0},{4,7},{5,6},{6,5},{7,4},{8,11},{9,10},{10,... | collective-permute-start | bytes 774152 | tf_op jit(solution)/shard_map/ppermute | solution.py:426
  46.6 16.9 %collective-permute-start.9 = (bf16[3,84,512]{2,1,0:T(8,128)(2,1)S(1)}, bf16[3,84,512]{2,1,0:T(8,128)(2,1)S(1)}, u32[]{:S(2)}, u32[]{:S(2)}) collective-permute-start(bf16[3,84,512]{2,1,0:T(8,128)(2,1)S(1)} %get-tuple-element.211), channel_id=1, source_target_pairs={{0,1},{1,0},{2,3},{3,2},{4,5},{5,4},{6,7},{7,6},{8,9},{9,8},{10,11... | collective-permute-start | bytes 774152 | tf_op jit(solution)/shard_map/ppermute | solution.py:426
  47.2 18.8 %copy-start.8 = (bf16[800,512]{1,0:T(8,128)(2,1)S(1)}, bf16[800,512]{1,0:T(8,128)(2,1)}, u32[]{:S(2)}) copy-start(bf16[800,512]{1,0:T(8,128)(2,1)} %copy-done.7) | copy-start | bytes 2457604
  47.2 18.7 %copy-start.12 = (bf16[1568,512]{1,0:T(8,128)(2,1)S(1)}, bf16[1568,512]{1,0:T(8,128)(2,1)}, u32[]{:S(2)}) copy-start(bf16[1568,512]{1,0:T(8,128)(2,1)} %copy-done.11) | copy-start | bytes 4816900
  63.6 2.4 %collective-permute-start.12 = (bf16[512,512]{1,0:T(8,128)(2,1)S(1)}, bf16[512,512]{1,0:T(8,128)(2,1)S(1)}, u32[]{:S(2)}, u32[]{:S(2)}) collective-permute-start(bf16[512,512]{1,0:T(8,128)(2,1)S(1)} %collective-permute-done.7.c2_), channel_id=1, source_target_pairs={{0,1},{1,0},{2,3},{3,2},{4,5},{5,4},{6,7},{7,6},{8,9},{9,8},{10,11... | collective-permute-start | bytes 1572872 | tf_op jit(solution)/shard_map/ppermute | solution.py:426
  63.6 2.3 %collective-permute-start.8 = (bf16[256,512]{1,0:T(8,128)(2,1)S(1)}, bf16[256,512]{1,0:T(8,128)(2,1)S(1)}, u32[]{:S(2)}, u32[]{:S(2)}) collective-permute-start(bf16[256,512]{1,0:T(8,128)(2,1)S(1)} %collective-permute-done.2.b2_), channel_id=1, source_target_pairs={{0,1},{1,0},{2,3},{3,2},{4,5},{5,4},{6,7},{7,6},{8,9},{9,8},{10,11... | collective-permute-start | bytes 786440 | tf_op jit(solution)/shard_map/ppermute | solution.py:426
  64.8 19.8 %copy-start.10 = (s32[3]{0:T(128)}, s32[3]{0:T(128)S(1)}, u32[]{:S(2)}) copy-start(s32[3]{0:T(128)S(1)} %compare_convert_fusion.live_ref) | copy-start | bytes 40
  85.6 7.4 %collective-permute-start.13 = (bf16[2,1088,512]{2,1,0:T(8,128)(2,1)}, bf16[2,1088,512]{2,1,0:T(8,128)(2,1)S(1)}, u32[]{:S(2)}, u32[]{:S(2)}) collective-permute-start(bf16[2,1088,512]{2,1,0:T(8,128)(2,1)} %get-tuple-element.104), channel_id=1, source_target_pairs={{0,1},{1,0},{2,3},{3,2},{4,5},{5,4},{6,7},{7,6},{8,9},{9,8},{10,11... | collective-permute-start | bytes 6684680 | tf_op jit(solution)/shard_map/ppermute | solution.py:426
  85.7 7.3 %copy-start.33 = (bf16[2,1088,512]{2,1,0:T(8,128)(2,1)S(1)}, bf16[2,1088,512]{2,1,0:T(8,128)(2,1)}, u32[]{:S(2)}) copy-start(bf16[2,1088,512]{2,1,0:T(8,128)(2,1)} %get-tuple-element.103) | copy-start | bytes 6684676
  93.0 4.9 %copy-start.24 = (bf16[3,336,512]{2,1,0:T(8,128)(2,1)S(1)}, bf16[3,336,512]{2,1,0:T(8,128)(2,1)}, u32[]{:S(2)}) copy-start(bf16[3,336,512]{2,1,0:T(8,128)(2,1)} %get-tuple-element.125.o_ref) | copy-start | bytes 3096580
  93.0 4.9 %copy-start.25 = (bf16[3,336,512]{2,1,0:T(8,128)(2,1)S(1)}, bf16[3,336,512]{2,1,0:T(8,128)(2,1)}, u32[]{:S(2)}) copy-start(bf16[3,336,512]{2,1,0:T(8,128)(2,1)} %get-tuple-element.119.x_ref) | copy-start | bytes 3096580
  93.1 4.9 %copy-start.26 = (bf16[3,336,512]{2,1,0:T(8,128)(2,1)S(1)}, bf16[3,336,512]{2,1,0:T(8,128)(2,1)}, u32[]{:S(2)}) copy-start(bf16[3,336,512]{2,1,0:T(8,128)(2,1)} %get-tuple-element.124.a1_ref) | copy-start | bytes 3096580
  93.1 4.9 %copy-start.28 = (bf16[3,336,512]{2,1,0:T(8,128)(2,1)S(1)}, bf16[3,336,512]{2,1,0:T(8,128)(2,1)}, u32[]{:S(2)}) copy-start(bf16[3,336,512]{2,1,0:T(8,128)(2,1)} %copy-done.27) | copy-start | bytes 3096580
  93.7 4.2 %copy-start.23 = (bf16[512,1536]{1,0:T(8,128)(2,1)S(1)}, bf16[512,1536]{1,0:T(8,128)(2,1)}, u32[]{:S(2)}) copy-start(bf16[512,1536]{1,0:T(8,128)(2,1)} %get-tuple-element.120.wq_ref) | copy-start | bytes 4718596
  93.7 4.2 %copy-start.29 = (bf16[512,512]{1,0:T(8,128)(2,1)S(1)}, bf16[512,512]{1,0:T(8,128)(2,1)}, u32[]{:S(2)}) copy-start(bf16[512,512]{1,0:T(8,128)(2,1)} %get-tuple-element.121.wo_ref) | copy-start | bytes 1572868
  93.8 4.1 %copy-start = (f32[3,336,512]{2,1,0:T(8,128)S(1)}, f32[3,336,512]{2,1,0:T(8,128)}, u32[]{:S(2)}) copy-start(f32[3,336,512]{2,1,0:T(8,128)} %get-tuple-element.107.y1_ref) | copy-start | bytes 6193156
  93.8 4.1 %copy-start.21 = (f32[512]{0:T(512)S(1)}, f32[512]{0:T(512)}, u32[]{:S(2)}) copy-start(f32[512]{0:T(512)} %param.18) | copy-start | bytes 6148
  93.9 4.1 %copy-start.22 = (f32[512]{0:T(512)S(1)}, f32[512]{0:T(512)}, u32[]{:S(2)}) copy-start(f32[512]{0:T(512)} %param.23) | copy-start | bytes 6148
  94.0 28.5 %collective-permute-start.15 = (bf16[2,272,512]{2,1,0:T(8,128)(2,1)S(1)}, bf16[2,272,512]{2,1,0:T(8,128)(2,1)S(1)}, u32[]{:S(2)}, u32[]{:S(2)}) collective-permute-start(bf16[2,272,512]{2,1,0:T(8,128)(2,1)S(1)} %constant_dynamic-slice_fusion.3), channel_id=1, source_target_pairs={{0,4},{4,0},{8,12},{12,8},{16,20},{20,16},{24,28},{28,24},{1,5},{5... | collective-permute-start | bytes 1671176 | tf_op jit(solution)/shard_map/ppermute | solution.py:426
  94.6 27.9 %collective-permute-start.14 = (bf16[544,512]{1,0:T(8,128)(2,1)S(1)}, bf16[544,512]{1,0:T(8,128)(2,1)S(1)}, u32[]{:S(2)}, u32[]{:S(2)}) collective-permute-start(bf16[544,512]{1,0:T(8,128)(2,1)S(1)} %slice_bitcast_fusion.1.after_ref), channel_id=1, source_target_pairs={{0,2},{1,3},{2,0},{3,1},{4,6},{5,7},{6,4},{7,5},{8,10},{9,11},{10,... | collective-permute-start | bytes 1671176 | tf_op jit(solution)/shard_map/ppermute | solution.py:426
  96.1 26.4 %collective-permute-start.16 = (bf16[3,84,512]{2,1,0:T(8,128)(2,1)S(1)}, bf16[3,84,512]{2,1,0:T(8,128)(2,1)S(1)}, u32[]{:S(2)}, u32[]{:S(2)}) collective-permute-start(bf16[3,84,512]{2,1,0:T(8,128)(2,1)S(1)} %copy-done.41), channel_id=1, source_target_pairs={{0,1},{1,0},{2,3},{3,2},{4,5},{5,4},{6,7},{7,6},{8,9},{9,8},{10,11... | collective-permute-start | bytes 774152 | tf_op jit(solution)/shard_map/ppermute | solution.py:426
  96.1 26.4 %collective-permute-start.17 = (bf16[3,84,512]{2,1,0:T(8,128)(2,1)S(1)}, bf16[3,84,512]{2,1,0:T(8,128)(2,1)S(1)}, u32[]{:S(2)}, u32[]{:S(2)}) collective-permute-start(bf16[3,84,512]{2,1,0:T(8,128)(2,1)S(1)} %copy-done.39), channel_id=1, source_target_pairs={{0,2},{1,3},{2,0},{3,1},{4,6},{5,7},{6,4},{7,5},{8,10},{9,11},{10,... | collective-permute-start | bytes 774152 | tf_op jit(solution)/shard_map/ppermute | solution.py:426
  96.7 25.8 %collective-permute-start.18 = (bf16[3,84,512]{2,1,0:T(8,128)(2,1)S(1)}, bf16[3,84,512]{2,1,0:T(8,128)(2,1)S(1)}, u32[]{:S(2)}, u32[]{:S(2)}) collective-permute-start(bf16[3,84,512]{2,1,0:T(8,128)(2,1)S(1)} %copy-done.38), channel_id=1, source_target_pairs={{0,3},{1,2},{2,1},{3,0},{4,7},{5,6},{6,5},{7,4},{8,11},{9,10},{10,... | collective-permute-start | bytes 774152 | tf_op jit(solution)/shard_map/ppermute | solution.py:426
  124.5 3.0 %collective-permute-start.19 = (bf16[2,576,512]{2,1,0:T(8,128)(2,1)S(1)}, bf16[2,576,512]{2,1,0:T(8,128)(2,1)}, u32[]{:S(2)}, u32[]{:S(2)}) collective-permute-start(bf16[2,576,512]{2,1,0:T(8,128)(2,1)S(1)} %get-tuple-element.135), channel_id=1, source_target_pairs={{0,1},{1,0},{2,3},{3,2},{4,5},{5,4},{6,7},{7,6},{8,9},{9,8},{10,11... | collective-permute-start | bytes 3538952 | tf_op jit(solution)/shard_map/ppermute | solution.py:426
  124.9 9.7 %collective-permute-start.23 = (bf16[272,512]{1,0:T(8,128)(2,1)}, bf16[272,512]{1,0:T(8,128)(2,1)S(1)}, u32[]{:S(2)}, u32[]{:S(2)}) collective-permute-start(bf16[272,512]{1,0:T(8,128)(2,1)} %slice_bitcast_fusion.5), channel_id=1, source_target_pairs={{0,2},{1,3},{2,0},{3,1},{4,6},{5,7},{6,4},{7,5},{8,10},{9,11},{10,... | collective-permute-start | bytes 835592 | tf_op jit(solution)/shard_map/ppermute | solution.py:426
  125.4 9.2 %collective-permute-start.22 = (bf16[272,512]{1,0:T(8,128)(2,1)}, bf16[272,512]{1,0:T(8,128)(2,1)S(1)}, u32[]{:S(2)}, u32[]{:S(2)}) collective-permute-start(bf16[272,512]{1,0:T(8,128)(2,1)} %constant_dynamic-slice_fusion.2), channel_id=1, source_target_pairs={{0,4},{4,0},{8,12},{12,8},{16,20},{20,16},{24,28},{28,24},{1,5},{5... | collective-permute-start | bytes 835592 | tf_op jit(solution)/shard_map/ppermute | solution.py:426
  129.2 9.9 %collective-permute-start.21 = (bf16[2,144,512]{2,1,0:T(8,128)(2,1)S(1)}, bf16[2,144,512]{2,1,0:T(8,128)(2,1)S(1)}, u32[]{:S(2)}, u32[]{:S(2)}) collective-permute-start(bf16[2,144,512]{2,1,0:T(8,128)(2,1)S(1)} %constant_dynamic-slice_fusion.1), channel_id=1, source_target_pairs={{0,8},{4,12},{8,0},{12,4},{16,24},{20,28},{24,16},{28,20},{1,9},{5... | collective-permute-start | bytes 884744 | tf_op jit(solution)/shard_map/ppermute | solution.py:426
  129.7 4.9 %copy-start.32 = (bf16[2,272,512]{2,1,0:T(8,128)(2,1)S(1)}, bf16[2,272,512]{2,1,0:T(8,128)(2,1)}, u32[]{:S(2)}) copy-start(bf16[2,272,512]{2,1,0:T(8,128)(2,1)} %copy-done.31) | copy-start | bytes 1671172
  129.7 4.9 %copy-start.35 = (bf16[544,512]{1,0:T(8,128)(2,1)S(1)}, bf16[544,512]{1,0:T(8,128)(2,1)}, u32[]{:S(2)}) copy-start(bf16[544,512]{1,0:T(8,128)(2,1)} %copy-done.34) | copy-start | bytes 1671172
  129.8 10.4 %collective-permute-start.20 = (bf16[288,512]{1,0:T(8,128)(2,1)S(1)}, bf16[288,512]{1,0:T(8,128)(2,1)S(1)}, u32[]{:S(2)}, u32[]{:S(2)}) collective-permute-start(bf16[288,512]{1,0:T(8,128)(2,1)S(1)} %slice_bitcast_fusion.3), channel_id=1, source_target_pairs={{0,2},{1,3},{2,0},{3,1},{4,6},{5,7},{6,4},{7,5},{8,10},{9,11},{10,... | collective-permute-start | bytes 884744 | tf_op jit(solution)/shard_map/ppermute | solution.py:426
  135.2 6.4 %copy-start.20 = (bf16[3,84,512]{2,1,0:T(8,128)(2,1)S(1)}, bf16[3,84,512]{2,1,0:T(8,128)(2,1)}, u32[]{:S(2)}) copy-start(bf16[3,84,512]{2,1,0:T(8,128)(2,1)} %copy-done.19) | copy-start | bytes 774148
  135.2 6.4 %copy-start.18 = (bf16[3,84,512]{2,1,0:T(8,128)(2,1)S(1)}, bf16[3,84,512]{2,1,0:T(8,128)(2,1)}, u32[]{:S(2)}) copy-start(bf16[3,84,512]{2,1,0:T(8,128)(2,1)} %copy-done.17) | copy-start | bytes 774148
  135.2 9.9 %copy-start.16 = (bf16[3,84,512]{2,1,0:T(8,128)(2,1)S(1)}, bf16[3,84,512]{2,1,0:T(8,128)(2,1)}, u32[]{:S(2)}) copy-start(bf16[3,84,512]{2,1,0:T(8,128)(2,1)} %copy-done.15) | copy-start | bytes 774148
  135.2 9.9 %collective-permute-start.26 = (bf16[272,512]{1,0:T(8,128)(2,1)S(1)}, bf16[272,512]{1,0:T(8,128)(2,1)S(1)}, u32[]{:S(2)}, u32[]{:S(2)}) collective-permute-start(bf16[272,512]{1,0:T(8,128)(2,1)S(1)} %fusion.5), channel_id=1, source_target_pairs={{0,8},{4,12},{8,0},{12,4},{16,24},{20,28},{24,16},{28,20},{1,9},{5... | collective-permute-start | bytes 835592 | tf_op jit(solution)/shard_map/ppermute | solution.py:426
  140.2 6.0 %collective-permute-start.25 = (bf16[144,512]{1,0:T(8,128)(2,1)S(1)}, bf16[144,512]{1,0:T(8,128)(2,1)S(1)}, u32[]{:S(2)}, u32[]{:S(2)}) collective-permute-start(bf16[144,512]{1,0:T(8,128)(2,1)S(1)} %slice_bitcast_fusion.7), channel_id=1, source_target_pairs={{0,2},{1,3},{2,0},{3,1},{4,6},{5,7},{6,4},{7,5},{8,10},{9,11},{10,... | collective-permute-start | bytes 442376 | tf_op jit(solution)/shard_map/ppermute | solution.py:426
  140.9 6.7 %collective-permute-start.24 = (bf16[144,512]{1,0:T(8,128)(2,1)S(1)}, bf16[144,512]{1,0:T(8,128)(2,1)S(1)}, u32[]{:S(2)}, u32[]{:S(2)}) collective-permute-start(bf16[144,512]{1,0:T(8,128)(2,1)S(1)} %constant_dynamic-slice_fusion), channel_id=1, source_target_pairs={{0,8},{4,12},{8,0},{12,4},{16,24},{20,28},{24,16},{28,20},{1,9},{5... | collective-permute-start | bytes 442376 | tf_op jit(solution)/shard_map/ppermute | solution.py:426
  141.6 10.5 %collective-permute-start.28 = (bf16[3,84,512]{2,1,0:T(8,128)(2,1)S(1)}, bf16[3,84,512]{2,1,0:T(8,128)(2,1)S(1)}, u32[]{:S(2)}, u32[]{:S(2)}) collective-permute-start(bf16[3,84,512]{2,1,0:T(8,128)(2,1)S(1)} %copy-done.20), channel_id=1, source_target_pairs={{0,1},{1,0},{2,3},{3,2},{4,5},{5,4},{6,7},{7,6},{8,9},{9,8},{10,11... | collective-permute-start | bytes 774152 | tf_op jit(solution)/shard_map/ppermute | solution.py:426
  141.6 10.5 %collective-permute-start.29 = (bf16[3,84,512]{2,1,0:T(8,128)(2,1)S(1)}, bf16[3,84,512]{2,1,0:T(8,128)(2,1)S(1)}, u32[]{:S(2)}, u32[]{:S(2)}) collective-permute-start(bf16[3,84,512]{2,1,0:T(8,128)(2,1)S(1)} %copy-done.18), channel_id=1, source_target_pairs={{0,2},{1,3},{2,0},{3,1},{4,6},{5,7},{6,4},{7,5},{8,10},{9,11},{10,... | collective-permute-start | bytes 774152 | tf_op jit(solution)/shard_map/ppermute | solution.py:426
  145.1 11.1 %collective-permute-start.30 = (bf16[3,84,512]{2,1,0:T(8,128)(2,1)S(1)}, bf16[3,84,512]{2,1,0:T(8,128)(2,1)S(1)}, u32[]{:S(2)}, u32[]{:S(2)}) collective-permute-start(bf16[3,84,512]{2,1,0:T(8,128)(2,1)S(1)} %copy-done.16), channel_id=1, source_target_pairs={{0,3},{1,2},{2,1},{3,0},{4,7},{5,6},{6,5},{7,4},{8,11},{9,10},{10,... | collective-permute-start | bytes 774152 | tf_op jit(solution)/shard_map/ppermute | solution.py:426
  147.9 8.3 %collective-permute-start.27 = (bf16[144,512]{1,0:T(8,128)(2,1)S(1)}, bf16[144,512]{1,0:T(8,128)(2,1)S(1)}, u32[]{:S(2)}, u32[]{:S(2)}) collective-permute-start(bf16[144,512]{1,0:T(8,128)(2,1)S(1)} %fusion.7), channel_id=1, source_target_pairs={{0,4},{4,0},{8,12},{12,8},{16,20},{20,16},{24,28},{28,24},{1,5},{5... | collective-permute-start | bytes 442376 | tf_op jit(solution)/shard_map/ppermute | solution.py:426
  149.5 17.8 %collective-permute-start.32 = (bf16[272,512]{1,0:T(8,128)(2,1)S(1)}, bf16[272,512]{1,0:T(8,128)(2,1)S(1)}, u32[]{:S(2)}, u32[]{:S(2)}) collective-permute-start(bf16[272,512]{1,0:T(8,128)(2,1)S(1)} %add_convert_fusion.5), channel_id=1, source_target_pairs={{0,16},{4,20},{8,24},{12,28},{16,0},{20,4},{24,8},{28,12},{1,17},{... | collective-permute-start | bytes 835592 | tf_op jit(solution)/shard_map/ppermute | solution.py:426
  156.4 14.1 %collective-permute-start.31 = (bf16[144,512]{1,0:T(8,128)(2,1)S(1)}, bf16[144,512]{1,0:T(8,128)(2,1)S(1)}, u32[]{:S(2)}, u32[]{:S(2)}) collective-permute-start(bf16[144,512]{1,0:T(8,128)(2,1)S(1)} %add_convert_fusion.8), channel_id=1, source_target_pairs={{0,16},{4,20},{8,24},{12,28},{16,0},{20,4},{24,8},{28,12},{1,17},{... | collective-permute-start | bytes 442376 | tf_op jit(solution)/shard_map/ppermute | solution.py:426
  167.5 5.9 %collective-permute-start.35 = (bf16[136,512]{1,0:T(8,128)(2,1)S(1)}, bf16[136,512]{1,0:T(8,128)(2,1)S(1)}, u32[]{:S(2)}, u32[]{:S(2)}) collective-permute-start(bf16[136,512]{1,0:T(8,128)(2,1)S(1)} %get-tuple-element.222), channel_id=1, source_target_pairs={{0,8},{4,12},{8,0},{12,4},{16,24},{20,28},{24,16},{28,20},{1,9},{5... | collective-permute-start | bytes 417800 | tf_op jit(solution)/shard_map/ppermute | solution.py:426
  168.4 5.3 %collective-permute-start.36 = (bf16[136,512]{1,0:T(8,128)(2,1)S(1)}, bf16[136,512]{1,0:T(8,128)(2,1)S(1)}, u32[]{:S(2)}, u32[]{:S(2)}) collective-permute-start(bf16[136,512]{1,0:T(8,128)(2,1)S(1)} %get-tuple-element.221), channel_id=1, source_target_pairs={{0,4},{4,0},{8,12},{12,8},{16,20},{20,16},{24,28},{28,24},{1,5},{5... | collective-permute-start | bytes 417800 | tf_op jit(solution)/shard_map/ppermute | solution.py:426
  170.5 5.8 %collective-permute-start.33 = (bf16[72,512]{1,0:T(8,128)(2,1)S(1)}, bf16[72,512]{1,0:T(8,128)(2,1)S(1)}, u32[]{:S(2)}, u32[]{:S(2)}) collective-permute-start(bf16[72,512]{1,0:T(8,128)(2,1)S(1)} %get-tuple-element.228), channel_id=1, source_target_pairs={{0,4},{4,0},{8,12},{12,8},{16,20},{20,16},{24,28},{28,24},{1,5},{5... | collective-permute-start | bytes 221192 | tf_op jit(solution)/shard_map/ppermute | solution.py:426
  171.1 5.3 %collective-permute-start.34 = (bf16[72,512]{1,0:T(8,128)(2,1)S(1)}, bf16[72,512]{1,0:T(8,128)(2,1)S(1)}, u32[]{:S(2)}, u32[]{:S(2)}) collective-permute-start(bf16[72,512]{1,0:T(8,128)(2,1)S(1)} %get-tuple-element.227), channel_id=1, source_target_pairs={{0,8},{4,12},{8,0},{12,4},{16,24},{20,28},{24,16},{28,20},{1,9},{5... | collective-permute-start | bytes 221192 | tf_op jit(solution)/shard_map/ppermute | solution.py:426
  173.7 14.3 %collective-permute-start.40 = (bf16[2,136,512]{2,1,0:T(8,128)(2,1)S(1)}, bf16[2,136,512]{2,1,0:T(8,128)(2,1)S(1)}, u32[]{:S(2)}, u32[]{:S(2)}) collective-permute-start(bf16[2,136,512]{2,1,0:T(8,128)(2,1)S(1)} %maximum_select_fusion.5), channel_id=1, source_target_pairs={{0,8},{4,12},{8,0},{12,4},{16,24},{20,28},{24,16},{28,20},{1,9},{5... | collective-permute-start | bytes 835592 | tf_op jit(solution)/shard_map/ppermute | solution.py:426
  175.7 12.4 %collective-permute-start.39 = (bf16[2,136,512]{2,1,0:T(8,128)(2,1)S(1)}, bf16[2,136,512]{2,1,0:T(8,128)(2,1)}, u32[]{:S(2)}, u32[]{:S(2)}) collective-permute-start(bf16[2,136,512]{2,1,0:T(8,128)(2,1)S(1)} %maximum_select_fusion.4), channel_id=1, source_target_pairs={{0,4},{4,0},{8,12},{12,8},{16,20},{20,16},{24,28},{28,24},{1,5},{5... | collective-permute-start | bytes 835592 | tf_op jit(solution)/shard_map/ppermute | solution.py:426
  176.4 8.8 %collective-permute-start.38 = (bf16[2,72,512]{2,1,0:T(8,128)(2,1)S(1)}, bf16[2,72,512]{2,1,0:T(8,128)(2,1)S(1)}, u32[]{:S(2)}, u32[]{:S(2)}) collective-permute-start(bf16[2,72,512]{2,1,0:T(8,128)(2,1)S(1)} %maximum_select_fusion.10), channel_id=1, source_target_pairs={{0,4},{4,0},{8,12},{12,8},{16,20},{20,16},{24,28},{28,24},{1,5},{5... | collective-permute-start | bytes 442376 | tf_op jit(solution)/shard_map/ppermute | solution.py:426
  178.0 7.2 %collective-permute-start.37 = (bf16[2,72,512]{2,1,0:T(8,128)(2,1)S(1)}, bf16[2,72,512]{2,1,0:T(8,128)(2,1)S(1)}, u32[]{:S(2)}, u32[]{:S(2)}) collective-permute-start(bf16[2,72,512]{2,1,0:T(8,128)(2,1)S(1)} %maximum_select_fusion.9), channel_id=1, source_target_pairs={{0,8},{4,12},{8,0},{12,4},{16,24},{20,28},{24,16},{28,20},{1,9},{5... | collective-permute-start | bytes 442376 | tf_op jit(solution)/shard_map/ppermute | solution.py:426
  (20 other events, 33.8 us)

commit v3 on v2

--- a/solution.py
+++ b/solution.py
@@ -101,7 +101,7 @@
     d = wqkv.shape[0]
     half = d // 2
     return call(pack_kernel, (y, z), (wqkv, wout, ub, up, down),
-                [struct((3 * d + 32, d), BF16), struct((d + half + 32, d), BF16)], name="pack_weights")
+                [struct((3 * d + 32, d), BF16), struct((d + half + 32, d), BF16)], name="pack_weights", vmem=56 << 20)
 
 
 def place_kernel(me_ref, b0, b1, b2, b3, out_ref):
@@ -110,9 +110,18 @@
         out_ref[pl.ds((me_ref[0] ^ k) * each, each)] = b[...]
 
 
+def far_specs(a):
+    return [pl.BlockSpec((a.shape[0] // 2, *a.shape[1:]), lambda *_, n=n: (n, 0, 0)) for n in range(2)]
+
+
+def far_seq_specs(a):
+    return [pl.BlockSpec((1, *a.shape[1:]), lambda s, *_, n=n: (n * (a.shape[0] // 2) + s, 0, 0)) for n in range(2)]
+
+
 def place(me, blocks):
     each, rows, d = blocks[0].shape
-    return call(place_kernel, (me,), blocks, [struct((4 * each, rows, d), BF16)], name="place")[0]
+    return call(place_kernel, (me,), blocks, [struct((4 * each, rows, d), BF16)],
+                in_specs=[full(blocks[0]), full(blocks[1])] + far_specs(blocks[2]), name="place")[0]
 
 
 def attn_fwd_kernel(me_ref, ff_ref, t0, t1, t2, t3, w0, w1, w2, w3,
@@ -192,13 +201,13 @@
     weights = [struct((d, 3 * d), BF16), struct((d, d), BF16), struct((4, 8, d), F32)]
     return call(
         attn_fwd_kernel, (me, ff), (*t, *w, *small), outs + weights, grid=(seqs,),
-        in_specs=[per_seq(a) for a in t] + [pl.BlockSpec((d + 32, d), lambda *_: (0, 0))] * 4 + [full(a) for a in small],
+        in_specs=[per_seq(a) for a in t[:2]] + far_seq_specs(t[2]) + [pl.BlockSpec((d + 32, d), lambda *_: (0, 0))] * 4 + [full(a) for a in small],
         out_specs=[per_seq(o) for o in outs] + [full(o) for o in weights],
         scratch=[pltpu.VMEM((4, rows, d), F32), pltpu.VMEM((length, length), F32), pltpu.VMEM((length, d), F32)],
         flops=2 * seqs * length * (4 * d * d + 2 * d * length), name="attention_forward", vmem=56 << 20)
 
 
-def ff_kernel(me_ref, y_ref, z_ref, live_ref, w0, w1, a2_, b2_, c2_, a3_, b3_, c3_, ub_ref, a2_ref, c0, c1, c2, c3,
+def ff_kernel(me_ref, y_ref, z_ref, count_ref, w0, w1, a2_, b2_, c2_, d2_, a3_, b3_, c3_, d3_, ub_ref, a2_ref, c0, c1, c2, c3,
               hm_ref, du_ref, gm_ref, send_ref, keep_ref, w_ref, wbuf, sems, out_sems, blk_sc, row_sc):
     c = pl.program_id(0)
     seqs, length, d = a2_ref.shape
@@ -213,9 +222,9 @@
     ] + [
         [pltpu.make_async_copy(a.at[pl.ds(2 * pitch, half)], quarter(k, y, z), sems.at[k, 0]),
          pltpu.make_async_copy(b, quarter(k, y, 1 - z), sems.at[k, 1]),
-         pltpu.make_async_copy(c.at[0:half], quarter(k, 1 - y, z), sems.at[k, 2]),
-         pltpu.make_async_copy(c.at[half:d], quarter(k, 1 - y, 1 - z), sems.at[k, 3])]
-        for k, (a, b, c) in ((2, (a2_, b2_, c2_)), (3, (a3_, b3_, c3_)))
+         pltpu.make_async_copy(c, quarter(k, 1 - y, z), sems.at[k, 2]),
+         pltpu.make_async_copy(e, quarter(k, 1 - y, 1 - z), sems.at[k, 3])]
+        for k, (a, b, c, e) in ((2, (a2_, b2_, c2_, d2_)), (3, (a3_, b3_, c3_, d3_)))
     ]
     out_copies = [pltpu.make_async_copy(wbuf.at[k], w_ref.at[k], out_sems.at[k]) for k in range(4)]
     order = (3, 1, 2, 0)
@@ -227,7 +236,7 @@
                 cp.start()
         rows = length // 4
         for s in range(seqs):
-            live = live_ref[s] > 0
+            live = me_ref[0] * seqs + s < count_ref[0]
             for k, cot in enumerate((c0, c1, c2, c3)):
                 blk_sc[me_ref[0] ^ k] = jnp.where(live, cot[s].astype(F32), 0.0)
             for i in range(4):
@@ -281,7 +290,7 @@
             cp.wait()
 
 
-def ff(me, y, z, live, w, ub, a2, cots):
+def ff(me, y, z, count, w, ub, a2, cots):
     seqs, length, d = a2.shape
     total = seqs * length
     anys = pl.BlockSpec(memory_space=pl.ANY)
@@ -289,8 +298,8 @@
     outs = [struct((total, 4 * d), BF16)] * 2 + [struct((seqs, length, d), BF16)] + [
         struct((2, 2 * d + 64, d), BF16)] * 2 + [struct((4, 2, d, d), BF16)]
     return call(
-        ff_kernel, (me, y, z, live), (*w, ub, a2, *cots), outs, grid=(4,),
-        in_specs=[anys] * 8 + [full(a) for a in (ub, a2, *cots)],
+        ff_kernel, (me, y, z, count), (*w, ub, a2, *cots), outs, grid=(4,),
+        in_specs=[anys] * 10 + [full(a) for a in (ub, a2, *cots[:2])] + far_specs(cots[2]),
         out_specs=[pl.BlockSpec((total, d), column)] * 2 + [
             full(outs[2]),
             pl.BlockSpec((1, 2 * d + 64, d), lambda c, *_: (1 - jnp.minimum(c, 1), 0, 0)),
@@ -298,13 +307,13 @@
             anys],
         scratch=[pltpu.VMEM((4, 2, d, d), BF16), pltpu.SemaphoreType.DMA((4, 4)), pltpu.SemaphoreType.DMA((4,)),
                  pltpu.VMEM((4, length // 4, d), F32), pltpu.VMEM((length, d), F32)],
-        flops=16 * total * d * d, name="feed_forward", vmem=44 << 20)
+        flops=16 * total * d * d, name="feed_forward", vmem=56 << 20)
 
 
 def attn_bwd_kernel(me_ref, du_ref, gm_ref, y1_ref, x_ref, g1_ref, g2_ref, w_ref, wq_ref, wo_ref, qkv_ref, p_ref,
-                    a1_ref, o_ref, after_ref, d0, d1, d2, d3, send_ref, keep_ref,
+                    a1_ref, o_ref, after_ref, d0, d1, d2, send_ref, keep_ref,
                     do_sc, full_sc, blk_sc, small_ref, dqkv_ref, dqkv_sc, ga_sc):
-    dxs = (d0, d1, d2, d3)
+    dxs = (d0, d1, d2)
     s = pl.program_id(0)
     _, length, d = gm_ref.shape
     here = pl.ds(pl.multiple_of(s * length, 16), length)
@@ -377,15 +386,16 @@
     seqs, length, d = gm.shape
     total = seqs * length
     anys = pl.BlockSpec(memory_space=pl.ANY)
-    outs = [struct((seqs, length // 4, d), BF16)] * 4 + [struct((2, 576, d), BF16)] * 2
+    outs, out_specs = spread_outs(seqs, length // 4, d)
+    grads = [struct((2, 576, d), BF16)] * 2
     args = [du, gm, y1, x, g1, g2, w, wq, wo, qkv, p, a1, o, after]
     in_specs = [pl.BlockSpec((length, 4 * d), lambda s, *_: (s, 0)), per_seq(gm), per_seq(y1), per_seq(x), full(g1), full(g2),
                 once((4, 1, d, d)), once(wq.shape), once(wo.shape), per_seq(qkv), per_seq(p), once(a1.shape), once(o.shape), anys]
     scratch = [pltpu.VMEM((length, d), BF16), pltpu.VMEM((length, d), F32), pltpu.VMEM((4, length // 4, d), F32),
                pltpu.VMEM((8, d), F32), pltpu.VMEM((1, length, 3 * d), BF16), pltpu.VMEM((total, 3 * d), BF16),
                pltpu.VMEM((total, d), BF16)]
-    return call(attn_bwd_kernel, (me,), args, outs, grid=(seqs,), in_specs=in_specs,
-                out_specs=[per_seq(a) for a in outs[:4]] + [once(a.shape) for a in outs[4:]], scratch=scratch,
+    return call(attn_bwd_kernel, (me,), args, outs + grads, grid=(seqs,), in_specs=in_specs,
+                out_specs=out_specs + [once(a.shape) for a in grads], scratch=scratch,
                 flops=6 * total * (4 * d * d + 2 * d * length), name="attention_backward", vmem=40 << 20)
 
 
@@ -393,30 +403,41 @@
     rows = blk_sc.shape[1]
     for i in range(4):
         blk_sc[i] = full_sc[pl.ds(i * rows, rows), :]
-    for k, out in enumerate(refs):
-        out[0] = blk_sc[me ^ k].astype(BF16)
-
-
-def finish_out_kernel(me_ref, live_ref, hm_ref, w_ref, y1_ref, db_ref, after_ref, o0, o1, o2, o3, full_sc, blk_sc):
+    own, near, far = refs
+    s = pl.program_id(0)
+    each = far.shape[0] // 2
+    own[0] = blk_sc[me].astype(BF16)
+    near[0] = blk_sc[me ^ 1].astype(BF16)
+    far[s] = blk_sc[me ^ 2].astype(BF16)
+    far[each + s] = blk_sc[me ^ 3].astype(BF16)
+
+
+def spread_outs(seqs, rows, d):
+    one = struct((seqs, rows, d), BF16)
+    far = struct((2 * seqs, rows, d), BF16)
+    return [one, one, far], [per_seq(one), per_seq(one), once(far.shape)]
+
+
+def finish_out_kernel(me_ref, count_ref, hm_ref, w_ref, y1_ref, db_ref, after_ref, o0, o1, o2, full_sc, blk_sc):
     s = pl.program_id(0)
     d = y1_ref.shape[2]
     mlp = None
     for k in range(4):
         part = dot(hm_ref[:, pl.ds(k * d, d)], w_ref[k, 0])
         mlp = part if mlp is None else mlp + part
-    full_sc[...] = jnp.where(live_ref[s] > 0, y1_ref[0] + mlp + db_ref[...], 0.0)
-    spread((o0, o1, o2, o3), me_ref[0], full_sc, blk_sc)
-
-
-def finish_out(me, live, after, hm, w, y1, db):
+    full_sc[...] = jnp.where(me_ref[0] * pl.num_programs(0) + s < count_ref[0], y1_ref[0] + mlp + db_ref[...], 0.0)
+    spread((o0, o1, o2), me_ref[0], full_sc, blk_sc)
+
+
+def finish_out(me, count, after, hm, w, y1, db):
     seqs, length, d = y1.shape
-    outs = [struct((seqs, length // 4, d), BF16)] * 4
+    outs, out_specs = spread_outs(seqs, length // 4, d)
     return call(
-        finish_out_kernel, (me, live), (hm, w, y1, db, after), outs, grid=(seqs,),
+        finish_out_kernel, (me, count), (hm, w, y1, db, after), outs, grid=(seqs,),
         in_specs=[pl.BlockSpec((length, 4 * d), lambda s, *_: (s, 0)),
                   pl.BlockSpec((4, 1, d, d), lambda s, *_: (0, 1, 0, 0)), per_seq(y1), full(db),
                   pl.BlockSpec(memory_space=pl.ANY)],
-        out_specs=[per_seq(outs[0])] * 4,
+        out_specs=out_specs,
         scratch=[pltpu.VMEM((length, d), F32), pltpu.VMEM((4, length // 4, d), F32)],
         flops=2 * seqs * length * 4 * d * d, name="block_output", vmem=56 << 20)
 
@@ -429,11 +450,17 @@
 def split(rows, me):
     rows = rows.transpose(1, 0, 2)
     each = rows.shape[0] // 4
-    return [lax.dynamic_slice_in_dim(rows, (me ^ k) * each, each) for k in range(4)]
-
-
-def scatter(blocks):
-    return [blocks[0]] + [hop(blocks[k], "tensor", k) for k in (1, 2, 3)]
+    own, near, *far = (lax.dynamic_slice_in_dim(rows, (me ^ k) * each, each) for k in range(4))
+    return [own, near, jnp.concatenate(far)]
+
+
+def exchange(own, near, far):
+    far = hop(far, "tensor", 2)
+    return [own, hop(near, "tensor", 1), far, far]
+
+
+def forward(blocks, *after):
+    return [*blocks[:3], hop(tie(blocks[3], *after), "tensor", 1)]
 
 
 def halves(a, side, axis=0):
@@ -544,7 +571,6 @@
     me = mine.reshape(1)
     y = lax.axis_index("dp").astype(jnp.int32) % 2
     bit = y.reshape(1)
-    live = ((mine * seqs + jnp.arange(seqs, dtype=jnp.int32)) < seq_counts[0]).astype(jnp.int32)
     row = lambda a: a.reshape(1, -1)
     g1, b1, bo, g2, b2, db = map(row, (norm1_gain, norm1_bias, out_bias, norm2_gain, norm2_bias, down_bias))
 
@@ -554,26 +580,32 @@
     far_a = hop(far, "tensor", 2)
     near = hop(own, "tensor", 1)
     t = split(tie(tokens, near), mine)
-    t = [t[0]] + [hop(t[k], "tensor", k) for k in (1, 2, 3)]
+    t_far, t_near = hop(t[2], "tensor", 2), hop(t[1], "tensor", 1)
+    cot = split(tie(out_cotangent, t[2]), mine)
+    cot_near = hop(cot[1], "tensor", 1)
+    far_a = tie(far_a, t_far, t_near, cot[2], cot_near)
+    t = [t[0], t_near, t_far, hop(tie(t_far, far_a), "tensor", 1)]
+    diag_a = hop(far_a, "tensor", 1)
     far_2 = far_a[d + 32:]
-    far_b = hop(far_2, "dp", 2)
-    diag_a, diag_b = hop(tie(far_a, t[1]), "tensor", 1), hop(far_b, "tensor", 1)
-    far_c = hop(tie(jnp.concatenate([far_2, far_b]), diag_a, t[1], t[2], t[3]), "dp", 1)
+    far_2 = [far_2, hop(far_2, "dp", 2), hop(far_2, "dp", 1), hop(far_2, "dp", 3)]
     w1 = (own, near, far_a, diag_a)
-    cot = scatter(split(tie(out_cotangent, t[1], t[2]), mine))
+    cot_far = hop(tie(cot[2], t_far), "tensor", 2)
 
     qkv, p, o, x, y1, a1, a2, wq, wo, ub = attn_fwd(me, first_frame, t, w1, g1, b1, bo, g2, b2)
-    w2 = (own, near, far_a, far_b, far_c, diag_a, diag_b, hop(tie(far_c, a2, *cot), "tensor", 1))
-    hm, du, gm, send, keep, w2 = ff(me, bit, zbit, live, w2, ub, a2, cot)
+    near_2 = tie(far_2[1:], a2)
+    cot = forward([cot[0], cot_near, cot_far, cot_far], a2)
+    w2 = (own, near, far_a, *far_2[1:], diag_a, *(hop(b, "tensor", 1) for b in near_2))
+    hm, du, gm, send, keep, w2 = ff(me, bit, zbit, seq_counts, w2, ub, a2, cot)
 
     m, a = Sum(1, 2), Sum(2, 1)
     got = hop(send, "tensor", 1)
-    out = finish_out(me, live, a2, hm, w2, y1, db)
+    out = finish_out(me, seq_counts, a2, hm, w2, y1, db)
     ((got,),) = wait(out, [got])
     sent = m.step1(plus(keep, got))
-    out = scatter(tie(out, *sent))
+    out = exchange(*tie(out, *sent))
     *dx, send, keep = attn_bwd(me, tie(*sent), du, gm, y1, x, g1, g2, w2, wq, wo, qkv, p, a1, o)
-    m.got, out = wait([send], m.got, out)
+    m.got, out = wait([send], m.got, out[:3])
+    out = forward([*out, out[2]])
     sent = m.step2()
     got = hop(tie(send, *sent), "tensor", 1)
     ((got,),) = wait(sent, [got])
@@ -583,25 +615,25 @@
     sent = m.step3()
     (a.got,) = wait(sent, a.got)
     sent = a.step2()
-    dx = scatter(tie(dx, *sent))
+    dx = exchange(*tie(dx, *sent))
     (m.got,) = wait(sent, m.got)
     sent = m.step4()
     (a.got,) = wait(sent, a.got)
     sent = a.step3()
-    a.got, dx = wait(sent, a.got, dx)
+    (m.got,) = wait(sent, m.got)
+    sent = m.step5()
+    a.got, dx = wait(sent, a.got, dx[:3])
     sent = a.step4()
-    input_grad = place(me, tie(dx, *sent)).transpose(1, 0, 2)
-    (m.got,) = wait([input_grad], m.got)
-    sent = m.step5()
-    (a.got,) = wait(sent, a.got)
-    sent = a.step5()
+    dx = forward([*dx, dx[2]], *sent)
     (m.got,) = wait(sent, m.got)
     sent = m.step6()
-    (a.got,) = wait(sent, a.got)
-    sent = a.step6()
+    input_grad = place(me, tie(dx, *sent)).transpose(1, 0, 2)
+    (a.got,) = wait([input_grad], a.got)
+    sent = a.step5()
     (m.got,) = wait(sent, m.got)
     mlp_grad = m.result()
     (a.got,) = wait([mlp_grad], a.got)
+    a.step6()
     attn_grads = a.result()
 
     mlp_grad = mlp_grad.astype(F32)

time: 192 us -> 185 us (0.964)
  waiting for transfers between devices: 64.1 us -> 53.8 us
  local copies, waits for them, and re-layouts: 17.8 us -> 10.7 us
  starting transfers between devices: 35.7 us -> 42.5 us
  Pallas kernels: 65.8 us -> 69.8 us
    ppermute x41 -> x43, waiting for transfers between devices: 64.1 us -> 53.8 us  [hop(): return lax.ppermute(value, axis, [(i, i ^ bit) for i in range(n)])]
    unnamed x87 -> x77, local copies, waits for them, and re-layouts: 10.2 us -> 3.41 us
    ppermute x41 -> x43, starting transfers between devices: 35.7 us -> 42.5 us  [hop(): return lax.ppermute(value, axis, [(i, i ^ bit) for i in range(n)])]
    pallas_call x7, Pallas kernels: 65.8 us -> 69.8 us  [call(): pl.pallas_call(kernel, grid_spec=pltpu.PrefetchScalarGridSpec(num_scalar_...]
  transfers between devices with their start and end apart: 41 -> 43, of which waited for: 19 -> 19; matrix products, arithmetic and copies ran while one was open for 4% -> 4% of each run, Pallas kernels for 26% -> 27%
where the time goes in v3:
time: 185 us; the launch traced here: 184 us
  Pallas kernels  69.8 us (38%)
  waiting for transfers between devices  53.8 us (29%)
  starting transfers between devices  42.5 us (23%)
  local copies, waits for them, and re-layouts  10.7 us (6%)
  other arithmetic  5.27 us (3%)
  between operations  2.16 us (1%)
    pallas_call x7, Pallas kernels, call(): pl.pallas_call(kernel, grid_spec=pltpu.PrefetchScalarGridSpec(num_scalar_...  69.8 us
    ppermute x43, waiting for transfers between devices, hop(): return lax.ppermute(value, axis, [(i, i ^ bit) for i in range(n)])  53.8 us
    ppermute x43, starting transfers between devices, hop(): return lax.ppermute(value, axis, [(i, i ^ bit) for i in range(n)])  42.5 us
  transfers between devices with their start and end apart: 43, of which 19 were waited for; matrix products, arithmetic and copies ran while one was open for 4% of the time, Pallas kernels for 27%

profile of v3, /device:TPU:0, one launch (start us, length us, event | category | flops | bytes accessed | tf_op | source)
XLA Modules:
  0.0 184.3 jit_solution(7363424331593113390)
XLA Ops:
  0.7 3.1 %pack_weights.1 = (bf16[1568,512]{1,0:T(8,128)(2,1)}, bf16[800,512]{1,0:T(8,128)(2,1)}) custom-call(s32[1]{0:T(128)} %bitcast.1.y_ref, s32[1]{0:T(128)} %bitcast.2.z_ref, bf16[512,384]{1,0:T(8,128)(2,1)} %wqkv_ref.1, bf16[128,512]{1,0:T(8,128)(2,1)} %wout_ref.1, f32[1,512]{1,0:T(1,128)} %bitcast.122, bf16[512,512]{1,0:T(8,128)(2,1)} %up_ref.1, ...), custom_call_target="tpu_custom_call" | custom-call | bytes 3999744 | tf_op jit(solution)/shard_map/pack_weights/pallas_call | solution.py:56
  4.2 2.5 %collective-permute-start.1 = (bf16[800,512]{1,0:T(8,128)(2,1)}, bf16[800,512]{1,0:T(8,128)(2,1)S(1)}, u32[]{:S(2)}, u32[]{:S(2)}) collective-permute-start(bf16[800,512]{1,0:T(8,128)(2,1)} %get-tuple-element.92), channel_id=1, source_target_pairs={{0,2},{1,3},{2,0},{3,1},{4,6},{5,7},{6,4},{7,5},{8,10},{9,11},{10,... | collective-permute-start | bytes 2457608 | tf_op jit(solution)/shard_map/ppermute | solution.py:447
  6.7 0.8 collective-permute-done.w1
  7.5 0.9 dynamic-slice_bitcast_fusion.1
  8.8 2.9 %collective-permute-start.2 = (bf16[6,84,512]{2,1,0:T(8,128)(2,1)S(1)}, bf16[6,84,512]{2,1,0:T(8,128)(2,1)S(1)}, u32[]{:S(2)}, u32[]{:S(2)}) collective-permute-start(bf16[6,84,512]{2,1,0:T(8,128)(2,1)S(1)} %pad_maximum_fusion.2), channel_id=1, source_target_pairs={{0,2},{1,3},{2,0},{3,1},{4,6},{5,7},{6,4},{7,5},{8,10},{9,11},{10,... | collective-permute-start | bytes 1548296 | tf_op jit(solution)/shard_map/ppermute | solution.py:447
  11.7 0.8 dynamic-slice_bitcast_fusion
  12.4 0.5 collective-permute-start.3
  13.0 13.0 %collective-permute-done.1.w2.a2_ = bf16[800,512]{1,0:T(8,128)(2,1)S(1)} collective-permute-done((bf16[800,512]{1,0:T(8,128)(2,1)}, bf16[800,512]{1,0:T(8,128)(2,1)S(1)}, u32[]{:S(2)}, u32[]{:S(2)}) %collective-permute-start.1) | collective-permute-done | bytes 819232 | tf_op jit(solution)/shard_map/ppermute | solution.py:447
  26.1 11.4 %collective-permute-done.2.t2 = bf16[6,84,512]{2,1,0:T(8,128)(2,1)S(1)} collective-permute-done((bf16[6,84,512]{2,1,0:T(8,128)(2,1)S(1)}, bf16[6,84,512]{2,1,0:T(8,128)(2,1)S(1)}, u32[]{:S(2)}, u32[]{:S(2)}) %collective-permute-start.2) | collective-permute-done | bytes 516128 | tf_op jit(solution)/shard_map/ppermute | solution.py:447
  37.4 0.5 collective-permute-start.9
  38.0 1.7 collective-permute-start.13
  39.7 1.6 collective-permute-start.5
  41.4 1.5 collective-permute-start.6
  43.7 0.5 copy-done.23
  44.2 16.2 %attention_forward.1 = (bf16[3,336,1536]{2,1,0:T(8,128)(2,1)}, bf16[3,8,336,336]{3,2,1,0:T(8,128)(2,1)}, bf16[3,336,512]{2,1,0:T(8,128)(2,1)}, bf16[3,336,512]{2...) custom-call(s32[1]{0:T(128)} %bitcast.me_ref, ...), custom_call_target="tpu_custom_call" | custom-call | flops 2807562240 | bytes 23279616 | tf_op jit(solution)/shard_map/attention_forward/pallas_call | solution.py:56
  60.6 0.5 collective-permute-start.10
  62.3 0.5 collective-permute-done.10.b3_
  64.5 17.4 %feed_forward.1 = (bf16[1008,2048]{1,0:T(8,128)(2,1)}, bf16[1008,2048]{1,0:T(8,128)(2,1)}, bf16[3,336,512]{2,1,0:T(8,128)(2,1)}, bf16[2,1088,512]{2,1,0:T(8,128)...) custom-call(s32[1]{0:T(128)} %bitcast.me_ref, s32[1]{0:T(128)} %bitcast.1.y_ref, s32[1]{0:T(128)} %bitcast.2.z_ref, ...), custom_call_target="tpu_custom_call" | custom-call | flops 4227858432 | bytes 27009024 | tf_op jit(solution)/shard_map/feed_forward/pallas_call | solution.py:56
  82.1 6.6 %block_output.1 = (bf16[3,84,512]{2,1,0:T(8,128)(2,1)}, bf16[3,84,512]{2,1,0:T(8,128)(2,1)}, bf16[6,84,512]{2,1,0:T(8,128)(2,1)}) custom-call(s32[1]{0:T(128)} %bitcast.me_ref, s32[1]{0:T(128)S(6)} %copy.32.count_ref, bf16[1008,2048]{1,0:T(8,128)(2,1)} %get-tuple-element.106.hm_ref, bf16[4,2,512,512]{3,2,1,0:T(8,128)(2,1)} %get-tuple-element.107.w_ref, ...), custom_call_target="tpu_custom_call" | custom-call | flops 2113929216 | bytes 12453888 | tf_op jit(solution)/shard_map/block_output/pallas_call | solution.py:56
  88.8 0.6 add_convert_fusion
  89.7 1.5 collective-permute-start.17
  91.2 0.5 collective-permute-start.16
  91.8 1.5 collective-permute-start.19
  93.4 24.4 %attention_backward.1 = (bf16[3,84,512]{2,1,0:T(8,128)(2,1)S(1)}, bf16[3,84,512]{2,1,0:T(8,128)(2,1)S(1)}, bf16[6,84,512]{2,1,0:T(8,128)(2,1)S(1)}, bf16[2,576,5...) custom-call(s32[1]{0:T(128)} %bitcast.me_ref, bf16[1008,2048]{1,0:T(8,128)(2,1)} %get-tuple-element.116.du_ref, ...), custom_call_target="tpu_custom_call" | custom-call | flops 8422686720 | bytes 29081600 | tf_op jit(solution)/shard_map/attention_backward/pallas_call | solution.py:56
  118.0 0.9 slice_bitcast_fusion.5
  119.1 0.8 constant_dynamic-slice_fusion.2
  120.0 0.5 collective-permute-start.21
  120.4 0.6 collective-permute-start.25
  121.1 1.4 collective-permute-start.24
  122.5 0.5 collective-permute-done.21
  123.1 1.6 add_convert_fusion.1
  124.7 1.7 collective-permute-start.23
  126.4 0.6 collective-permute-start.22
  127.1 1.1 place.2
  128.1 1.1 collective-permute-done.25
  130.2 2.1 %collective-permute-start.28 = (bf16[272,512]{1,0:T(8,128)(2,1)S(1)}, bf16[272,512]{1,0:T(8,128)(2,1)S(1)}, u32[]{:S(2)}, u32[]{:S(2)}) collective-permute-start(bf16[272,512]{1,0:T(8,128)(2,1)S(1)} %fusion.5), channel_id=1, source_target_pairs={{0,8},{4,12},{8,0},{12,4},{16,24},{20,28},{24,16},{28,20},{1,9},{5... | collective-permute-start | bytes 835592 | tf_op jit(solution)/shard_map/ppermute | solution.py:447
  132.4 2.3 %collective-permute-done.23 = bf16[2,144,512]{2,1,0:T(8,128)(2,1)S(1)} collective-permute-done((bf16[2,144,512]{2,1,0:T(8,128)(2,1)S(1)}, bf16[2,144,512]{2,1,0:T(8,128)(2,1)S(1)}, u32[]{:S(2)}, u32[]{:S(2)}) %collective-permute-start.23) | collective-permute-done | bytes 294944 | tf_op jit(solution)/shard_map/ppermute | solution.py:447
  134.6 0.9 collective-permute-done.22
  135.7 0.8 collective-permute-start.27
  136.6 1.5 collective-permute-start.26
  138.1 2.6 %collective-permute-done.28 = bf16[272,512]{1,0:T(8,128)(2,1)S(1)} collective-permute-done((bf16[272,512]{1,0:T(8,128)(2,1)S(1)}, bf16[272,512]{1,0:T(8,128)(2,1)S(1)}, u32[]{:S(2)}, u32[]{:S(2)}) %collective-permute-start.28) | collective-permute-done | bytes 278560 | tf_op jit(solution)/shard_map/ppermute | solution.py:447
  141.0 2.7 %collective-permute-start.32 = (bf16[272,512]{1,0:T(8,128)(2,1)S(1)}, bf16[272,512]{1,0:T(8,128)(2,1)S(1)}, u32[]{:S(2)}, u32[]{:S(2)}) collective-permute-start(bf16[272,512]{1,0:T(8,128)(2,1)S(1)} %add_convert_fusion.5), channel_id=1, source_target_pairs={{0,16},{4,20},{8,24},{12,28},{16,0},{20,4},{24,8},{28,12},{1,17},{... | collective-permute-start | bytes 835592 | tf_op jit(solution)/shard_map/ppermute | solution.py:447
  143.7 0.6 collective-permute-start.31
  144.6 1.5 collective-permute-start.29
  146.1 9.4 %collective-permute-done.32 = bf16[272,512]{1,0:T(8,128)(2,1)S(1)} collective-permute-done((bf16[272,512]{1,0:T(8,128)(2,1)S(1)}, bf16[272,512]{1,0:T(8,128)(2,1)S(1)}, u32[]{:S(2)}, u32[]{:S(2)}) %collective-permute-start.32) | collective-permute-done | bytes 278560 | tf_op jit(solution)/shard_map/ppermute | solution.py:447
  155.6 0.7 collective-permute-start.34
  156.4 0.6 collective-permute-start.35
  157.3 3.4 %collective-permute-start.36 = (bf16[144,512]{1,0:T(8,128)(2,1)S(1)}, bf16[144,512]{1,0:T(8,128)(2,1)S(1)}, u32[]{:S(2)}, u32[]{:S(2)}) collective-permute-start(bf16[144,512]{1,0:T(8,128)(2,1)S(1)} %add_convert_fusion.8), channel_id=1, source_target_pairs={{0,16},{4,20},{8,24},{12,28},{16,0},{20,4},{24,8},{28,12},{1,17},{... | collective-permute-start | bytes 442376 | tf_op jit(solution)/shard_map/ppermute | solution.py:447
  160.8 0.9 collective-permute-done.35
  161.7 1.2 collective-permute-start.40
  162.9 0.7 collective-permute-start.39
  163.7 1.1 place.3
  164.7 3.7 %collective-permute-done.36 = bf16[144,512]{1,0:T(8,128)(2,1)S(1)} collective-permute-done((bf16[144,512]{1,0:T(8,128)(2,1)S(1)}, bf16[144,512]{1,0:T(8,128)(2,1)S(1)}, u32[]{:S(2)}, u32[]{:S(2)}) %collective-permute-start.36) | collective-permute-done | bytes 147488 | tf_op jit(solution)/shard_map/ppermute | solution.py:447
  168.5 1.5 collective-permute-start.37
  170.0 1.7 collective-permute-done.40
  172.3 1.5 fusion.8
  173.8 0.6 slice.122
  174.4 1.8 collective-permute-start.41
  176.2 1.5 collective-permute-start.42
  177.7 1.9 %collective-permute-done.41 = bf16[2,72,512]{2,1,0:T(8,128)(2,1)S(1)} collective-permute-done((bf16[2,72,512]{2,1,0:T(8,128)(2,1)S(1)}, bf16[2,72,512]{2,1,0:T(8,128)(2,1)S(1)}, u32[]{:S(2)}, u32[]{:S(2)}) %collective-permute-start.41) | collective-permute-done | bytes 147488 | tf_op jit(solution)/shard_map/ppermute | solution.py:447
  179.6 1.8 collective-permute-done.42
  181.7 0.7 slice.119
  182.4 0.6 fusion.9
  183.1 1.2 copy.31
  (160 shorter events, 8.3 us)
Async XLA Ops:
  0.6 6.9 %copy-start.19 = (bf16[84,12,512]{2,0,1:T(8,128)(2,1)S(1)}, bf16[84,12,512]{2,0,1:T(8,128)(2,1)}, u32[]{:S(2)}) copy-start(bf16[84,12,512]{2,0,1:T(8,128)(2,1)} %param.15) | copy-start | bytes 3096580
  3.8 3.7 %collective-permute-start = (bf16[1568,512]{1,0:T(8,128)(2,1)}, bf16[1568,512]{1,0:T(8,128)(2,1)S(1)}, u32[]{:S(2)}, u32[]{:S(2)}) collective-permute-start(bf16[1568,512]{1,0:T(8,128)(2,1)} %get-tuple-element.91.w0), channel_id=1, source_target_pairs={{0,1},{1,0},{2,3},{3,2},{4,5},{5,4},{6,7},{7,6},{8,9},{9,8},{10,11... | collective-permute-start | bytes 4816904 | tf_op jit(solution)/shard_map/ppermute | solution.py:447
  4.2 21.8 %collective-permute-start.1 = (bf16[800,512]{1,0:T(8,128)(2,1)}, bf16[800,512]{1,0:T(8,128)(2,1)S(1)}, u32[]{:S(2)}, u32[]{:S(2)}) collective-permute-start(bf16[800,512]{1,0:T(8,128)(2,1)} %get-tuple-element.92), channel_id=1, source_target_pairs={{0,2},{1,3},{2,0},{3,1},{4,6},{5,7},{6,4},{7,5},{8,10},{9,11},{10,... | collective-permute-start | bytes 2457608 | tf_op jit(solution)/shard_map/ppermute | solution.py:447
  6.7 4.9 %copy-start.20 = (bf16[84,12,512]{2,0,1:T(8,128)(2,1)S(1)}, bf16[84,12,512]{2,0,1:T(8,128)(2,1)}, u32[]{:S(2)}) copy-start(bf16[84,12,512]{2,0,1:T(8,128)(2,1)} %param.29) | copy-start | bytes 3096580
  8.8 28.7 %collective-permute-start.2 = (bf16[6,84,512]{2,1,0:T(8,128)(2,1)S(1)}, bf16[6,84,512]{2,1,0:T(8,128)(2,1)S(1)}, u32[]{:S(2)}, u32[]{:S(2)}) collective-permute-start(bf16[6,84,512]{2,1,0:T(8,128)(2,1)S(1)} %pad_maximum_fusion.2), channel_id=1, source_target_pairs={{0,2},{1,3},{2,0},{3,1},{4,6},{5,7},{6,4},{7,5},{8,10},{9,11},{10,... | collective-permute-start | bytes 1548296 | tf_op jit(solution)/shard_map/ppermute | solution.py:447
  12.4 13.6 %collective-permute-start.4 = (bf16[3,84,512]{2,1,0:T(8,128)(2,1)S(1)}, bf16[3,84,512]{2,1,0:T(8,128)(2,1)S(1)}, u32[]{:S(2)}, u32[]{:S(2)}) collective-permute-start(bf16[3,84,512]{2,1,0:T(8,128)(2,1)S(1)} %get-tuple-element.204), channel_id=1, source_target_pairs={{0,1},{1,0},{2,3},{3,2},{4,5},{5,4},{6,7},{7,6},{8,9},{9,8},{10,11... | collective-permute-start | bytes 774152 | tf_op jit(solution)/shard_map/ppermute | solution.py:447
  12.4 13.6 %collective-permute-start.3 = (bf16[3,84,512]{2,1,0:T(8,128)(2,1)S(1)}, bf16[3,84,512]{2,1,0:T(8,128)(2,1)S(1)}, u32[]{:S(2)}, u32[]{:S(2)}) collective-permute-start(bf16[3,84,512]{2,1,0:T(8,128)(2,1)S(1)} %get-tuple-element.208), channel_id=1, source_target_pairs={{0,1},{1,0},{2,3},{3,2},{4,5},{5,4},{6,7},{7,6},{8,9},{9,8},{10,11... | collective-permute-start | bytes 774152 | tf_op jit(solution)/shard_map/ppermute | solution.py:447
  26.0 17.3 %copy-start.21 = (bf16[800,512]{1,0:T(8,128)(2,1)}, bf16[800,512]{1,0:T(8,128)(2,1)S(1)}, u32[]{:S(2)}) copy-start(bf16[800,512]{1,0:T(8,128)(2,1)S(1)} %collective-permute-done.1.w2.a2_) | copy-start | bytes 2457604
  26.0 34.3 %copy-start.29 = (bf16[3,84,512]{2,1,0:T(8,128)(2,1)}, bf16[3,84,512]{2,1,0:T(8,128)(2,1)S(1)}, u32[]{:S(2)}) copy-start(bf16[3,84,512]{2,1,0:T(8,128)(2,1)S(1)} %collective-permute-done.4.c1) | copy-start | bytes 774148
  26.0 17.3 %copy-start.30 = (bf16[3,84,512]{2,1,0:T(8,128)(2,1)}, bf16[3,84,512]{2,1,0:T(8,128)(2,1)S(1)}, u32[]{:S(2)}) copy-start(bf16[3,84,512]{2,1,0:T(8,128)(2,1)S(1)} %collective-permute-done.3.t1) | copy-start | bytes 774148
  37.4 5.9 %copy-start.25 = (bf16[6,84,512]{2,1,0:T(8,128)(2,1)}, bf16[6,84,512]{2,1,0:T(8,128)(2,1)S(1)}, u32[]{:S(2)}) copy-start(bf16[6,84,512]{2,1,0:T(8,128)(2,1)S(1)} %collective-permute-done.2.t2) | copy-start | bytes 1548292
  37.4 5.9 %collective-permute-start.8 = (bf16[800,512]{1,0:T(8,128)(2,1)S(1)}, bf16[800,512]{1,0:T(8,128)(2,1)S(1)}, u32[]{:S(2)}, u32[]{:S(2)}) collective-permute-start(bf16[800,512]{1,0:T(8,128)(2,1)S(1)} %collective-permute-done.1.w2.a2_), channel_id=1, source_target_pairs={{0,1},{1,0},{2,3},{3,2},{4,5},{5,4},{6,7},{7,6},{8,9},{9,8},{10,11... | collective-permute-start | bytes 2457608 | tf_op jit(solution)/shard_map/ppermute | solution.py:447
  37.4 5.4 %collective-permute-start.9 = (bf16[6,84,512]{2,1,0:T(8,128)(2,1)S(1)}, bf16[6,84,512]{2,1,0:T(8,128)(2,1)S(1)}, u32[]{:S(2)}, u32[]{:S(2)}) collective-permute-start(bf16[6,84,512]{2,1,0:T(8,128)(2,1)S(1)} %collective-permute-done.2.t2), channel_id=1, source_target_pairs={{0,1},{1,0},{2,3},{3,2},{4,5},{5,4},{6,7},{7,6},{8,9},{9,8},{10,11... | collective-permute-start | bytes 1548296 | tf_op jit(solution)/shard_map/ppermute | solution.py:447
  38.0 22.4 %collective-permute-start.13 = (bf16[6,84,512]{2,1,0:T(8,128)(2,1)S(1)}, bf16[6,84,512]{2,1,0:T(8,128)(2,1)S(1)}, u32[]{:S(2)}, u32[]{:S(2)}) collective-permute-start(bf16[6,84,512]{2,1,0:T(8,128)(2,1)S(1)} %pad_maximum_fusion.3), channel_id=1, source_target_pairs={{0,2},{1,3},{2,0},{3,1},{4,6},{5,7},{6,4},{7,5},{8,10},{9,11},{10,... | collective-permute-start | bytes 1548296 | tf_op jit(solution)/shard_map/ppermute | solution.py:447
  39.7 20.8 %collective-permute-start.5 = (bf16[256,512]{1,0:T(8,128)(2,1)S(1)}, bf16[256,512]{1,0:T(8,128)(2,1)S(1)}, u32[]{:S(2)}, u32[]{:S(2)}) collective-permute-start(bf16[256,512]{1,0:T(8,128)(2,1)S(1)} %slice.78), channel_id=1, source_target_pairs={{0,8},{4,12},{8,0},{12,4},{16,24},{20,28},{24,16},{28,20},{1,9},{5... | collective-permute-start | bytes 786440 | tf_op jit(solution)/shard_map/ppermute | solution.py:447
  41.4 19.2 %collective-permute-start.6 = (bf16[256,512]{1,0:T(8,128)(2,1)S(1)}, bf16[256,512]{1,0:T(8,128)(2,1)S(1)}, u32[]{:S(2)}, u32[]{:S(2)}) collective-permute-start(bf16[256,512]{1,0:T(8,128)(2,1)S(1)} %slice.78), channel_id=1, source_target_pairs={{0,4},{4,0},{8,12},{12,8},{16,20},{20,16},{24,28},{28,24},{1,5},{5... | collective-permute-start | bytes 786440 | tf_op jit(solution)/shard_map/ppermute | solution.py:447
  42.9 17.7 %collective-permute-start.7 = (bf16[256,512]{1,0:T(8,128)(2,1)S(1)}, bf16[256,512]{1,0:T(8,128)(2,1)S(1)}, u32[]{:S(2)}, u32[]{:S(2)}) collective-permute-start(bf16[256,512]{1,0:T(8,128)(2,1)S(1)} %slice.78), channel_id=1, source_target_pairs={{0,12},{4,8},{8,4},{12,0},{16,28},{20,24},{24,20},{28,16},{1,13},{... | collective-permute-start | bytes 786440 | tf_op jit(solution)/shard_map/ppermute | solution.py:447
  60.4 3.1 %collective-permute-start.14 = (bf16[6,84,512]{2,1,0:T(8,128)(2,1)S(1)}, bf16[6,84,512]{2,1,0:T(8,128)(2,1)S(1)}, u32[]{:S(2)}, u32[]{:S(2)}) collective-permute-start(bf16[6,84,512]{2,1,0:T(8,128)(2,1)S(1)} %collective-permute-done.13.c2), channel_id=1, source_target_pairs={{0,1},{1,0},{2,3},{3,2},{4,5},{5,4},{6,7},{7,6},{8,9},{9,8},{10,11... | collective-permute-start | bytes 1548296 | tf_op jit(solution)/shard_map/ppermute | solution.py:447
  60.6 2.2 %collective-permute-start.10 = (bf16[256,512]{1,0:T(8,128)(2,1)S(1)}, bf16[256,512]{1,0:T(8,128)(2,1)S(1)}, u32[]{:S(2)}, u32[]{:S(2)}) collective-permute-start(bf16[256,512]{1,0:T(8,128)(2,1)S(1)} %collective-permute-done.5.b2_), channel_id=1, source_target_pairs={{0,1},{1,0},{2,3},{3,2},{4,5},{5,4},{6,7},{7,6},{8,9},{9,8},{10,11... | collective-permute-start | bytes 786440 | tf_op jit(solution)/shard_map/ppermute | solution.py:447
  61.1 2.1 %collective-permute-start.11 = (bf16[256,512]{1,0:T(8,128)(2,1)S(1)}, bf16[256,512]{1,0:T(8,128)(2,1)S(1)}, u32[]{:S(2)}, u32[]{:S(2)}) collective-permute-start(bf16[256,512]{1,0:T(8,128)(2,1)S(1)} %collective-permute-done.6.c2_), channel_id=1, source_target_pairs={{0,1},{1,0},{2,3},{3,2},{4,5},{5,4},{6,7},{7,6},{8,9},{9,8},{10,11... | collective-permute-start | bytes 786440 | tf_op jit(solution)/shard_map/ppermute | solution.py:447
  61.2 2.4 %collective-permute-start.12 = (bf16[256,512]{1,0:T(8,128)(2,1)S(1)}, bf16[256,512]{1,0:T(8,128)(2,1)S(1)}, u32[]{:S(2)}, u32[]{:S(2)}) collective-permute-start(bf16[256,512]{1,0:T(8,128)(2,1)S(1)} %collective-permute-done.7.d2_), channel_id=1, source_target_pairs={{0,1},{1,0},{2,3},{3,2},{4,5},{5,4},{6,7},{7,6},{8,9},{9,8},{10,11... | collective-permute-start | bytes 786440 | tf_op jit(solution)/shard_map/ppermute | solution.py:447
  81.9 6.8 %collective-permute-start.15 = (bf16[2,1088,512]{2,1,0:T(8,128)(2,1)}, bf16[2,1088,512]{2,1,0:T(8,128)(2,1)S(1)}, u32[]{:S(2)}, u32[]{:S(2)}) collective-permute-start(bf16[2,1088,512]{2,1,0:T(8,128)(2,1)} %get-tuple-element.105), channel_id=1, source_target_pairs={{0,1},{1,0},{2,3},{3,2},{4,5},{5,4},{6,7},{7,6},{8,9},{9,8},{10,11... | collective-permute-start | bytes 6684680 | tf_op jit(solution)/shard_map/ppermute | solution.py:447
  82.1 6.7 %copy-start.16 = (bf16[2,1088,512]{2,1,0:T(8,128)(2,1)S(1)}, bf16[2,1088,512]{2,1,0:T(8,128)(2,1)}, u32[]{:S(2)}) copy-start(bf16[2,1088,512]{2,1,0:T(8,128)(2,1)} %get-tuple-element.104) | copy-start | bytes 6684676
  88.8 4.5 %copy-start.9 = (bf16[3,336,512]{2,1,0:T(8,128)(2,1)S(1)}, bf16[3,336,512]{2,1,0:T(8,128)(2,1)}, u32[]{:S(2)}) copy-start(bf16[3,336,512]{2,1,0:T(8,128)(2,1)} %get-tuple-element.124.o_ref) | copy-start | bytes 3096580
  88.8 4.5 %copy-start.10 = (bf16[3,336,512]{2,1,0:T(8,128)(2,1)S(1)}, bf16[3,336,512]{2,1,0:T(8,128)(2,1)}, u32[]{:S(2)}) copy-start(bf16[3,336,512]{2,1,0:T(8,128)(2,1)} %get-tuple-element.118.x_ref) | copy-start | bytes 3096580
  88.8 4.5 %copy-start.11 = (bf16[3,336,512]{2,1,0:T(8,128)(2,1)S(1)}, bf16[3,336,512]{2,1,0:T(8,128)(2,1)}, u32[]{:S(2)}) copy-start(bf16[3,336,512]{2,1,0:T(8,128)(2,1)} %get-tuple-element.123.a1_ref) | copy-start | bytes 3096580
  88.8 4.5 %copy-start.12 = (bf16[3,336,512]{2,1,0:T(8,128)(2,1)S(1)}, bf16[3,336,512]{2,1,0:T(8,128)(2,1)}, u32[]{:S(2)}) copy-start(bf16[3,336,512]{2,1,0:T(8,128)(2,1)} %get-tuple-element.117.gm_ref) | copy-start | bytes 3096580
  89.4 3.8 %copy-start.31 = (bf16[3,84,512]{2,1,0:T(8,128)(2,1)S(1)}, bf16[3,84,512]{2,1,0:T(8,128)(2,1)}, u32[]{:S(2)}) copy-start(bf16[3,84,512]{2,1,0:T(8,128)(2,1)} %get-tuple-element.114) | copy-start | bytes 774148
  89.5 3.9 %copy-start.8 = (bf16[512,1536]{1,0:T(8,128)(2,1)S(1)}, bf16[512,1536]{1,0:T(8,128)(2,1)}, u32[]{:S(2)}) copy-start(bf16[512,1536]{1,0:T(8,128)(2,1)} %get-tuple-element.119.wq_ref) | copy-start | bytes 4718596
  89.5 3.9 %copy-start.13 = (bf16[512,512]{1,0:T(8,128)(2,1)S(1)}, bf16[512,512]{1,0:T(8,128)(2,1)}, u32[]{:S(2)}) copy-start(bf16[512,512]{1,0:T(8,128)(2,1)} %get-tuple-element.120.wo_ref) | copy-start | bytes 1572868
  89.6 3.8 %copy-start = (f32[3,336,512]{2,1,0:T(8,128)S(1)}, f32[3,336,512]{2,1,0:T(8,128)}, u32[]{:S(2)}) copy-start(f32[3,336,512]{2,1,0:T(8,128)} %get-tuple-element.108.y1_ref) | copy-start | bytes 6193156
  89.6 3.8 %copy-start.6 = (f32[512]{0:T(512)S(1)}, f32[512]{0:T(512)}, u32[]{:S(2)}) copy-start(f32[512]{0:T(512)} %param.18) | copy-start | bytes 6148
  89.6 3.8 %copy-start.7 = (f32[512]{0:T(512)S(1)}, f32[512]{0:T(512)}, u32[]{:S(2)}) copy-start(f32[512]{0:T(512)} %param.23) | copy-start | bytes 6148
  89.7 28.1 %collective-permute-start.17 = (bf16[2,272,512]{2,1,0:T(8,128)(2,1)S(1)}, bf16[2,272,512]{2,1,0:T(8,128)(2,1)S(1)}, u32[]{:S(2)}, u32[]{:S(2)}) collective-permute-start(bf16[2,272,512]{2,1,0:T(8,128)(2,1)S(1)} %constant_dynamic-slice_fusion.3), channel_id=1, source_target_pairs={{0,4},{4,0},{8,12},{12,8},{16,20},{20,16},{24,28},{28,24},{1,5},{5... | collective-permute-start | bytes 1671176 | tf_op jit(solution)/shard_map/ppermute | solution.py:447
  91.2 26.6 %collective-permute-start.16 = (bf16[544,512]{1,0:T(8,128)(2,1)S(1)}, bf16[544,512]{1,0:T(8,128)(2,1)S(1)}, u32[]{:S(2)}, u32[]{:S(2)}) collective-permute-start(bf16[544,512]{1,0:T(8,128)(2,1)S(1)} %slice_bitcast_fusion.1.after_ref), channel_id=1, source_target_pairs={{0,2},{1,3},{2,0},{3,1},{4,6},{5,7},{6,4},{7,5},{8,10},{9,11},{10,... | collective-permute-start | bytes 1671176 | tf_op jit(solution)/shard_map/ppermute | solution.py:447
  91.8 26.0 %collective-permute-start.19 = (bf16[6,84,512]{2,1,0:T(8,128)(2,1)S(1)}, bf16[6,84,512]{2,1,0:T(8,128)(2,1)S(1)}, u32[]{:S(2)}, u32[]{:S(2)}) collective-permute-start(bf16[6,84,512]{2,1,0:T(8,128)(2,1)S(1)} %copy-done.27), channel_id=1, source_target_pairs={{0,2},{1,3},{2,0},{3,1},{4,6},{5,7},{6,4},{7,5},{8,10},{9,11},{10,... | collective-permute-start | bytes 1548296 | tf_op jit(solution)/shard_map/ppermute | solution.py:447
  93.3 24.5 %collective-permute-start.18 = (bf16[3,84,512]{2,1,0:T(8,128)(2,1)S(1)}, bf16[3,84,512]{2,1,0:T(8,128)(2,1)S(1)}, u32[]{:S(2)}, u32[]{:S(2)}) collective-permute-start(bf16[3,84,512]{2,1,0:T(8,128)(2,1)S(1)} %copy-done.31), channel_id=1, source_target_pairs={{0,1},{1,0},{2,3},{3,2},{4,5},{5,4},{6,7},{7,6},{8,9},{9,8},{10,11... | collective-permute-start | bytes 774152 | tf_op jit(solution)/shard_map/ppermute | solution.py:447
  120.0 3.1 %collective-permute-start.21 = (bf16[2,576,512]{2,1,0:T(8,128)(2,1)S(1)}, bf16[2,576,512]{2,1,0:T(8,128)(2,1)}, u32[]{:S(2)}, u32[]{:S(2)}) collective-permute-start(bf16[2,576,512]{2,1,0:T(8,128)(2,1)S(1)} %get-tuple-element.133), channel_id=1, source_target_pairs={{0,1},{1,0},{2,3},{3,2},{4,5},{5,4},{6,7},{7,6},{8,9},{9,8},{10,11... | collective-permute-start | bytes 3538952 | tf_op jit(solution)/shard_map/ppermute | solution.py:447
  120.4 8.8 %collective-permute-start.25 = (bf16[272,512]{1,0:T(8,128)(2,1)}, bf16[272,512]{1,0:T(8,128)(2,1)S(1)}, u32[]{:S(2)}, u32[]{:S(2)}) collective-permute-start(bf16[272,512]{1,0:T(8,128)(2,1)} %slice_bitcast_fusion.5), channel_id=1, source_target_pairs={{0,2},{1,3},{2,0},{3,1},{4,6},{5,7},{6,4},{7,5},{8,10},{9,11},{10,... | collective-permute-start | bytes 835592 | tf_op jit(solution)/shard_map/ppermute | solution.py:447
  121.1 8.6 %collective-permute-start.24 = (bf16[272,512]{1,0:T(8,128)(2,1)}, bf16[272,512]{1,0:T(8,128)(2,1)S(1)}, u32[]{:S(2)}, u32[]{:S(2)}) collective-permute-start(bf16[272,512]{1,0:T(8,128)(2,1)} %constant_dynamic-slice_fusion.2), channel_id=1, source_target_pairs={{0,4},{4,0},{8,12},{12,8},{16,20},{20,16},{24,28},{28,24},{1,5},{5... | collective-permute-start | bytes 835592 | tf_op jit(solution)/shard_map/ppermute | solution.py:447
  122.5 4.5 %collective-permute-start.20 = (bf16[6,84,512]{2,1,0:T(8,128)(2,1)S(1)}, bf16[6,84,512]{2,1,0:T(8,128)(2,1)S(1)}, u32[]{:S(2)}, u32[]{:S(2)}) collective-permute-start(bf16[6,84,512]{2,1,0:T(8,128)(2,1)S(1)} %collective-permute-done.19.b2), channel_id=1, source_target_pairs={{0,1},{1,0},{2,3},{3,2},{4,5},{5,4},{6,7},{7,6},{8,9},{9,8},{10,11... | collective-permute-start | bytes 1548296 | tf_op jit(solution)/shard_map/ppermute | solution.py:447
  124.7 9.9 %collective-permute-start.23 = (bf16[2,144,512]{2,1,0:T(8,128)(2,1)S(1)}, bf16[2,144,512]{2,1,0:T(8,128)(2,1)S(1)}, u32[]{:S(2)}, u32[]{:S(2)}) collective-permute-start(bf16[2,144,512]{2,1,0:T(8,128)(2,1)S(1)} %constant_dynamic-slice_fusion.1), channel_id=1, source_target_pairs={{0,8},{4,12},{8,0},{12,4},{16,24},{20,28},{24,16},{28,20},{1,9},{5... | collective-permute-start | bytes 884744 | tf_op jit(solution)/shard_map/ppermute | solution.py:447
  126.4 3.3 %copy-start.15 = (bf16[2,272,512]{2,1,0:T(8,128)(2,1)S(1)}, bf16[2,272,512]{2,1,0:T(8,128)(2,1)}, u32[]{:S(2)}) copy-start(bf16[2,272,512]{2,1,0:T(8,128)(2,1)} %copy-done.14) | copy-start | bytes 1671172
  126.4 3.3 %copy-start.18 = (bf16[544,512]{1,0:T(8,128)(2,1)S(1)}, bf16[544,512]{1,0:T(8,128)(2,1)}, u32[]{:S(2)}) copy-start(bf16[544,512]{1,0:T(8,128)(2,1)} %copy-done.17) | copy-start | bytes 1671172
  126.4 9.1 %collective-permute-start.22 = (bf16[288,512]{1,0:T(8,128)(2,1)S(1)}, bf16[288,512]{1,0:T(8,128)(2,1)S(1)}, u32[]{:S(2)}, u32[]{:S(2)}) collective-permute-start(bf16[288,512]{1,0:T(8,128)(2,1)S(1)} %slice_bitcast_fusion.3), channel_id=1, source_target_pairs={{0,2},{1,3},{2,0},{3,1},{4,6},{5,7},{6,4},{7,5},{8,10},{9,11},{10,... | collective-permute-start | bytes 884744 | tf_op jit(solution)/shard_map/ppermute | solution.py:447
  130.2 10.4 %collective-permute-start.28 = (bf16[272,512]{1,0:T(8,128)(2,1)S(1)}, bf16[272,512]{1,0:T(8,128)(2,1)S(1)}, u32[]{:S(2)}, u32[]{:S(2)}) collective-permute-start(bf16[272,512]{1,0:T(8,128)(2,1)S(1)} %fusion.5), channel_id=1, source_target_pairs={{0,8},{4,12},{8,0},{12,4},{16,24},{20,28},{24,16},{28,20},{1,9},{5... | collective-permute-start | bytes 835592 | tf_op jit(solution)/shard_map/ppermute | solution.py:447
  135.7 8.0 %copy-start.3 = (bf16[6,84,512]{2,1,0:T(8,128)(2,1)S(1)}, bf16[6,84,512]{2,1,0:T(8,128)(2,1)}, u32[]{:S(2)}) copy-start(bf16[6,84,512]{2,1,0:T(8,128)(2,1)} %copy-done.2) | copy-start | bytes 1548292
  135.7 8.6 %copy-start.5 = (bf16[3,84,512]{2,1,0:T(8,128)(2,1)S(1)}, bf16[3,84,512]{2,1,0:T(8,128)(2,1)}, u32[]{:S(2)}) copy-start(bf16[3,84,512]{2,1,0:T(8,128)(2,1)} %copy-done.4) | copy-start | bytes 774148
  135.7 8.6 %collective-permute-start.27 = (bf16[144,512]{1,0:T(8,128)(2,1)S(1)}, bf16[144,512]{1,0:T(8,128)(2,1)S(1)}, u32[]{:S(2)}, u32[]{:S(2)}) collective-permute-start(bf16[144,512]{1,0:T(8,128)(2,1)S(1)} %slice_bitcast_fusion.7), channel_id=1, source_target_pairs={{0,2},{1,3},{2,0},{3,1},{4,6},{5,7},{6,4},{7,5},{8,10},{9,11},{10,... | collective-permute-start | bytes 442376 | tf_op jit(solution)/shard_map/ppermute | solution.py:447
  136.6 7.7 %collective-permute-start.26 = (bf16[144,512]{1,0:T(8,128)(2,1)S(1)}, bf16[144,512]{1,0:T(8,128)(2,1)S(1)}, u32[]{:S(2)}, u32[]{:S(2)}) collective-permute-start(bf16[144,512]{1,0:T(8,128)(2,1)S(1)} %constant_dynamic-slice_fusion), channel_id=1, source_target_pairs={{0,8},{4,12},{8,0},{12,4},{16,24},{20,28},{24,16},{28,20},{1,9},{5... | collective-permute-start | bytes 442376 | tf_op jit(solution)/shard_map/ppermute | solution.py:447
  141.0 14.5 %collective-permute-start.32 = (bf16[272,512]{1,0:T(8,128)(2,1)S(1)}, bf16[272,512]{1,0:T(8,128)(2,1)S(1)}, u32[]{:S(2)}, u32[]{:S(2)}) collective-permute-start(bf16[272,512]{1,0:T(8,128)(2,1)S(1)} %add_convert_fusion.5), channel_id=1, source_target_pairs={{0,16},{4,20},{8,24},{12,28},{16,0},{20,4},{24,8},{28,12},{1,17},{... | collective-permute-start | bytes 835592 | tf_op jit(solution)/shard_map/ppermute | solution.py:447
  143.7 13.3 %collective-permute-start.31 = (bf16[6,84,512]{2,1,0:T(8,128)(2,1)S(1)}, bf16[6,84,512]{2,1,0:T(8,128)(2,1)S(1)}, u32[]{:S(2)}, u32[]{:S(2)}) collective-permute-start(bf16[6,84,512]{2,1,0:T(8,128)(2,1)S(1)} %copy-done.3), channel_id=1, source_target_pairs={{0,2},{1,3},{2,0},{3,1},{4,6},{5,7},{6,4},{7,5},{8,10},{9,11},{10,... | collective-permute-start | bytes 1548296 | tf_op jit(solution)/shard_map/ppermute | solution.py:447
  144.3 12.7 %collective-permute-start.30 = (bf16[3,84,512]{2,1,0:T(8,128)(2,1)S(1)}, bf16[3,84,512]{2,1,0:T(8,128)(2,1)S(1)}, u32[]{:S(2)}, u32[]{:S(2)}) collective-permute-start(bf16[3,84,512]{2,1,0:T(8,128)(2,1)S(1)} %copy-done.5), channel_id=1, source_target_pairs={{0,1},{1,0},{2,3},{3,2},{4,5},{5,4},{6,7},{7,6},{8,9},{9,8},{10,11... | collective-permute-start | bytes 774152 | tf_op jit(solution)/shard_map/ppermute | solution.py:447
  144.6 12.4 %collective-permute-start.29 = (bf16[144,512]{1,0:T(8,128)(2,1)S(1)}, bf16[144,512]{1,0:T(8,128)(2,1)S(1)}, u32[]{:S(2)}, u32[]{:S(2)}) collective-permute-start(bf16[144,512]{1,0:T(8,128)(2,1)S(1)} %fusion.7), channel_id=1, source_target_pairs={{0,4},{4,0},{8,12},{12,8},{16,20},{20,16},{24,28},{28,24},{1,5},{5... | collective-permute-start | bytes 442376 | tf_op jit(solution)/shard_map/ppermute | solution.py:447
  155.6 5.1 %collective-permute-start.34 = (bf16[136,512]{1,0:T(8,128)(2,1)S(1)}, bf16[136,512]{1,0:T(8,128)(2,1)S(1)}, u32[]{:S(2)}, u32[]{:S(2)}) collective-permute-start(bf16[136,512]{1,0:T(8,128)(2,1)S(1)} %get-tuple-element.216), channel_id=1, source_target_pairs={{0,8},{4,12},{8,0},{12,4},{16,24},{20,28},{24,16},{28,20},{1,9},{5... | collective-permute-start | bytes 417800 | tf_op jit(solution)/shard_map/ppermute | solution.py:447
  156.4 5.3 %collective-permute-start.35 = (bf16[136,512]{1,0:T(8,128)(2,1)S(1)}, bf16[136,512]{1,0:T(8,128)(2,1)S(1)}, u32[]{:S(2)}, u32[]{:S(2)}) collective-permute-start(bf16[136,512]{1,0:T(8,128)(2,1)S(1)} %get-tuple-element.215), channel_id=1, source_target_pairs={{0,4},{4,0},{8,12},{12,8},{16,20},{20,16},{24,28},{28,24},{1,5},{5... | collective-permute-start | bytes 417800 | tf_op jit(solution)/shard_map/ppermute | solution.py:447
  157.2 6.5 %collective-permute-start.33 = (bf16[6,84,512]{2,1,0:T(8,128)(2,1)S(1)}, bf16[6,84,512]{2,1,0:T(8,128)(2,1)S(1)}, u32[]{:S(2)}, u32[]{:S(2)}) collective-permute-start(bf16[6,84,512]{2,1,0:T(8,128)(2,1)S(1)} %collective-permute-done.31.b2), channel_id=1, source_target_pairs={{0,1},{1,0},{2,3},{3,2},{4,5},{5,4},{6,7},{7,6},{8,9},{9,8},{10,11... | collective-permute-start | bytes 1548296 | tf_op jit(solution)/shard_map/ppermute | solution.py:447
  157.3 11.1 %collective-permute-start.36 = (bf16[144,512]{1,0:T(8,128)(2,1)S(1)}, bf16[144,512]{1,0:T(8,128)(2,1)S(1)}, u32[]{:S(2)}, u32[]{:S(2)}) collective-permute-start(bf16[144,512]{1,0:T(8,128)(2,1)S(1)} %add_convert_fusion.8), channel_id=1, source_target_pairs={{0,16},{4,20},{8,24},{12,28},{16,0},{20,4},{24,8},{28,12},{1,17},{... | collective-permute-start | bytes 442376 | tf_op jit(solution)/shard_map/ppermute | solution.py:447
  161.7 9.9 %collective-permute-start.40 = (bf16[2,136,512]{2,1,0:T(8,128)(2,1)S(1)}, bf16[2,136,512]{2,1,0:T(8,128)(2,1)S(1)}, u32[]{:S(2)}, u32[]{:S(2)}) collective-permute-start(bf16[2,136,512]{2,1,0:T(8,128)(2,1)S(1)} %maximum_select_fusion.5), channel_id=1, source_target_pairs={{0,8},{4,12},{8,0},{12,4},{16,24},{20,28},{24,16},{28,20},{1,9},{5... | collective-permute-start | bytes 835592 | tf_op jit(solution)/shard_map/ppermute | solution.py:447
  162.9 8.7 %collective-permute-start.39 = (bf16[2,136,512]{2,1,0:T(8,128)(2,1)S(1)}, bf16[2,136,512]{2,1,0:T(8,128)(2,1)S(1)}, u32[]{:S(2)}, u32[]{:S(2)}) collective-permute-start(bf16[2,136,512]{2,1,0:T(8,128)(2,1)S(1)} %maximum_select_fusion.4), channel_id=1, source_target_pairs={{0,4},{4,0},{8,12},{12,8},{16,20},{20,16},{24,28},{28,24},{1,5},{5... | collective-permute-start | bytes 835592 | tf_op jit(solution)/shard_map/ppermute | solution.py:447
  168.5 5.9 %collective-permute-start.37 = (bf16[72,512]{1,0:T(8,128)(2,1)S(1)}, bf16[72,512]{1,0:T(8,128)(2,1)S(1)}, u32[]{:S(2)}, u32[]{:S(2)}) collective-permute-start(bf16[72,512]{1,0:T(8,128)(2,1)S(1)} %get-tuple-element.222), channel_id=1, source_target_pairs={{0,4},{4,0},{8,12},{12,8},{16,20},{20,16},{24,28},{28,24},{1,5},{5... | collective-permute-start | bytes 221192 | tf_op jit(solution)/shard_map/ppermute | solution.py:447
  170.0 4.4 %collective-permute-start.38 = (bf16[72,512]{1,0:T(8,128)(2,1)S(1)}, bf16[72,512]{1,0:T(8,128)(2,1)S(1)}, u32[]{:S(2)}, u32[]{:S(2)}) collective-permute-start(bf16[72,512]{1,0:T(8,128)(2,1)S(1)} %get-tuple-element.221), channel_id=1, source_target_pairs={{0,8},{4,12},{8,0},{12,4},{16,24},{20,28},{24,16},{28,20},{1,9},{5... | collective-permute-start | bytes 221192 | tf_op jit(solution)/shard_map/ppermute | solution.py:447
  174.4 5.2 %collective-permute-start.41 = (bf16[2,72,512]{2,1,0:T(8,128)(2,1)S(1)}, bf16[2,72,512]{2,1,0:T(8,128)(2,1)S(1)}, u32[]{:S(2)}, u32[]{:S(2)}) collective-permute-start(bf16[2,72,512]{2,1,0:T(8,128)(2,1)S(1)} %maximum_select_fusion.9), channel_id=1, source_target_pairs={{0,8},{4,12},{8,0},{12,4},{16,24},{20,28},{24,16},{28,20},{1,9},{5... | collective-permute-start | bytes 442376 | tf_op jit(solution)/shard_map/ppermute | solution.py:447
  176.2 5.2 %collective-permute-start.42 = (bf16[2,72,512]{2,1,0:T(8,128)(2,1)S(1)}, bf16[2,72,512]{2,1,0:T(8,128)(2,1)S(1)}, u32[]{:S(2)}, u32[]{:S(2)}) collective-permute-start(bf16[2,72,512]{2,1,0:T(8,128)(2,1)S(1)} %maximum_select_fusion.11), channel_id=1, source_target_pairs={{0,4},{4,0},{8,12},{12,8},{16,20},{20,16},{24,28},{28,24},{1,5},{5... | collective-permute-start | bytes 442376 | tf_op jit(solution)/shard_map/ppermute | solution.py:447
  (17 other events, 29.1 us)

commit v4 on v3

--- a/solution.py
+++ b/solution.py
@@ -336,12 +336,12 @@
     do_sc[...] = dot(ga, wo_ref[...], NT).astype(BF16)
     lane = lax.broadcasted_iota(jnp.int32, (length, 128), 1)
     scale = HD ** -0.5
+    cut = min(256, length)
     for p in range(4):
         q = qkv_ref[0, :, pl.ds(p * 384, 128)]
         k = qkv_ref[0, :, pl.ds(p * 384 + 128, 128)]
         v = qkv_ref[0, :, pl.ds(p * 384 + 256, 128)]
         do = do_sc[:, pl.ds(p * 128, 128)]
-        dq = dk = dv = None
         for h in range(2):
             mine = (lane < HD) if h == 0 else (lane >= HD)
             zero = jnp.zeros_like(q)
@@ -351,11 +351,14 @@
             probs = prob.astype(F32)
             pd = probs * dp
             ds = (pd - probs * jnp.sum(pd, axis=0, keepdims=True)).astype(BF16)
-            parts = dot(ds, kh, TN), dot(ds, qh), dot(prob, doh)
-            dq, dk, dv = parts if dq is None else (dq + parts[0], dk + parts[1], dv + parts[2])
-        dqkv_ref[0, :, pl.ds(p * 384, 128)] = (dq * scale).astype(BF16)
-        dqkv_ref[0, :, pl.ds(p * 384 + 128, 128)] = (dk * scale).astype(BF16)
-        dqkv_ref[0, :, pl.ds(p * 384 + 256, 128)] = dv.astype(BF16)
+            pq = dot(ds[:cut, :cut], kh[:cut], TN), dot(ds[:, cut:], kh, TN)
+            pk = dot(ds[:cut], qh), dot(ds[cut:, cut:], qh[cut:])
+            pv = dot(prob[:cut], doh), dot(prob[cut:, cut:], doh[cut:])
+            parts = (pq, pk, pv)
+            total = parts if h == 0 else [[b + c for b, c in zip(*pair)] for pair in zip(total, parts)]
+        for n, (kind, factor) in enumerate(zip(total, (scale, scale, 1.0))):
+            for rows, value in zip((pl.ds(0, cut), pl.ds(cut, length - cut)), kind):
+                dqkv_ref[0, rows, pl.ds(p * 384 + 128 * n, 128)] = (value * factor).astype(BF16)
 
     da1 = dot(dqkv_ref[0], wq_ref[...], NT)
     hat, inv = stats(x_ref[0].astype(F32))

time: 185 us -> 183 us (0.989)
  transfers between devices with their start and end apart: 43 -> 43, of which waited for: 19 -> 20; matrix products, arithmetic and copies ran while one was open for 4% -> 4% of each run, Pallas kernels for 27% -> 26%
where the time goes in v4:
time: 183 us
  Pallas kernels  68.2 us (37%)
  waiting for transfers between devices  55.1 us (30%)
  starting transfers between devices  41.5 us (23%)
  local copies, waits for them, and re-layouts  10.6 us (6%)
  other arithmetic  5.27 us (3%)
  between operations  2.14 us (1%)
    pallas_call x7, Pallas kernels, call(): pl.pallas_call(kernel, grid_spec=pltpu.PrefetchScalarGridSpec(num_scalar_...  68.2 us
    ppermute x43, waiting for transfers between devices, hop(): return lax.ppermute(value, axis, [(i, i ^ bit) for i in range(n)])  55.1 us
    ppermute x43, starting transfers between devices, hop(): return lax.ppermute(value, axis, [(i, i ^ bit) for i in range(n)])  41.5 us
  transfers between devices with their start and end apart: 43, of which 20 were waited for; matrix products, arithmetic and copies ran while one was open for 4% of the time, Pallas kernels for 26%

profile of v4, /device:TPU:0, one launch (start us, length us, event | category | flops | bytes accessed | tf_op | source)
XLA Modules:
  0.0 182.8 jit_solution(4830520339635752915)
XLA Ops:
  0.7 3.1 %pack_weights.1 = (bf16[1568,512]{1,0:T(8,128)(2,1)}, bf16[800,512]{1,0:T(8,128)(2,1)}) custom-call(s32[1]{0:T(128)} %bitcast.1.y_ref, s32[1]{0:T(128)} %bitcast.2.z_ref, bf16[512,384]{1,0:T(8,128)(2,1)} %wqkv_ref.1, bf16[128,512]{1,0:T(8,128)(2,1)} %wout_ref.1, f32[1,512]{1,0:T(1,128)} %bitcast.122, bf16[512,512]{1,0:T(8,128)(2,1)} %up_ref.1, ...), custom_call_target="tpu_custom_call" | custom-call | bytes 3999744 | tf_op jit(solution)/shard_map/pack_weights/pallas_call | solution.py:56
  3.8 0.5 collective-permute-start
  4.2 2.5 %collective-permute-start.1 = (bf16[800,512]{1,0:T(8,128)(2,1)}, bf16[800,512]{1,0:T(8,128)(2,1)S(1)}, u32[]{:S(2)}, u32[]{:S(2)}) collective-permute-start(bf16[800,512]{1,0:T(8,128)(2,1)} %get-tuple-element.92), channel_id=1, source_target_pairs={{0,2},{1,3},{2,0},{3,1},{4,6},{5,7},{6,4},{7,5},{8,10},{9,11},{10,... | collective-permute-start | bytes 2457608 | tf_op jit(solution)/shard_map/ppermute | solution.py:450
  6.7 0.8 collective-permute-done.w1
  7.5 0.9 dynamic-slice_bitcast_fusion.1
  8.8 2.9 %collective-permute-start.2 = (bf16[6,84,512]{2,1,0:T(8,128)(2,1)S(1)}, bf16[6,84,512]{2,1,0:T(8,128)(2,1)S(1)}, u32[]{:S(2)}, u32[]{:S(2)}) collective-permute-start(bf16[6,84,512]{2,1,0:T(8,128)(2,1)S(1)} %pad_maximum_fusion.2), channel_id=1, source_target_pairs={{0,2},{1,3},{2,0},{3,1},{4,6},{5,7},{6,4},{7,5},{8,10},{9,11},{10,... | collective-permute-start | bytes 1548296 | tf_op jit(solution)/shard_map/ppermute | solution.py:450
  11.7 0.8 dynamic-slice_bitcast_fusion
  12.4 0.5 collective-permute-start.3
  13.0 13.0 %collective-permute-done.1.w2.a2_ = bf16[800,512]{1,0:T(8,128)(2,1)S(1)} collective-permute-done((bf16[800,512]{1,0:T(8,128)(2,1)}, bf16[800,512]{1,0:T(8,128)(2,1)S(1)}, u32[]{:S(2)}, u32[]{:S(2)}) %collective-permute-start.1) | collective-permute-done | bytes 819232 | tf_op jit(solution)/shard_map/ppermute | solution.py:450
  26.1 11.4 %collective-permute-done.2.t2 = bf16[6,84,512]{2,1,0:T(8,128)(2,1)S(1)} collective-permute-done((bf16[6,84,512]{2,1,0:T(8,128)(2,1)S(1)}, bf16[6,84,512]{2,1,0:T(8,128)(2,1)S(1)}, u32[]{:S(2)}, u32[]{:S(2)}) %collective-permute-start.2) | collective-permute-done | bytes 516128 | tf_op jit(solution)/shard_map/ppermute | solution.py:450
  37.4 0.5 collective-permute-start.9
  38.0 1.7 collective-permute-start.13
  39.7 1.6 collective-permute-start.5
  41.4 1.5 collective-permute-start.6
  42.9 0.4 collective-permute-start.7
  43.7 0.5 copy-done.23
  44.2 16.2 %attention_forward.1 = (bf16[3,336,1536]{2,1,0:T(8,128)(2,1)}, bf16[3,8,336,336]{3,2,1,0:T(8,128)(2,1)}, bf16[3,336,512]{2,1,0:T(8,128)(2,1)}, bf16[3,336,512]{2...) custom-call(s32[1]{0:T(128)} %bitcast.me_ref, ...), custom_call_target="tpu_custom_call" | custom-call | flops 2807562240 | bytes 23279616 | tf_op jit(solution)/shard_map/attention_forward/pallas_call | solution.py:56
  60.6 0.5 collective-permute-start.10
  62.3 0.5 collective-permute-done.10.b3_
  64.5 17.4 %feed_forward.1 = (bf16[1008,2048]{1,0:T(8,128)(2,1)}, bf16[1008,2048]{1,0:T(8,128)(2,1)}, bf16[3,336,512]{2,1,0:T(8,128)(2,1)}, bf16[2,1088,512]{2,1,0:T(8,128)...) custom-call(s32[1]{0:T(128)} %bitcast.me_ref, s32[1]{0:T(128)} %bitcast.1.y_ref, s32[1]{0:T(128)} %bitcast.2.z_ref, ...), custom_call_target="tpu_custom_call" | custom-call | flops 4227858432 | bytes 27009024 | tf_op jit(solution)/shard_map/feed_forward/pallas_call | solution.py:56
  82.1 6.6 %block_output.1 = (bf16[3,84,512]{2,1,0:T(8,128)(2,1)}, bf16[3,84,512]{2,1,0:T(8,128)(2,1)}, bf16[6,84,512]{2,1,0:T(8,128)(2,1)}) custom-call(s32[1]{0:T(128)} %bitcast.me_ref, s32[1]{0:T(128)S(6)} %copy.32.count_ref, bf16[1008,2048]{1,0:T(8,128)(2,1)} %get-tuple-element.106.hm_ref, bf16[4,2,512,512]{3,2,1,0:T(8,128)(2,1)} %get-tuple-element.107.w_ref, ...), custom_call_target="tpu_custom_call" | custom-call | flops 2113929216 | bytes 12453888 | tf_op jit(solution)/shard_map/block_output/pallas_call | solution.py:56
  88.8 0.6 add_convert_fusion
  89.7 1.5 collective-permute-start.17
  91.2 0.5 collective-permute-start.16
  91.8 1.5 collective-permute-start.19
  93.4 22.8 %attention_backward.1 = (bf16[3,84,512]{2,1,0:T(8,128)(2,1)S(1)}, bf16[3,84,512]{2,1,0:T(8,128)(2,1)S(1)}, bf16[6,84,512]{2,1,0:T(8,128)(2,1)S(1)}, bf16[2,576,5...) custom-call(s32[1]{0:T(128)} %bitcast.me_ref, bf16[1008,2048]{1,0:T(8,128)(2,1)} %get-tuple-element.116.du_ref, ...), custom_call_target="tpu_custom_call" | custom-call | flops 8422686720 | bytes 29081600 | tf_op jit(solution)/shard_map/attention_backward/pallas_call | solution.py:56
  116.2 1.3 collective-permute-done.19.b2
  117.6 0.8 slice_bitcast_fusion.5
  118.6 0.8 constant_dynamic-slice_fusion.2
  119.4 0.6 collective-permute-start.25
  120.0 1.5 collective-permute-start.24
  121.5 0.9 collective-permute-done.21
  122.4 1.6 add_convert_fusion.1
  124.1 1.6 collective-permute-start.23
  125.8 0.6 collective-permute-start.22
  126.4 1.1 place.2
  127.5 1.6 collective-permute-done.25
  129.6 1.7 collective-permute-start.28
  131.3 2.7 %collective-permute-done.23 = bf16[2,144,512]{2,1,0:T(8,128)(2,1)S(1)} collective-permute-done((bf16[2,144,512]{2,1,0:T(8,128)(2,1)S(1)}, bf16[2,144,512]{2,1,0:T(8,128)(2,1)S(1)}, u32[]{:S(2)}, u32[]{:S(2)}) %collective-permute-start.23) | collective-permute-done | bytes 294944 | tf_op jit(solution)/shard_map/ppermute | solution.py:450
  134.0 1.0 collective-permute-done.22
  135.2 0.6 collective-permute-start.27
  135.9 1.6 collective-permute-start.26
  137.5 2.5 %collective-permute-done.28 = bf16[272,512]{1,0:T(8,128)(2,1)S(1)} collective-permute-done((bf16[272,512]{1,0:T(8,128)(2,1)S(1)}, bf16[272,512]{1,0:T(8,128)(2,1)S(1)}, u32[]{:S(2)}, u32[]{:S(2)}) %collective-permute-start.28) | collective-permute-done | bytes 278560 | tf_op jit(solution)/shard_map/ppermute | solution.py:450
  140.4 2.7 %collective-permute-start.32 = (bf16[272,512]{1,0:T(8,128)(2,1)S(1)}, bf16[272,512]{1,0:T(8,128)(2,1)S(1)}, u32[]{:S(2)}, u32[]{:S(2)}) collective-permute-start(bf16[272,512]{1,0:T(8,128)(2,1)S(1)} %add_convert_fusion.5), channel_id=1, source_target_pairs={{0,16},{4,20},{8,24},{12,28},{16,0},{20,4},{24,8},{28,12},{1,17},{... | collective-permute-start | bytes 835592 | tf_op jit(solution)/shard_map/ppermute | solution.py:450
  143.4 2.0 %collective-permute-start.29 = (bf16[144,512]{1,0:T(8,128)(2,1)S(1)}, bf16[144,512]{1,0:T(8,128)(2,1)S(1)}, u32[]{:S(2)}, u32[]{:S(2)}) collective-permute-start(bf16[144,512]{1,0:T(8,128)(2,1)S(1)} %fusion.7), channel_id=1, source_target_pairs={{0,4},{4,0},{8,12},{12,8},{16,20},{20,16},{24,28},{28,24},{1,5},{5... | collective-permute-start | bytes 442376 | tf_op jit(solution)/shard_map/ppermute | solution.py:450
  145.4 8.9 %collective-permute-done.32 = bf16[272,512]{1,0:T(8,128)(2,1)S(1)} collective-permute-done((bf16[272,512]{1,0:T(8,128)(2,1)S(1)}, bf16[272,512]{1,0:T(8,128)(2,1)S(1)}, u32[]{:S(2)}, u32[]{:S(2)}) %collective-permute-start.32) | collective-permute-done | bytes 278560 | tf_op jit(solution)/shard_map/ppermute | solution.py:450
  154.5 0.7 collective-permute-start.34
  156.0 3.4 %collective-permute-start.36 = (bf16[144,512]{1,0:T(8,128)(2,1)S(1)}, bf16[144,512]{1,0:T(8,128)(2,1)S(1)}, u32[]{:S(2)}, u32[]{:S(2)}) collective-permute-start(bf16[144,512]{1,0:T(8,128)(2,1)S(1)} %add_convert_fusion.8), channel_id=1, source_target_pairs={{0,16},{4,20},{8,24},{12,28},{16,0},{20,4},{24,8},{28,12},{1,17},{... | collective-permute-start | bytes 442376 | tf_op jit(solution)/shard_map/ppermute | solution.py:450
  159.7 0.9 collective-permute-done.35
  160.6 1.2 collective-permute-start.40
  161.8 0.5 collective-permute-start.39
  162.4 1.1 place.3
  163.4 3.7 %collective-permute-done.36 = bf16[144,512]{1,0:T(8,128)(2,1)S(1)} collective-permute-done((bf16[144,512]{1,0:T(8,128)(2,1)S(1)}, bf16[144,512]{1,0:T(8,128)(2,1)S(1)}, u32[]{:S(2)}, u32[]{:S(2)}) %collective-permute-start.36) | collective-permute-done | bytes 147488 | tf_op jit(solution)/shard_map/ppermute | solution.py:450
  167.2 1.7 collective-permute-start.37
  168.9 1.4 collective-permute-done.40
  170.9 1.5 fusion.8
  172.4 0.6 slice.122
  173.2 1.4 collective-permute-start.41
  174.7 1.9 %collective-permute-start.42 = (bf16[2,72,512]{2,1,0:T(8,128)(2,1)S(1)}, bf16[2,72,512]{2,1,0:T(8,128)(2,1)S(1)}, u32[]{:S(2)}, u32[]{:S(2)}) collective-permute-start(bf16[2,72,512]{2,1,0:T(8,128)(2,1)S(1)} %maximum_select_fusion.11), channel_id=1, source_target_pairs={{0,4},{4,0},{8,12},{12,8},{16,20},{20,16},{24,28},{28,24},{1,5},{5... | collective-permute-start | bytes 442376 | tf_op jit(solution)/shard_map/ppermute | solution.py:450
  176.6 1.8 %collective-permute-done.41 = bf16[2,72,512]{2,1,0:T(8,128)(2,1)S(1)} collective-permute-done((bf16[2,72,512]{2,1,0:T(8,128)(2,1)S(1)}, bf16[2,72,512]{2,1,0:T(8,128)(2,1)S(1)}, u32[]{:S(2)}, u32[]{:S(2)}) %collective-permute-start.41) | collective-permute-done | bytes 147488 | tf_op jit(solution)/shard_map/ppermute | solution.py:450
  178.5 1.4 collective-permute-done.42
  180.2 0.7 slice.119
  180.9 0.6 fusion.9
  181.6 1.2 copy.31
  (160 shorter events, 7.9 us)
Async XLA Ops:
  0.6 6.9 %copy-start.19 = (bf16[84,12,512]{2,0,1:T(8,128)(2,1)S(1)}, bf16[84,12,512]{2,0,1:T(8,128)(2,1)}, u32[]{:S(2)}) copy-start(bf16[84,12,512]{2,0,1:T(8,128)(2,1)} %param.15) | copy-start | bytes 3096580
  3.8 3.7 %collective-permute-start = (bf16[1568,512]{1,0:T(8,128)(2,1)}, bf16[1568,512]{1,0:T(8,128)(2,1)S(1)}, u32[]{:S(2)}, u32[]{:S(2)}) collective-permute-start(bf16[1568,512]{1,0:T(8,128)(2,1)} %get-tuple-element.91.w0), channel_id=1, source_target_pairs={{0,1},{1,0},{2,3},{3,2},{4,5},{5,4},{6,7},{7,6},{8,9},{9,8},{10,11... | collective-permute-start | bytes 4816904 | tf_op jit(solution)/shard_map/ppermute | solution.py:450
  4.2 21.8 %collective-permute-start.1 = (bf16[800,512]{1,0:T(8,128)(2,1)}, bf16[800,512]{1,0:T(8,128)(2,1)S(1)}, u32[]{:S(2)}, u32[]{:S(2)}) collective-permute-start(bf16[800,512]{1,0:T(8,128)(2,1)} %get-tuple-element.92), channel_id=1, source_target_pairs={{0,2},{1,3},{2,0},{3,1},{4,6},{5,7},{6,4},{7,5},{8,10},{9,11},{10,... | collective-permute-start | bytes 2457608 | tf_op jit(solution)/shard_map/ppermute | solution.py:450
  6.7 4.9 %copy-start.20 = (bf16[84,12,512]{2,0,1:T(8,128)(2,1)S(1)}, bf16[84,12,512]{2,0,1:T(8,128)(2,1)}, u32[]{:S(2)}) copy-start(bf16[84,12,512]{2,0,1:T(8,128)(2,1)} %param.29) | copy-start | bytes 3096580
  8.8 28.7 %collective-permute-start.2 = (bf16[6,84,512]{2,1,0:T(8,128)(2,1)S(1)}, bf16[6,84,512]{2,1,0:T(8,128)(2,1)S(1)}, u32[]{:S(2)}, u32[]{:S(2)}) collective-permute-start(bf16[6,84,512]{2,1,0:T(8,128)(2,1)S(1)} %pad_maximum_fusion.2), channel_id=1, source_target_pairs={{0,2},{1,3},{2,0},{3,1},{4,6},{5,7},{6,4},{7,5},{8,10},{9,11},{10,... | collective-permute-start | bytes 1548296 | tf_op jit(solution)/shard_map/ppermute | solution.py:450
  12.4 13.6 %collective-permute-start.4 = (bf16[3,84,512]{2,1,0:T(8,128)(2,1)S(1)}, bf16[3,84,512]{2,1,0:T(8,128)(2,1)S(1)}, u32[]{:S(2)}, u32[]{:S(2)}) collective-permute-start(bf16[3,84,512]{2,1,0:T(8,128)(2,1)S(1)} %get-tuple-element.204), channel_id=1, source_target_pairs={{0,1},{1,0},{2,3},{3,2},{4,5},{5,4},{6,7},{7,6},{8,9},{9,8},{10,11... | collective-permute-start | bytes 774152 | tf_op jit(solution)/shard_map/ppermute | solution.py:450
  12.4 13.6 %collective-permute-start.3 = (bf16[3,84,512]{2,1,0:T(8,128)(2,1)S(1)}, bf16[3,84,512]{2,1,0:T(8,128)(2,1)S(1)}, u32[]{:S(2)}, u32[]{:S(2)}) collective-permute-start(bf16[3,84,512]{2,1,0:T(8,128)(2,1)S(1)} %get-tuple-element.208), channel_id=1, source_target_pairs={{0,1},{1,0},{2,3},{3,2},{4,5},{5,4},{6,7},{7,6},{8,9},{9,8},{10,11... | collective-permute-start | bytes 774152 | tf_op jit(solution)/shard_map/ppermute | solution.py:450
  26.0 17.3 %copy-start.21 = (bf16[800,512]{1,0:T(8,128)(2,1)}, bf16[800,512]{1,0:T(8,128)(2,1)S(1)}, u32[]{:S(2)}) copy-start(bf16[800,512]{1,0:T(8,128)(2,1)S(1)} %collective-permute-done.1.w2.a2_) | copy-start | bytes 2457604
  26.0 34.3 %copy-start.29 = (bf16[3,84,512]{2,1,0:T(8,128)(2,1)}, bf16[3,84,512]{2,1,0:T(8,128)(2,1)S(1)}, u32[]{:S(2)}) copy-start(bf16[3,84,512]{2,1,0:T(8,128)(2,1)S(1)} %collective-permute-done.4.c1) | copy-start | bytes 774148
  26.0 17.3 %copy-start.30 = (bf16[3,84,512]{2,1,0:T(8,128)(2,1)}, bf16[3,84,512]{2,1,0:T(8,128)(2,1)S(1)}, u32[]{:S(2)}) copy-start(bf16[3,84,512]{2,1,0:T(8,128)(2,1)S(1)} %collective-permute-done.3.t1) | copy-start | bytes 774148
  37.4 5.9 %copy-start.25 = (bf16[6,84,512]{2,1,0:T(8,128)(2,1)}, bf16[6,84,512]{2,1,0:T(8,128)(2,1)S(1)}, u32[]{:S(2)}) copy-start(bf16[6,84,512]{2,1,0:T(8,128)(2,1)S(1)} %collective-permute-done.2.t2) | copy-start | bytes 1548292
  37.4 5.9 %collective-permute-start.8 = (bf16[800,512]{1,0:T(8,128)(2,1)S(1)}, bf16[800,512]{1,0:T(8,128)(2,1)S(1)}, u32[]{:S(2)}, u32[]{:S(2)}) collective-permute-start(bf16[800,512]{1,0:T(8,128)(2,1)S(1)} %collective-permute-done.1.w2.a2_), channel_id=1, source_target_pairs={{0,1},{1,0},{2,3},{3,2},{4,5},{5,4},{6,7},{7,6},{8,9},{9,8},{10,11... | collective-permute-start | bytes 2457608 | tf_op jit(solution)/shard_map/ppermute | solution.py:450
  37.4 5.4 %collective-permute-start.9 = (bf16[6,84,512]{2,1,0:T(8,128)(2,1)S(1)}, bf16[6,84,512]{2,1,0:T(8,128)(2,1)S(1)}, u32[]{:S(2)}, u32[]{:S(2)}) collective-permute-start(bf16[6,84,512]{2,1,0:T(8,128)(2,1)S(1)} %collective-permute-done.2.t2), channel_id=1, source_target_pairs={{0,1},{1,0},{2,3},{3,2},{4,5},{5,4},{6,7},{7,6},{8,9},{9,8},{10,11... | collective-permute-start | bytes 1548296 | tf_op jit(solution)/shard_map/ppermute | solution.py:450
  38.0 22.4 %collective-permute-start.13 = (bf16[6,84,512]{2,1,0:T(8,128)(2,1)S(1)}, bf16[6,84,512]{2,1,0:T(8,128)(2,1)S(1)}, u32[]{:S(2)}, u32[]{:S(2)}) collective-permute-start(bf16[6,84,512]{2,1,0:T(8,128)(2,1)S(1)} %pad_maximum_fusion.3), channel_id=1, source_target_pairs={{0,2},{1,3},{2,0},{3,1},{4,6},{5,7},{6,4},{7,5},{8,10},{9,11},{10,... | collective-permute-start | bytes 1548296 | tf_op jit(solution)/shard_map/ppermute | solution.py:450
  39.7 20.8 %collective-permute-start.5 = (bf16[256,512]{1,0:T(8,128)(2,1)S(1)}, bf16[256,512]{1,0:T(8,128)(2,1)S(1)}, u32[]{:S(2)}, u32[]{:S(2)}) collective-permute-start(bf16[256,512]{1,0:T(8,128)(2,1)S(1)} %slice.78), channel_id=1, source_target_pairs={{0,8},{4,12},{8,0},{12,4},{16,24},{20,28},{24,16},{28,20},{1,9},{5... | collective-permute-start | bytes 786440 | tf_op jit(solution)/shard_map/ppermute | solution.py:450
  41.4 19.2 %collective-permute-start.6 = (bf16[256,512]{1,0:T(8,128)(2,1)S(1)}, bf16[256,512]{1,0:T(8,128)(2,1)S(1)}, u32[]{:S(2)}, u32[]{:S(2)}) collective-permute-start(bf16[256,512]{1,0:T(8,128)(2,1)S(1)} %slice.78), channel_id=1, source_target_pairs={{0,4},{4,0},{8,12},{12,8},{16,20},{20,16},{24,28},{28,24},{1,5},{5... | collective-permute-start | bytes 786440 | tf_op jit(solution)/shard_map/ppermute | solution.py:450
  42.9 17.7 %collective-permute-start.7 = (bf16[256,512]{1,0:T(8,128)(2,1)S(1)}, bf16[256,512]{1,0:T(8,128)(2,1)S(1)}, u32[]{:S(2)}, u32[]{:S(2)}) collective-permute-start(bf16[256,512]{1,0:T(8,128)(2,1)S(1)} %slice.78), channel_id=1, source_target_pairs={{0,12},{4,8},{8,4},{12,0},{16,28},{20,24},{24,20},{28,16},{1,13},{... | collective-permute-start | bytes 786440 | tf_op jit(solution)/shard_map/ppermute | solution.py:450
  60.4 3.1 %collective-permute-start.14 = (bf16[6,84,512]{2,1,0:T(8,128)(2,1)S(1)}, bf16[6,84,512]{2,1,0:T(8,128)(2,1)S(1)}, u32[]{:S(2)}, u32[]{:S(2)}) collective-permute-start(bf16[6,84,512]{2,1,0:T(8,128)(2,1)S(1)} %collective-permute-done.13.c2), channel_id=1, source_target_pairs={{0,1},{1,0},{2,3},{3,2},{4,5},{5,4},{6,7},{7,6},{8,9},{9,8},{10,11... | collective-permute-start | bytes 1548296 | tf_op jit(solution)/shard_map/ppermute | solution.py:450
  60.6 2.2 %collective-permute-start.10 = (bf16[256,512]{1,0:T(8,128)(2,1)S(1)}, bf16[256,512]{1,0:T(8,128)(2,1)S(1)}, u32[]{:S(2)}, u32[]{:S(2)}) collective-permute-start(bf16[256,512]{1,0:T(8,128)(2,1)S(1)} %collective-permute-done.5.b2_), channel_id=1, source_target_pairs={{0,1},{1,0},{2,3},{3,2},{4,5},{5,4},{6,7},{7,6},{8,9},{9,8},{10,11... | collective-permute-start | bytes 786440 | tf_op jit(solution)/shard_map/ppermute | solution.py:450
  61.1 2.1 %collective-permute-start.11 = (bf16[256,512]{1,0:T(8,128)(2,1)S(1)}, bf16[256,512]{1,0:T(8,128)(2,1)S(1)}, u32[]{:S(2)}, u32[]{:S(2)}) collective-permute-start(bf16[256,512]{1,0:T(8,128)(2,1)S(1)} %collective-permute-done.6.c2_), channel_id=1, source_target_pairs={{0,1},{1,0},{2,3},{3,2},{4,5},{5,4},{6,7},{7,6},{8,9},{9,8},{10,11... | collective-permute-start | bytes 786440 | tf_op jit(solution)/shard_map/ppermute | solution.py:450
  61.2 2.4 %collective-permute-start.12 = (bf16[256,512]{1,0:T(8,128)(2,1)S(1)}, bf16[256,512]{1,0:T(8,128)(2,1)S(1)}, u32[]{:S(2)}, u32[]{:S(2)}) collective-permute-start(bf16[256,512]{1,0:T(8,128)(2,1)S(1)} %collective-permute-done.7.d2_), channel_id=1, source_target_pairs={{0,1},{1,0},{2,3},{3,2},{4,5},{5,4},{6,7},{7,6},{8,9},{9,8},{10,11... | collective-permute-start | bytes 786440 | tf_op jit(solution)/shard_map/ppermute | solution.py:450
  81.9 6.8 %collective-permute-start.15 = (bf16[2,1088,512]{2,1,0:T(8,128)(2,1)}, bf16[2,1088,512]{2,1,0:T(8,128)(2,1)S(1)}, u32[]{:S(2)}, u32[]{:S(2)}) collective-permute-start(bf16[2,1088,512]{2,1,0:T(8,128)(2,1)} %get-tuple-element.105), channel_id=1, source_target_pairs={{0,1},{1,0},{2,3},{3,2},{4,5},{5,4},{6,7},{7,6},{8,9},{9,8},{10,11... | collective-permute-start | bytes 6684680 | tf_op jit(solution)/shard_map/ppermute | solution.py:450
  82.1 6.7 %copy-start.16 = (bf16[2,1088,512]{2,1,0:T(8,128)(2,1)S(1)}, bf16[2,1088,512]{2,1,0:T(8,128)(2,1)}, u32[]{:S(2)}) copy-start(bf16[2,1088,512]{2,1,0:T(8,128)(2,1)} %get-tuple-element.104) | copy-start | bytes 6684676
  88.8 4.5 %copy-start.9 = (bf16[3,336,512]{2,1,0:T(8,128)(2,1)S(1)}, bf16[3,336,512]{2,1,0:T(8,128)(2,1)}, u32[]{:S(2)}) copy-start(bf16[3,336,512]{2,1,0:T(8,128)(2,1)} %get-tuple-element.124.o_ref) | copy-start | bytes 3096580
  88.8 4.5 %copy-start.10 = (bf16[3,336,512]{2,1,0:T(8,128)(2,1)S(1)}, bf16[3,336,512]{2,1,0:T(8,128)(2,1)}, u32[]{:S(2)}) copy-start(bf16[3,336,512]{2,1,0:T(8,128)(2,1)} %get-tuple-element.118.x_ref) | copy-start | bytes 3096580
  88.8 4.5 %copy-start.11 = (bf16[3,336,512]{2,1,0:T(8,128)(2,1)S(1)}, bf16[3,336,512]{2,1,0:T(8,128)(2,1)}, u32[]{:S(2)}) copy-start(bf16[3,336,512]{2,1,0:T(8,128)(2,1)} %get-tuple-element.123.a1_ref) | copy-start | bytes 3096580
  88.8 4.5 %copy-start.12 = (bf16[3,336,512]{2,1,0:T(8,128)(2,1)S(1)}, bf16[3,336,512]{2,1,0:T(8,128)(2,1)}, u32[]{:S(2)}) copy-start(bf16[3,336,512]{2,1,0:T(8,128)(2,1)} %get-tuple-element.117.gm_ref) | copy-start | bytes 3096580
  89.4 3.8 %copy-start.31 = (bf16[3,84,512]{2,1,0:T(8,128)(2,1)S(1)}, bf16[3,84,512]{2,1,0:T(8,128)(2,1)}, u32[]{:S(2)}) copy-start(bf16[3,84,512]{2,1,0:T(8,128)(2,1)} %get-tuple-element.114) | copy-start | bytes 774148
  89.5 3.9 %copy-start.8 = (bf16[512,1536]{1,0:T(8,128)(2,1)S(1)}, bf16[512,1536]{1,0:T(8,128)(2,1)}, u32[]{:S(2)}) copy-start(bf16[512,1536]{1,0:T(8,128)(2,1)} %get-tuple-element.119.wq_ref) | copy-start | bytes 4718596
  89.5 3.9 %copy-start.13 = (bf16[512,512]{1,0:T(8,128)(2,1)S(1)}, bf16[512,512]{1,0:T(8,128)(2,1)}, u32[]{:S(2)}) copy-start(bf16[512,512]{1,0:T(8,128)(2,1)} %get-tuple-element.120.wo_ref) | copy-start | bytes 1572868
  89.6 3.8 %copy-start = (f32[3,336,512]{2,1,0:T(8,128)S(1)}, f32[3,336,512]{2,1,0:T(8,128)}, u32[]{:S(2)}) copy-start(f32[3,336,512]{2,1,0:T(8,128)} %get-tuple-element.108.y1_ref) | copy-start | bytes 6193156
  89.6 3.8 %copy-start.6 = (f32[512]{0:T(512)S(1)}, f32[512]{0:T(512)}, u32[]{:S(2)}) copy-start(f32[512]{0:T(512)} %param.18) | copy-start | bytes 6148
  89.6 3.8 %copy-start.7 = (f32[512]{0:T(512)S(1)}, f32[512]{0:T(512)}, u32[]{:S(2)}) copy-start(f32[512]{0:T(512)} %param.23) | copy-start | bytes 6148
  89.7 27.7 %collective-permute-start.17 = (bf16[2,272,512]{2,1,0:T(8,128)(2,1)S(1)}, bf16[2,272,512]{2,1,0:T(8,128)(2,1)S(1)}, u32[]{:S(2)}, u32[]{:S(2)}) collective-permute-start(bf16[2,272,512]{2,1,0:T(8,128)(2,1)S(1)} %constant_dynamic-slice_fusion.3), channel_id=1, source_target_pairs={{0,4},{4,0},{8,12},{12,8},{16,20},{20,16},{24,28},{28,24},{1,5},{5... | collective-permute-start | bytes 1671176 | tf_op jit(solution)/shard_map/ppermute | solution.py:450
  91.2 26.2 %collective-permute-start.16 = (bf16[544,512]{1,0:T(8,128)(2,1)S(1)}, bf16[544,512]{1,0:T(8,128)(2,1)S(1)}, u32[]{:S(2)}, u32[]{:S(2)}) collective-permute-start(bf16[544,512]{1,0:T(8,128)(2,1)S(1)} %slice_bitcast_fusion.1.after_ref), channel_id=1, source_target_pairs={{0,2},{1,3},{2,0},{3,1},{4,6},{5,7},{6,4},{7,5},{8,10},{9,11},{10,... | collective-permute-start | bytes 1671176 | tf_op jit(solution)/shard_map/ppermute | solution.py:450
  91.8 25.7 %collective-permute-start.19 = (bf16[6,84,512]{2,1,0:T(8,128)(2,1)S(1)}, bf16[6,84,512]{2,1,0:T(8,128)(2,1)S(1)}, u32[]{:S(2)}, u32[]{:S(2)}) collective-permute-start(bf16[6,84,512]{2,1,0:T(8,128)(2,1)S(1)} %copy-done.27), channel_id=1, source_target_pairs={{0,2},{1,3},{2,0},{3,1},{4,6},{5,7},{6,4},{7,5},{8,10},{9,11},{10,... | collective-permute-start | bytes 1548296 | tf_op jit(solution)/shard_map/ppermute | solution.py:450
  93.3 22.9 %collective-permute-start.18 = (bf16[3,84,512]{2,1,0:T(8,128)(2,1)S(1)}, bf16[3,84,512]{2,1,0:T(8,128)(2,1)S(1)}, u32[]{:S(2)}, u32[]{:S(2)}) collective-permute-start(bf16[3,84,512]{2,1,0:T(8,128)(2,1)S(1)} %copy-done.31), channel_id=1, source_target_pairs={{0,1},{1,0},{2,3},{3,2},{4,5},{5,4},{6,7},{7,6},{8,9},{9,8},{10,11... | collective-permute-start | bytes 774152 | tf_op jit(solution)/shard_map/ppermute | solution.py:450
  119.4 3.0 %collective-permute-start.21 = (bf16[2,576,512]{2,1,0:T(8,128)(2,1)S(1)}, bf16[2,576,512]{2,1,0:T(8,128)(2,1)}, u32[]{:S(2)}, u32[]{:S(2)}) collective-permute-start(bf16[2,576,512]{2,1,0:T(8,128)(2,1)S(1)} %get-tuple-element.133), channel_id=1, source_target_pairs={{0,1},{1,0},{2,3},{3,2},{4,5},{5,4},{6,7},{7,6},{8,9},{9,8},{10,11... | collective-permute-start | bytes 3538952 | tf_op jit(solution)/shard_map/ppermute | solution.py:450
  119.4 9.6 %collective-permute-start.25 = (bf16[272,512]{1,0:T(8,128)(2,1)}, bf16[272,512]{1,0:T(8,128)(2,1)S(1)}, u32[]{:S(2)}, u32[]{:S(2)}) collective-permute-start(bf16[272,512]{1,0:T(8,128)(2,1)} %slice_bitcast_fusion.5), channel_id=1, source_target_pairs={{0,2},{1,3},{2,0},{3,1},{4,6},{5,7},{6,4},{7,5},{8,10},{9,11},{10,... | collective-permute-start | bytes 835592 | tf_op jit(solution)/shard_map/ppermute | solution.py:450
  120.0 9.1 %collective-permute-start.24 = (bf16[272,512]{1,0:T(8,128)(2,1)}, bf16[272,512]{1,0:T(8,128)(2,1)S(1)}, u32[]{:S(2)}, u32[]{:S(2)}) collective-permute-start(bf16[272,512]{1,0:T(8,128)(2,1)} %constant_dynamic-slice_fusion.2), channel_id=1, source_target_pairs={{0,4},{4,0},{8,12},{12,8},{16,20},{20,16},{24,28},{28,24},{1,5},{5... | collective-permute-start | bytes 835592 | tf_op jit(solution)/shard_map/ppermute | solution.py:450
  121.5 4.9 %collective-permute-start.20 = (bf16[6,84,512]{2,1,0:T(8,128)(2,1)S(1)}, bf16[6,84,512]{2,1,0:T(8,128)(2,1)S(1)}, u32[]{:S(2)}, u32[]{:S(2)}) collective-permute-start(bf16[6,84,512]{2,1,0:T(8,128)(2,1)S(1)} %collective-permute-done.19.b2), channel_id=1, source_target_pairs={{0,1},{1,0},{2,3},{3,2},{4,5},{5,4},{6,7},{7,6},{8,9},{9,8},{10,11... | collective-permute-start | bytes 1548296 | tf_op jit(solution)/shard_map/ppermute | solution.py:450
  124.1 9.9 %collective-permute-start.23 = (bf16[2,144,512]{2,1,0:T(8,128)(2,1)S(1)}, bf16[2,144,512]{2,1,0:T(8,128)(2,1)S(1)}, u32[]{:S(2)}, u32[]{:S(2)}) collective-permute-start(bf16[2,144,512]{2,1,0:T(8,128)(2,1)S(1)} %constant_dynamic-slice_fusion.1), channel_id=1, source_target_pairs={{0,8},{4,12},{8,0},{12,4},{16,24},{20,28},{24,16},{28,20},{1,9},{5... | collective-permute-start | bytes 884744 | tf_op jit(solution)/shard_map/ppermute | solution.py:450
  125.8 3.3 %copy-start.15 = (bf16[2,272,512]{2,1,0:T(8,128)(2,1)S(1)}, bf16[2,272,512]{2,1,0:T(8,128)(2,1)}, u32[]{:S(2)}) copy-start(bf16[2,272,512]{2,1,0:T(8,128)(2,1)} %copy-done.14) | copy-start | bytes 1671172
  125.8 3.3 %copy-start.18 = (bf16[544,512]{1,0:T(8,128)(2,1)S(1)}, bf16[544,512]{1,0:T(8,128)(2,1)}, u32[]{:S(2)}) copy-start(bf16[544,512]{1,0:T(8,128)(2,1)} %copy-done.17) | copy-start | bytes 1671172
  125.8 9.2 %collective-permute-start.22 = (bf16[288,512]{1,0:T(8,128)(2,1)S(1)}, bf16[288,512]{1,0:T(8,128)(2,1)S(1)}, u32[]{:S(2)}, u32[]{:S(2)}) collective-permute-start(bf16[288,512]{1,0:T(8,128)(2,1)S(1)} %slice_bitcast_fusion.3), channel_id=1, source_target_pairs={{0,2},{1,3},{2,0},{3,1},{4,6},{5,7},{6,4},{7,5},{8,10},{9,11},{10,... | collective-permute-start | bytes 884744 | tf_op jit(solution)/shard_map/ppermute | solution.py:450
  129.6 10.4 %collective-permute-start.28 = (bf16[272,512]{1,0:T(8,128)(2,1)S(1)}, bf16[272,512]{1,0:T(8,128)(2,1)S(1)}, u32[]{:S(2)}, u32[]{:S(2)}) collective-permute-start(bf16[272,512]{1,0:T(8,128)(2,1)S(1)} %fusion.5), channel_id=1, source_target_pairs={{0,8},{4,12},{8,0},{12,4},{16,24},{20,28},{24,16},{28,20},{1,9},{5... | collective-permute-start | bytes 835592 | tf_op jit(solution)/shard_map/ppermute | solution.py:450
  135.2 7.9 %copy-start.3 = (bf16[6,84,512]{2,1,0:T(8,128)(2,1)S(1)}, bf16[6,84,512]{2,1,0:T(8,128)(2,1)}, u32[]{:S(2)}) copy-start(bf16[6,84,512]{2,1,0:T(8,128)(2,1)} %copy-done.2) | copy-start | bytes 1548292
  135.2 8.0 %copy-start.5 = (bf16[3,84,512]{2,1,0:T(8,128)(2,1)S(1)}, bf16[3,84,512]{2,1,0:T(8,128)(2,1)}, u32[]{:S(2)}) copy-start(bf16[3,84,512]{2,1,0:T(8,128)(2,1)} %copy-done.4) | copy-start | bytes 774148
  135.2 8.0 %collective-permute-start.27 = (bf16[144,512]{1,0:T(8,128)(2,1)S(1)}, bf16[144,512]{1,0:T(8,128)(2,1)S(1)}, u32[]{:S(2)}, u32[]{:S(2)}) collective-permute-start(bf16[144,512]{1,0:T(8,128)(2,1)S(1)} %slice_bitcast_fusion.7), channel_id=1, source_target_pairs={{0,2},{1,3},{2,0},{3,1},{4,6},{5,7},{6,4},{7,5},{8,10},{9,11},{10,... | collective-permute-start | bytes 442376 | tf_op jit(solution)/shard_map/ppermute | solution.py:450
  135.9 7.3 %collective-permute-start.26 = (bf16[144,512]{1,0:T(8,128)(2,1)S(1)}, bf16[144,512]{1,0:T(8,128)(2,1)S(1)}, u32[]{:S(2)}, u32[]{:S(2)}) collective-permute-start(bf16[144,512]{1,0:T(8,128)(2,1)S(1)} %constant_dynamic-slice_fusion), channel_id=1, source_target_pairs={{0,8},{4,12},{8,0},{12,4},{16,24},{20,28},{24,16},{28,20},{1,9},{5... | collective-permute-start | bytes 442376 | tf_op jit(solution)/shard_map/ppermute | solution.py:450
  140.4 14.0 %collective-permute-start.32 = (bf16[272,512]{1,0:T(8,128)(2,1)S(1)}, bf16[272,512]{1,0:T(8,128)(2,1)S(1)}, u32[]{:S(2)}, u32[]{:S(2)}) collective-permute-start(bf16[272,512]{1,0:T(8,128)(2,1)S(1)} %add_convert_fusion.5), channel_id=1, source_target_pairs={{0,16},{4,20},{8,24},{12,28},{16,0},{20,4},{24,8},{28,12},{1,17},{... | collective-permute-start | bytes 835592 | tf_op jit(solution)/shard_map/ppermute | solution.py:450
  143.0 12.7 %collective-permute-start.31 = (bf16[6,84,512]{2,1,0:T(8,128)(2,1)S(1)}, bf16[6,84,512]{2,1,0:T(8,128)(2,1)S(1)}, u32[]{:S(2)}, u32[]{:S(2)}) collective-permute-start(bf16[6,84,512]{2,1,0:T(8,128)(2,1)S(1)} %copy-done.3), channel_id=1, source_target_pairs={{0,2},{1,3},{2,0},{3,1},{4,6},{5,7},{6,4},{7,5},{8,10},{9,11},{10,... | collective-permute-start | bytes 1548296 | tf_op jit(solution)/shard_map/ppermute | solution.py:450
  143.2 12.5 %collective-permute-start.30 = (bf16[3,84,512]{2,1,0:T(8,128)(2,1)S(1)}, bf16[3,84,512]{2,1,0:T(8,128)(2,1)S(1)}, u32[]{:S(2)}, u32[]{:S(2)}) collective-permute-start(bf16[3,84,512]{2,1,0:T(8,128)(2,1)S(1)} %copy-done.5), channel_id=1, source_target_pairs={{0,1},{1,0},{2,3},{3,2},{4,5},{5,4},{6,7},{7,6},{8,9},{9,8},{10,11... | collective-permute-start | bytes 774152 | tf_op jit(solution)/shard_map/ppermute | solution.py:450
  143.4 12.3 %collective-permute-start.29 = (bf16[144,512]{1,0:T(8,128)(2,1)S(1)}, bf16[144,512]{1,0:T(8,128)(2,1)S(1)}, u32[]{:S(2)}, u32[]{:S(2)}) collective-permute-start(bf16[144,512]{1,0:T(8,128)(2,1)S(1)} %fusion.7), channel_id=1, source_target_pairs={{0,4},{4,0},{8,12},{12,8},{16,20},{20,16},{24,28},{28,24},{1,5},{5... | collective-permute-start | bytes 442376 | tf_op jit(solution)/shard_map/ppermute | solution.py:450
  154.5 5.1 %collective-permute-start.34 = (bf16[136,512]{1,0:T(8,128)(2,1)S(1)}, bf16[136,512]{1,0:T(8,128)(2,1)S(1)}, u32[]{:S(2)}, u32[]{:S(2)}) collective-permute-start(bf16[136,512]{1,0:T(8,128)(2,1)S(1)} %get-tuple-element.216), channel_id=1, source_target_pairs={{0,8},{4,12},{8,0},{12,4},{16,24},{20,28},{24,16},{28,20},{1,9},{5... | collective-permute-start | bytes 417800 | tf_op jit(solution)/shard_map/ppermute | solution.py:450
  155.3 5.3 %collective-permute-start.35 = (bf16[136,512]{1,0:T(8,128)(2,1)S(1)}, bf16[136,512]{1,0:T(8,128)(2,1)S(1)}, u32[]{:S(2)}, u32[]{:S(2)}) collective-permute-start(bf16[136,512]{1,0:T(8,128)(2,1)S(1)} %get-tuple-element.215), channel_id=1, source_target_pairs={{0,4},{4,0},{8,12},{12,8},{16,20},{20,16},{24,28},{28,24},{1,5},{5... | collective-permute-start | bytes 417800 | tf_op jit(solution)/shard_map/ppermute | solution.py:450
  155.9 6.5 %collective-permute-start.33 = (bf16[6,84,512]{2,1,0:T(8,128)(2,1)S(1)}, bf16[6,84,512]{2,1,0:T(8,128)(2,1)S(1)}, u32[]{:S(2)}, u32[]{:S(2)}) collective-permute-start(bf16[6,84,512]{2,1,0:T(8,128)(2,1)S(1)} %collective-permute-done.31.b2), channel_id=1, source_target_pairs={{0,1},{1,0},{2,3},{3,2},{4,5},{5,4},{6,7},{7,6},{8,9},{9,8},{10,11... | collective-permute-start | bytes 1548296 | tf_op jit(solution)/shard_map/ppermute | solution.py:450
  156.0 11.1 %collective-permute-start.36 = (bf16[144,512]{1,0:T(8,128)(2,1)S(1)}, bf16[144,512]{1,0:T(8,128)(2,1)S(1)}, u32[]{:S(2)}, u32[]{:S(2)}) collective-permute-start(bf16[144,512]{1,0:T(8,128)(2,1)S(1)} %add_convert_fusion.8), channel_id=1, source_target_pairs={{0,16},{4,20},{8,24},{12,28},{16,0},{20,4},{24,8},{28,12},{1,17},{... | collective-permute-start | bytes 442376 | tf_op jit(solution)/shard_map/ppermute | solution.py:450
  160.6 9.7 %collective-permute-start.40 = (bf16[2,136,512]{2,1,0:T(8,128)(2,1)S(1)}, bf16[2,136,512]{2,1,0:T(8,128)(2,1)S(1)}, u32[]{:S(2)}, u32[]{:S(2)}) collective-permute-start(bf16[2,136,512]{2,1,0:T(8,128)(2,1)S(1)} %maximum_select_fusion.5), channel_id=1, source_target_pairs={{0,8},{4,12},{8,0},{12,4},{16,24},{20,28},{24,16},{28,20},{1,9},{5... | collective-permute-start | bytes 835592 | tf_op jit(solution)/shard_map/ppermute | solution.py:450
  161.8 8.5 %collective-permute-start.39 = (bf16[2,136,512]{2,1,0:T(8,128)(2,1)S(1)}, bf16[2,136,512]{2,1,0:T(8,128)(2,1)S(1)}, u32[]{:S(2)}, u32[]{:S(2)}) collective-permute-start(bf16[2,136,512]{2,1,0:T(8,128)(2,1)S(1)} %maximum_select_fusion.4), channel_id=1, source_target_pairs={{0,4},{4,0},{8,12},{12,8},{16,20},{20,16},{24,28},{28,24},{1,5},{5... | collective-permute-start | bytes 835592 | tf_op jit(solution)/shard_map/ppermute | solution.py:450
  167.2 5.8 %collective-permute-start.37 = (bf16[72,512]{1,0:T(8,128)(2,1)S(1)}, bf16[72,512]{1,0:T(8,128)(2,1)S(1)}, u32[]{:S(2)}, u32[]{:S(2)}) collective-permute-start(bf16[72,512]{1,0:T(8,128)(2,1)S(1)} %get-tuple-element.222), channel_id=1, source_target_pairs={{0,4},{4,0},{8,12},{12,8},{16,20},{20,16},{24,28},{28,24},{1,5},{5... | collective-permute-start | bytes 221192 | tf_op jit(solution)/shard_map/ppermute | solution.py:450
  168.9 4.4 %collective-permute-start.38 = (bf16[72,512]{1,0:T(8,128)(2,1)S(1)}, bf16[72,512]{1,0:T(8,128)(2,1)S(1)}, u32[]{:S(2)}, u32[]{:S(2)}) collective-permute-start(bf16[72,512]{1,0:T(8,128)(2,1)S(1)} %get-tuple-element.221), channel_id=1, source_target_pairs={{0,8},{4,12},{8,0},{12,4},{16,24},{20,28},{24,16},{28,20},{1,9},{5... | collective-permute-start | bytes 221192 | tf_op jit(solution)/shard_map/ppermute | solution.py:450
  173.2 5.2 %collective-permute-start.41 = (bf16[2,72,512]{2,1,0:T(8,128)(2,1)S(1)}, bf16[2,72,512]{2,1,0:T(8,128)(2,1)S(1)}, u32[]{:S(2)}, u32[]{:S(2)}) collective-permute-start(bf16[2,72,512]{2,1,0:T(8,128)(2,1)S(1)} %maximum_select_fusion.9), channel_id=1, source_target_pairs={{0,8},{4,12},{8,0},{12,4},{16,24},{20,28},{24,16},{28,20},{1,9},{5... | collective-permute-start | bytes 442376 | tf_op jit(solution)/shard_map/ppermute | solution.py:450
  174.7 5.2 %collective-permute-start.42 = (bf16[2,72,512]{2,1,0:T(8,128)(2,1)S(1)}, bf16[2,72,512]{2,1,0:T(8,128)(2,1)S(1)}, u32[]{:S(2)}, u32[]{:S(2)}) collective-permute-start(bf16[2,72,512]{2,1,0:T(8,128)(2,1)S(1)} %maximum_select_fusion.11), channel_id=1, source_target_pairs={{0,4},{4,0},{8,12},{12,8},{16,20},{20,16},{24,28},{28,24},{1,5},{5... | collective-permute-start | bytes 442376 | tf_op jit(solution)/shard_map/ppermute | solution.py:450
  (17 other events, 31.2 us)

commit v5 on v4

--- a/solution.py
+++ b/solution.py
@@ -139,7 +139,9 @@
         pitch = half + 16
         for k, w in enumerate((w0, w1, w2, w3)):
             for h in range(2):
-                wq_ref[pl.ds(h * half, half), pl.ds(384 * k, 384)] = w[pl.ds(h * pitch, half), 0:384]
+                q_cols = w[pl.ds(h * pitch, half), 0:128].astype(F32) * (HD ** -0.5)
+                wq_ref[pl.ds(h * half, half), pl.ds(384 * k, 128)] = q_cols.astype(BF16)
+                wq_ref[pl.ds(h * half, half), pl.ds(384 * k + 128, 256)] = w[pl.ds(h * pitch, half), 128:384]
                 for j in range(half // 128):
                     wo_ref[pl.ds(128 * k, 128), pl.ds(h * half + 128 * j, 128)] = w[pl.ds(h * pitch + 128 * j, 128), 384:512]
             ub = w[half:pitch, :].astype(F32)
@@ -168,7 +170,7 @@
             mine = (lane < HD) if h == 0 else (lane >= HD)
             kh = jnp.where(mine, k, jnp.zeros_like(k))
             vh = jnp.where(mine, v, jnp.zeros_like(v))
-            st = dot(kh, q, NT) * (HD ** -0.5) + bias_sc[...]
+            st = dot(kh, q, NT) + bias_sc[...]
             e = jnp.exp(st - jnp.max(st, axis=0, keepdims=True))
             prob = (e * (1.0 / jnp.sum(e, axis=0, keepdims=True))).astype(BF16)
             p_ref[0, 2 * p + h] = prob
@@ -307,7 +309,7 @@
             anys],
         scratch=[pltpu.VMEM((4, 2, d, d), BF16), pltpu.SemaphoreType.DMA((4, 4)), pltpu.SemaphoreType.DMA((4,)),
                  pltpu.VMEM((4, length // 4, d), F32), pltpu.VMEM((length, d), F32)],
-        flops=16 * total * d * d, name="feed_forward", vmem=56 << 20)
+        flops=16 * total * d * d, name="feed_forward", vmem=50 << 20)
 
 
 def attn_bwd_kernel(me_ref, du_ref, gm_ref, y1_ref, x_ref, g1_ref, g2_ref, w_ref, wq_ref, wo_ref, qkv_ref, p_ref,
@@ -335,7 +337,6 @@
     sums = [jnp.sum(v, axis=0, keepdims=True) for v in (da2 * hat, da2, ga.astype(F32), gy)]
     do_sc[...] = dot(ga, wo_ref[...], NT).astype(BF16)
     lane = lax.broadcasted_iota(jnp.int32, (length, 128), 1)
-    scale = HD ** -0.5
     cut = min(256, length)
     for p in range(4):
         q = qkv_ref[0, :, pl.ds(p * 384, 128)]
@@ -356,9 +357,9 @@
             pv = dot(prob[:cut], doh), dot(prob[cut:, cut:], doh[cut:])
             parts = (pq, pk, pv)
             total = parts if h == 0 else [[b + c for b, c in zip(*pair)] for pair in zip(total, parts)]
-        for n, (kind, factor) in enumerate(zip(total, (scale, scale, 1.0))):
+        for n, kind in enumerate(total):
             for rows, value in zip((pl.ds(0, cut), pl.ds(cut, length - cut)), kind):
-                dqkv_ref[0, rows, pl.ds(p * 384 + 128 * n, 128)] = (value * factor).astype(BF16)
+                dqkv_ref[0, rows, pl.ds(p * 384 + 128 * n, 128)] = value.astype(BF16)
 
     da1 = dot(dqkv_ref[0], wq_ref[...], NT)
     hat, inv = stats(x_ref[0].astype(F32))
@@ -380,7 +381,9 @@
         extra = jnp.concatenate([small_ref[...], jnp.zeros((56, d), F32)], axis=0).astype(BF16)
         for k in range(4):
             ref = send_ref if k % 2 else keep_ref
-            ref[k // 2, 0:384] = dot(dqkv_sc[:, pl.ds(384 * k, 384)], a1_ref[...].reshape(total, d), TN).astype(BF16)
+            grad = dot(dqkv_sc[:, pl.ds(384 * k, 384)], a1_ref[...].reshape(total, d), TN)
+            ref[k // 2, 0:128] = (grad[0:128] * (HD ** -0.5)).astype(BF16)
+            ref[k // 2, 128:384] = grad[128:384].astype(BF16)
             ref[k // 2, 384:512] = dot(o_ref[:, :, pl.ds(128 * k, 128)].reshape(total, 128), ga_sc[...], TN).astype(BF16)
             ref[k // 2, 512:576] = extra
 

time: 183 us -> 183 us (level)
    unnamed x77 -> x63, local copies, waits for them, and re-layouts: 3.41 us -> 4.52 us
where the time goes in v5:
time: 183 us
  Pallas kernels  67.2 us (37%)
  waiting for transfers between devices  56 us (31%)
  starting transfers between devices  41.4 us (23%)
  local copies, waits for them, and re-layouts  11 us (6%)
  other arithmetic  5.27 us (3%)
  between operations  2.08 us (1%)
    pallas_call x7, Pallas kernels, call(): pl.pallas_call(kernel, grid_spec=pltpu.PrefetchScalarGridSpec(num_scalar_...  67.2 us
    ppermute x43, waiting for transfers between devices, hop(): return lax.ppermute(value, axis, [(i, i ^ bit) for i in range(n)])  56 us
    ppermute x43, starting transfers between devices, hop(): return lax.ppermute(value, axis, [(i, i ^ bit) for i in range(n)])  41.4 us
    unnamed x63, local copies, waits for them, and re-layouts  4.52 us
  transfers between devices with their start and end apart: 43, of which 20 were waited for; matrix products, arithmetic and copies ran while one was open for 4% of the time, Pallas kernels for 26%

profile of v5, /device:TPU:0, one launch (start us, length us, event | category | flops | bytes accessed | tf_op | source)
XLA Modules:
  0.0 182.9 jit_solution(4082189904755745829)
XLA Ops:
  0.7 3.1 %pack_weights.1 = (bf16[1568,512]{1,0:T(8,128)(2,1)}, bf16[800,512]{1,0:T(8,128)(2,1)}) custom-call(s32[1]{0:T(128)} %bitcast.1.y_ref, s32[1]{0:T(128)} %bitcast.2.z_ref, bf16[512,384]{1,0:T(8,128)(2,1)} %wqkv_ref.1, bf16[128,512]{1,0:T(8,128)(2,1)} %wout_ref.1, f32[1,512]{1,0:T(1,128)} %bitcast.122, bf16[512,512]{1,0:T(8,128)(2,1)} %up_ref.1, ...), custom_call_target="tpu_custom_call" | custom-call | bytes 3999744 | tf_op jit(solution)/shard_map/pack_weights/pallas_call | solution.py:56
  3.8 0.5 collective-permute-start
  4.2 2.5 %collective-permute-start.1 = (bf16[800,512]{1,0:T(8,128)(2,1)}, bf16[800,512]{1,0:T(8,128)(2,1)S(1)}, u32[]{:S(2)}, u32[]{:S(2)}) collective-permute-start(bf16[800,512]{1,0:T(8,128)(2,1)} %get-tuple-element.92), channel_id=1, source_target_pairs={{0,2},{1,3},{2,0},{3,1},{4,6},{5,7},{6,4},{7,5},{8,10},{9,11},{10,... | collective-permute-start | bytes 2457608 | tf_op jit(solution)/shard_map/ppermute | solution.py:453
  6.7 0.8 collective-permute-done.w1
  7.5 0.9 dynamic-slice_bitcast_fusion.1
  8.8 2.9 %collective-permute-start.2 = (bf16[6,84,512]{2,1,0:T(8,128)(2,1)S(1)}, bf16[6,84,512]{2,1,0:T(8,128)(2,1)S(1)}, u32[]{:S(2)}, u32[]{:S(2)}) collective-permute-start(bf16[6,84,512]{2,1,0:T(8,128)(2,1)S(1)} %pad_maximum_fusion.2), channel_id=1, source_target_pairs={{0,2},{1,3},{2,0},{3,1},{4,6},{5,7},{6,4},{7,5},{8,10},{9,11},{10,... | collective-permute-start | bytes 1548296 | tf_op jit(solution)/shard_map/ppermute | solution.py:453
  11.8 0.5 collective-permute-start.3
  12.4 13.7 %collective-permute-done.1.w2.a2_ = bf16[800,512]{1,0:T(8,128)(2,1)S(1)} collective-permute-done((bf16[800,512]{1,0:T(8,128)(2,1)}, bf16[800,512]{1,0:T(8,128)(2,1)S(1)}, u32[]{:S(2)}, u32[]{:S(2)}) %collective-permute-start.1) | collective-permute-done | bytes 819232 | tf_op jit(solution)/shard_map/ppermute | solution.py:453
  26.1 11.4 %collective-permute-done.2.t2 = bf16[6,84,512]{2,1,0:T(8,128)(2,1)S(1)} collective-permute-done((bf16[6,84,512]{2,1,0:T(8,128)(2,1)S(1)}, bf16[6,84,512]{2,1,0:T(8,128)(2,1)S(1)}, u32[]{:S(2)}, u32[]{:S(2)}) %collective-permute-start.2) | collective-permute-done | bytes 516128 | tf_op jit(solution)/shard_map/ppermute | solution.py:453
  37.4 0.5 collective-permute-start.9
  38.0 1.7 collective-permute-start.13
  39.7 1.6 collective-permute-start.5
  41.4 1.5 collective-permute-start.6
  43.7 0.5 copy-done.25
  44.2 15.8 %attention_forward.1 = (bf16[3,336,1536]{2,1,0:T(8,128)(2,1)}, bf16[3,8,336,336]{3,2,1,0:T(8,128)(2,1)}, bf16[3,336,512]{2,1,0:T(8,128)(2,1)}, bf16[3,336,512]{2...) custom-call(s32[1]{0:T(128)} %bitcast.me_ref, ...), custom_call_target="tpu_custom_call" | custom-call | flops 2807562240 | bytes 23279616 | tf_op jit(solution)/shard_map/attention_forward/pallas_call | solution.py:56
  60.2 0.5 collective-permute-start.10
  61.9 0.6 collective-permute-done.10.b3_
  63.2 1.1 copy-done.3
  64.3 0.8 copy-done.16
  65.2 16.8 %feed_forward.1 = (bf16[1008,2048]{1,0:T(8,128)(2,1)}, bf16[1008,2048]{1,0:T(8,128)(2,1)}, bf16[3,336,512]{2,1,0:T(8,128)(2,1)}, bf16[2,1088,512]{2,1,0:T(8,128)...) custom-call(s32[1]{0:T(128)} %bitcast.me_ref, s32[1]{0:T(128)} %bitcast.1.y_ref, s32[1]{0:T(128)} %bitcast.2.z_ref, ...), custom_call_target="tpu_custom_call" | custom-call | flops 4227858432 | bytes 27009024 | tf_op jit(solution)/shard_map/feed_forward/pallas_call | solution.py:56
  82.2 6.6 %block_output.1 = (bf16[3,84,512]{2,1,0:T(8,128)(2,1)}, bf16[3,84,512]{2,1,0:T(8,128)(2,1)}, bf16[6,84,512]{2,1,0:T(8,128)(2,1)}) custom-call(s32[1]{0:T(128)} %bitcast.me_ref, s32[1]{0:T(128)S(6)} %copy.32.count_ref, bf16[1008,2048]{1,0:T(8,128)(2,1)} %get-tuple-element.106.hm_ref, bf16[4,2,512,512]{3,2,1,0:T(8,128)(2,1)} %get-tuple-element.107.w_ref, ...), custom_call_target="tpu_custom_call" | custom-call | flops 2113929216 | bytes 12453888 | tf_op jit(solution)/shard_map/block_output/pallas_call | solution.py:56
  88.9 0.6 add_convert_fusion
  89.8 1.5 collective-permute-start.17
  91.3 0.5 collective-permute-start.16
  91.9 1.5 collective-permute-start.19
  93.4 22.8 %attention_backward.1 = (bf16[3,84,512]{2,1,0:T(8,128)(2,1)S(1)}, bf16[3,84,512]{2,1,0:T(8,128)(2,1)S(1)}, bf16[6,84,512]{2,1,0:T(8,128)(2,1)S(1)}, bf16[2,576,5...) custom-call(s32[1]{0:T(128)} %bitcast.me_ref, bf16[1008,2048]{1,0:T(8,128)(2,1)} %get-tuple-element.116.du_ref, ...), custom_call_target="tpu_custom_call" | custom-call | flops 8422686720 | bytes 29081600 | tf_op jit(solution)/shard_map/attention_backward/pallas_call | solution.py:56
  116.3 1.3 collective-permute-done.19.b2
  117.7 0.8 slice_bitcast_fusion.5
  118.6 0.8 constant_dynamic-slice_fusion.2
  119.5 0.5 collective-permute-start.25
  120.1 1.5 collective-permute-start.24
  121.6 0.9 collective-permute-done.21
  122.5 1.6 add_convert_fusion.1
  124.2 1.6 collective-permute-start.23
  125.9 0.6 collective-permute-start.22
  126.5 1.1 place.2
  127.5 1.7 collective-permute-done.25
  129.8 1.6 collective-permute-start.28
  131.4 2.7 %collective-permute-done.23 = bf16[2,144,512]{2,1,0:T(8,128)(2,1)S(1)} collective-permute-done((bf16[2,144,512]{2,1,0:T(8,128)(2,1)S(1)}, bf16[2,144,512]{2,1,0:T(8,128)(2,1)S(1)}, u32[]{:S(2)}, u32[]{:S(2)}) %collective-permute-start.23) | collective-permute-done | bytes 294944 | tf_op jit(solution)/shard_map/ppermute | solution.py:453
  134.1 1.0 collective-permute-done.22
  135.3 0.6 collective-permute-start.27
  136.0 1.6 collective-permute-start.26
  137.6 2.5 %collective-permute-done.28 = bf16[272,512]{1,0:T(8,128)(2,1)S(1)} collective-permute-done((bf16[272,512]{1,0:T(8,128)(2,1)S(1)}, bf16[272,512]{1,0:T(8,128)(2,1)S(1)}, u32[]{:S(2)}, u32[]{:S(2)}) %collective-permute-start.28) | collective-permute-done | bytes 278560 | tf_op jit(solution)/shard_map/ppermute | solution.py:453
  140.5 2.6 %collective-permute-start.32 = (bf16[272,512]{1,0:T(8,128)(2,1)S(1)}, bf16[272,512]{1,0:T(8,128)(2,1)S(1)}, u32[]{:S(2)}, u32[]{:S(2)}) collective-permute-start(bf16[272,512]{1,0:T(8,128)(2,1)S(1)} %add_convert_fusion.5), channel_id=1, source_target_pairs={{0,16},{4,20},{8,24},{12,28},{16,0},{20,4},{24,8},{28,12},{1,17},{... | collective-permute-start | bytes 835592 | tf_op jit(solution)/shard_map/ppermute | solution.py:453
  143.5 2.0 %collective-permute-start.29 = (bf16[144,512]{1,0:T(8,128)(2,1)S(1)}, bf16[144,512]{1,0:T(8,128)(2,1)S(1)}, u32[]{:S(2)}, u32[]{:S(2)}) collective-permute-start(bf16[144,512]{1,0:T(8,128)(2,1)S(1)} %fusion.7), channel_id=1, source_target_pairs={{0,4},{4,0},{8,12},{12,8},{16,20},{20,16},{24,28},{28,24},{1,5},{5... | collective-permute-start | bytes 442376 | tf_op jit(solution)/shard_map/ppermute | solution.py:453
  145.5 8.9 %collective-permute-done.32 = bf16[272,512]{1,0:T(8,128)(2,1)S(1)} collective-permute-done((bf16[272,512]{1,0:T(8,128)(2,1)S(1)}, bf16[272,512]{1,0:T(8,128)(2,1)S(1)}, u32[]{:S(2)}, u32[]{:S(2)}) %collective-permute-start.32) | collective-permute-done | bytes 278560 | tf_op jit(solution)/shard_map/ppermute | solution.py:453
  154.6 0.7 collective-permute-start.34
  156.1 3.4 %collective-permute-start.36 = (bf16[144,512]{1,0:T(8,128)(2,1)S(1)}, bf16[144,512]{1,0:T(8,128)(2,1)S(1)}, u32[]{:S(2)}, u32[]{:S(2)}) collective-permute-start(bf16[144,512]{1,0:T(8,128)(2,1)S(1)} %add_convert_fusion.8), channel_id=1, source_target_pairs={{0,16},{4,20},{8,24},{12,28},{16,0},{20,4},{24,8},{28,12},{1,17},{... | collective-permute-start | bytes 442376 | tf_op jit(solution)/shard_map/ppermute | solution.py:453
  159.7 0.9 collective-permute-done.35
  160.7 1.2 collective-permute-start.40
  161.9 0.5 collective-permute-start.39
  162.4 1.1 place.3
  163.5 3.7 %collective-permute-done.36 = bf16[144,512]{1,0:T(8,128)(2,1)S(1)} collective-permute-done((bf16[144,512]{1,0:T(8,128)(2,1)S(1)}, bf16[144,512]{1,0:T(8,128)(2,1)S(1)}, u32[]{:S(2)}, u32[]{:S(2)}) %collective-permute-start.36) | collective-permute-done | bytes 147488 | tf_op jit(solution)/shard_map/ppermute | solution.py:453
  167.3 1.7 collective-permute-start.37
  168.9 1.4 collective-permute-done.40
  171.0 1.5 fusion.8
  172.5 0.6 slice.122
  173.3 1.4 collective-permute-start.41
  174.8 1.9 %collective-permute-start.42 = (bf16[2,72,512]{2,1,0:T(8,128)(2,1)S(1)}, bf16[2,72,512]{2,1,0:T(8,128)(2,1)S(1)}, u32[]{:S(2)}, u32[]{:S(2)}) collective-permute-start(bf16[2,72,512]{2,1,0:T(8,128)(2,1)S(1)} %maximum_select_fusion.11), channel_id=1, source_target_pairs={{0,4},{4,0},{8,12},{12,8},{16,20},{20,16},{24,28},{28,24},{1,5},{5... | collective-permute-start | bytes 442376 | tf_op jit(solution)/shard_map/ppermute | solution.py:453
  176.7 1.8 %collective-permute-done.41 = bf16[2,72,512]{2,1,0:T(8,128)(2,1)S(1)} collective-permute-done((bf16[2,72,512]{2,1,0:T(8,128)(2,1)S(1)}, bf16[2,72,512]{2,1,0:T(8,128)(2,1)S(1)}, u32[]{:S(2)}, u32[]{:S(2)}) %collective-permute-start.41) | collective-permute-done | bytes 147488 | tf_op jit(solution)/shard_map/ppermute | solution.py:453
  178.6 1.4 collective-permute-done.42
  180.3 0.7 slice.119
  181.0 0.6 fusion.9
  181.7 1.2 copy.31
  (146 shorter events, 7.6 us)
Async XLA Ops:
  0.6 6.9 %copy-start.22 = (bf16[84,12,512]{2,0,1:T(8,128)(2,1)S(1)}, bf16[84,12,512]{2,0,1:T(8,128)(2,1)}, u32[]{:S(2)}) copy-start(bf16[84,12,512]{2,0,1:T(8,128)(2,1)} %param.15) | copy-start | bytes 3096580
  3.8 3.7 %collective-permute-start = (bf16[1568,512]{1,0:T(8,128)(2,1)}, bf16[1568,512]{1,0:T(8,128)(2,1)S(1)}, u32[]{:S(2)}, u32[]{:S(2)}) collective-permute-start(bf16[1568,512]{1,0:T(8,128)(2,1)} %get-tuple-element.91.w0), channel_id=1, source_target_pairs={{0,1},{1,0},{2,3},{3,2},{4,5},{5,4},{6,7},{7,6},{8,9},{9,8},{10,11... | collective-permute-start | bytes 4816904 | tf_op jit(solution)/shard_map/ppermute | solution.py:453
  4.2 21.8 %collective-permute-start.1 = (bf16[800,512]{1,0:T(8,128)(2,1)}, bf16[800,512]{1,0:T(8,128)(2,1)S(1)}, u32[]{:S(2)}, u32[]{:S(2)}) collective-permute-start(bf16[800,512]{1,0:T(8,128)(2,1)} %get-tuple-element.92), channel_id=1, source_target_pairs={{0,2},{1,3},{2,0},{3,1},{4,6},{5,7},{6,4},{7,5},{8,10},{9,11},{10,... | collective-permute-start | bytes 2457608 | tf_op jit(solution)/shard_map/ppermute | solution.py:453
  6.7 4.9 %copy-start.23 = (bf16[84,12,512]{2,0,1:T(8,128)(2,1)S(1)}, bf16[84,12,512]{2,0,1:T(8,128)(2,1)}, u32[]{:S(2)}) copy-start(bf16[84,12,512]{2,0,1:T(8,128)(2,1)} %param.29) | copy-start | bytes 3096580
  8.8 28.6 %collective-permute-start.2 = (bf16[6,84,512]{2,1,0:T(8,128)(2,1)S(1)}, bf16[6,84,512]{2,1,0:T(8,128)(2,1)S(1)}, u32[]{:S(2)}, u32[]{:S(2)}) collective-permute-start(bf16[6,84,512]{2,1,0:T(8,128)(2,1)S(1)} %pad_maximum_fusion.2), channel_id=1, source_target_pairs={{0,2},{1,3},{2,0},{3,1},{4,6},{5,7},{6,4},{7,5},{8,10},{9,11},{10,... | collective-permute-start | bytes 1548296 | tf_op jit(solution)/shard_map/ppermute | solution.py:453
  11.7 14.3 %collective-permute-start.4 = (bf16[3,84,512]{2,1,0:T(8,128)(2,1)S(1)}, bf16[3,84,512]{2,1,0:T(8,128)(2,1)S(1)}, u32[]{:S(2)}, u32[]{:S(2)}) collective-permute-start(bf16[3,84,512]{2,1,0:T(8,128)(2,1)S(1)} %get-tuple-element.204), channel_id=1, source_target_pairs={{0,1},{1,0},{2,3},{3,2},{4,5},{5,4},{6,7},{7,6},{8,9},{9,8},{10,11... | collective-permute-start | bytes 774152 | tf_op jit(solution)/shard_map/ppermute | solution.py:453
  11.8 14.2 %collective-permute-start.3 = (bf16[3,84,512]{2,1,0:T(8,128)(2,1)S(1)}, bf16[3,84,512]{2,1,0:T(8,128)(2,1)S(1)}, u32[]{:S(2)}, u32[]{:S(2)}) collective-permute-start(bf16[3,84,512]{2,1,0:T(8,128)(2,1)S(1)} %get-tuple-element.208), channel_id=1, source_target_pairs={{0,1},{1,0},{2,3},{3,2},{4,5},{5,4},{6,7},{7,6},{8,9},{9,8},{10,11... | collective-permute-start | bytes 774152 | tf_op jit(solution)/shard_map/ppermute | solution.py:453
  26.0 17.3 %copy-start.2 = (bf16[800,512]{1,0:T(8,128)(2,1)}, bf16[800,512]{1,0:T(8,128)(2,1)S(1)}, u32[]{:S(2)}) copy-start(bf16[800,512]{1,0:T(8,128)(2,1)S(1)} %collective-permute-done.1.w2.a2_) | copy-start | bytes 2457604
  26.0 17.3 %copy-start.29 = (bf16[3,84,512]{2,1,0:T(8,128)(2,1)}, bf16[3,84,512]{2,1,0:T(8,128)(2,1)S(1)}, u32[]{:S(2)}) copy-start(bf16[3,84,512]{2,1,0:T(8,128)(2,1)S(1)} %collective-permute-done.3.t1) | copy-start | bytes 774148
  37.4 5.9 %copy-start.26 = (bf16[6,84,512]{2,1,0:T(8,128)(2,1)}, bf16[6,84,512]{2,1,0:T(8,128)(2,1)S(1)}, u32[]{:S(2)}) copy-start(bf16[6,84,512]{2,1,0:T(8,128)(2,1)S(1)} %collective-permute-done.2.t2) | copy-start | bytes 1548292
  37.4 5.9 %collective-permute-start.8 = (bf16[800,512]{1,0:T(8,128)(2,1)S(1)}, bf16[800,512]{1,0:T(8,128)(2,1)S(1)}, u32[]{:S(2)}, u32[]{:S(2)}) collective-permute-start(bf16[800,512]{1,0:T(8,128)(2,1)S(1)} %collective-permute-done.1.w2.a2_), channel_id=1, source_target_pairs={{0,1},{1,0},{2,3},{3,2},{4,5},{5,4},{6,7},{7,6},{8,9},{9,8},{10,11... | collective-permute-start | bytes 2457608 | tf_op jit(solution)/shard_map/ppermute | solution.py:453
  37.4 5.4 %collective-permute-start.9 = (bf16[6,84,512]{2,1,0:T(8,128)(2,1)S(1)}, bf16[6,84,512]{2,1,0:T(8,128)(2,1)S(1)}, u32[]{:S(2)}, u32[]{:S(2)}) collective-permute-start(bf16[6,84,512]{2,1,0:T(8,128)(2,1)S(1)} %collective-permute-done.2.t2), channel_id=1, source_target_pairs={{0,1},{1,0},{2,3},{3,2},{4,5},{5,4},{6,7},{7,6},{8,9},{9,8},{10,11... | collective-permute-start | bytes 1548296 | tf_op jit(solution)/shard_map/ppermute | solution.py:453
  38.0 22.1 %collective-permute-start.13 = (bf16[6,84,512]{2,1,0:T(8,128)(2,1)S(1)}, bf16[6,84,512]{2,1,0:T(8,128)(2,1)S(1)}, u32[]{:S(2)}, u32[]{:S(2)}) collective-permute-start(bf16[6,84,512]{2,1,0:T(8,128)(2,1)S(1)} %pad_maximum_fusion.3), channel_id=1, source_target_pairs={{0,2},{1,3},{2,0},{3,1},{4,6},{5,7},{6,4},{7,5},{8,10},{9,11},{10,... | collective-permute-start | bytes 1548296 | tf_op jit(solution)/shard_map/ppermute | solution.py:453
  39.7 20.4 %collective-permute-start.5 = (bf16[256,512]{1,0:T(8,128)(2,1)S(1)}, bf16[256,512]{1,0:T(8,128)(2,1)S(1)}, u32[]{:S(2)}, u32[]{:S(2)}) collective-permute-start(bf16[256,512]{1,0:T(8,128)(2,1)S(1)} %slice.78), channel_id=1, source_target_pairs={{0,8},{4,12},{8,0},{12,4},{16,24},{20,28},{24,16},{28,20},{1,9},{5... | collective-permute-start | bytes 786440 | tf_op jit(solution)/shard_map/ppermute | solution.py:453
  41.4 18.8 %collective-permute-start.6 = (bf16[256,512]{1,0:T(8,128)(2,1)S(1)}, bf16[256,512]{1,0:T(8,128)(2,1)S(1)}, u32[]{:S(2)}, u32[]{:S(2)}) collective-permute-start(bf16[256,512]{1,0:T(8,128)(2,1)S(1)} %slice.78), channel_id=1, source_target_pairs={{0,4},{4,0},{8,12},{12,8},{16,20},{20,16},{24,28},{28,24},{1,5},{5... | collective-permute-start | bytes 786440 | tf_op jit(solution)/shard_map/ppermute | solution.py:453
  42.9 17.3 %collective-permute-start.7 = (bf16[256,512]{1,0:T(8,128)(2,1)S(1)}, bf16[256,512]{1,0:T(8,128)(2,1)S(1)}, u32[]{:S(2)}, u32[]{:S(2)}) collective-permute-start(bf16[256,512]{1,0:T(8,128)(2,1)S(1)} %slice.78), channel_id=1, source_target_pairs={{0,12},{4,8},{8,4},{12,0},{16,28},{20,24},{24,20},{28,16},{1,13},{... | collective-permute-start | bytes 786440 | tf_op jit(solution)/shard_map/ppermute | solution.py:453
  60.0 3.1 %collective-permute-start.14 = (bf16[6,84,512]{2,1,0:T(8,128)(2,1)S(1)}, bf16[6,84,512]{2,1,0:T(8,128)(2,1)S(1)}, u32[]{:S(2)}, u32[]{:S(2)}) collective-permute-start(bf16[6,84,512]{2,1,0:T(8,128)(2,1)S(1)} %collective-permute-done.13.c2), channel_id=1, source_target_pairs={{0,1},{1,0},{2,3},{3,2},{4,5},{5,4},{6,7},{7,6},{8,9},{9,8},{10,11... | collective-permute-start | bytes 1548296 | tf_op jit(solution)/shard_map/ppermute | solution.py:453
  60.2 2.3 %collective-permute-start.10 = (bf16[256,512]{1,0:T(8,128)(2,1)S(1)}, bf16[256,512]{1,0:T(8,128)(2,1)S(1)}, u32[]{:S(2)}, u32[]{:S(2)}) collective-permute-start(bf16[256,512]{1,0:T(8,128)(2,1)S(1)} %collective-permute-done.5.b2_), channel_id=1, source_target_pairs={{0,1},{1,0},{2,3},{3,2},{4,5},{5,4},{6,7},{7,6},{8,9},{9,8},{10,11... | collective-permute-start | bytes 786440 | tf_op jit(solution)/shard_map/ppermute | solution.py:453
  60.7 2.1 %collective-permute-start.11 = (bf16[256,512]{1,0:T(8,128)(2,1)S(1)}, bf16[256,512]{1,0:T(8,128)(2,1)S(1)}, u32[]{:S(2)}, u32[]{:S(2)}) collective-permute-start(bf16[256,512]{1,0:T(8,128)(2,1)S(1)} %collective-permute-done.6.c2_), channel_id=1, source_target_pairs={{0,1},{1,0},{2,3},{3,2},{4,5},{5,4},{6,7},{7,6},{8,9},{9,8},{10,11... | collective-permute-start | bytes 786440 | tf_op jit(solution)/shard_map/ppermute | solution.py:453
  60.8 2.4 %collective-permute-start.12 = (bf16[256,512]{1,0:T(8,128)(2,1)S(1)}, bf16[256,512]{1,0:T(8,128)(2,1)S(1)}, u32[]{:S(2)}, u32[]{:S(2)}) collective-permute-start(bf16[256,512]{1,0:T(8,128)(2,1)S(1)} %collective-permute-done.7.d2_), channel_id=1, source_target_pairs={{0,1},{1,0},{2,3},{3,2},{4,5},{5,4},{6,7},{7,6},{8,9},{9,8},{10,11... | collective-permute-start | bytes 786440 | tf_op jit(solution)/shard_map/ppermute | solution.py:453
  82.0 6.9 %collective-permute-start.15 = (bf16[2,1088,512]{2,1,0:T(8,128)(2,1)}, bf16[2,1088,512]{2,1,0:T(8,128)(2,1)S(1)}, u32[]{:S(2)}, u32[]{:S(2)}) collective-permute-start(bf16[2,1088,512]{2,1,0:T(8,128)(2,1)} %get-tuple-element.105), channel_id=1, source_target_pairs={{0,1},{1,0},{2,3},{3,2},{4,5},{5,4},{6,7},{7,6},{8,9},{9,8},{10,11... | collective-permute-start | bytes 6684680 | tf_op jit(solution)/shard_map/ppermute | solution.py:453
  82.2 6.7 %copy-start.19 = (bf16[2,1088,512]{2,1,0:T(8,128)(2,1)S(1)}, bf16[2,1088,512]{2,1,0:T(8,128)(2,1)}, u32[]{:S(2)}) copy-start(bf16[2,1088,512]{2,1,0:T(8,128)(2,1)} %get-tuple-element.104) | copy-start | bytes 6684676
  88.8 3.0 %copy-start.27 = (bf16[6,84,512]{2,1,0:T(8,128)(2,1)S(1)}, bf16[6,84,512]{2,1,0:T(8,128)(2,1)}, u32[]{:S(2)}) copy-start(bf16[6,84,512]{2,1,0:T(8,128)(2,1)} %get-tuple-element.115) | copy-start | bytes 1548292
  88.8 4.5 %copy-start.11 = (bf16[3,336,512]{2,1,0:T(8,128)(2,1)S(1)}, bf16[3,336,512]{2,1,0:T(8,128)(2,1)}, u32[]{:S(2)}) copy-start(bf16[3,336,512]{2,1,0:T(8,128)(2,1)} %get-tuple-element.124.o_ref) | copy-start | bytes 3096580
  88.9 4.5 %copy-start.12 = (bf16[3,336,512]{2,1,0:T(8,128)(2,1)S(1)}, bf16[3,336,512]{2,1,0:T(8,128)(2,1)}, u32[]{:S(2)}) copy-start(bf16[3,336,512]{2,1,0:T(8,128)(2,1)} %get-tuple-element.118.x_ref) | copy-start | bytes 3096580
  88.9 4.5 %copy-start.13 = (bf16[3,336,512]{2,1,0:T(8,128)(2,1)S(1)}, bf16[3,336,512]{2,1,0:T(8,128)(2,1)}, u32[]{:S(2)}) copy-start(bf16[3,336,512]{2,1,0:T(8,128)(2,1)} %get-tuple-element.123.a1_ref) | copy-start | bytes 3096580
  88.9 4.5 %copy-start.14 = (bf16[3,336,512]{2,1,0:T(8,128)(2,1)S(1)}, bf16[3,336,512]{2,1,0:T(8,128)(2,1)}, u32[]{:S(2)}) copy-start(bf16[3,336,512]{2,1,0:T(8,128)(2,1)} %get-tuple-element.117.gm_ref) | copy-start | bytes 3096580
  89.5 3.8 %copy-start.30 = (bf16[3,84,512]{2,1,0:T(8,128)(2,1)S(1)}, bf16[3,84,512]{2,1,0:T(8,128)(2,1)}, u32[]{:S(2)}) copy-start(bf16[3,84,512]{2,1,0:T(8,128)(2,1)} %get-tuple-element.114) | copy-start | bytes 774148
  89.5 3.9 %copy-start.10 = (bf16[512,1536]{1,0:T(8,128)(2,1)S(1)}, bf16[512,1536]{1,0:T(8,128)(2,1)}, u32[]{:S(2)}) copy-start(bf16[512,1536]{1,0:T(8,128)(2,1)} %get-tuple-element.119.wq_ref) | copy-start | bytes 4718596
  89.6 3.9 %copy-start.15 = (bf16[512,512]{1,0:T(8,128)(2,1)S(1)}, bf16[512,512]{1,0:T(8,128)(2,1)}, u32[]{:S(2)}) copy-start(bf16[512,512]{1,0:T(8,128)(2,1)} %get-tuple-element.120.wo_ref) | copy-start | bytes 1572868
  89.6 3.8 %copy-start = (f32[3,336,512]{2,1,0:T(8,128)S(1)}, f32[3,336,512]{2,1,0:T(8,128)}, u32[]{:S(2)}) copy-start(f32[3,336,512]{2,1,0:T(8,128)} %get-tuple-element.108.y1_ref) | copy-start | bytes 6193156
  89.7 3.8 %copy-start.8 = (f32[512]{0:T(512)S(1)}, f32[512]{0:T(512)}, u32[]{:S(2)}) copy-start(f32[512]{0:T(512)} %param.18) | copy-start | bytes 6148
  89.7 3.8 %copy-start.9 = (f32[512]{0:T(512)S(1)}, f32[512]{0:T(512)}, u32[]{:S(2)}) copy-start(f32[512]{0:T(512)} %param.23) | copy-start | bytes 6148
  89.8 27.7 %collective-permute-start.17 = (bf16[2,272,512]{2,1,0:T(8,128)(2,1)S(1)}, bf16[2,272,512]{2,1,0:T(8,128)(2,1)S(1)}, u32[]{:S(2)}, u32[]{:S(2)}) collective-permute-start(bf16[2,272,512]{2,1,0:T(8,128)(2,1)S(1)} %constant_dynamic-slice_fusion.3), channel_id=1, source_target_pairs={{0,4},{4,0},{8,12},{12,8},{16,20},{20,16},{24,28},{28,24},{1,5},{5... | collective-permute-start | bytes 1671176 | tf_op jit(solution)/shard_map/ppermute | solution.py:453
  91.3 26.2 %collective-permute-start.16 = (bf16[544,512]{1,0:T(8,128)(2,1)S(1)}, bf16[544,512]{1,0:T(8,128)(2,1)S(1)}, u32[]{:S(2)}, u32[]{:S(2)}) collective-permute-start(bf16[544,512]{1,0:T(8,128)(2,1)S(1)} %slice_bitcast_fusion.1.after_ref), channel_id=1, source_target_pairs={{0,2},{1,3},{2,0},{3,1},{4,6},{5,7},{6,4},{7,5},{8,10},{9,11},{10,... | collective-permute-start | bytes 1671176 | tf_op jit(solution)/shard_map/ppermute | solution.py:453
  91.9 25.7 %collective-permute-start.19 = (bf16[6,84,512]{2,1,0:T(8,128)(2,1)S(1)}, bf16[6,84,512]{2,1,0:T(8,128)(2,1)S(1)}, u32[]{:S(2)}, u32[]{:S(2)}) collective-permute-start(bf16[6,84,512]{2,1,0:T(8,128)(2,1)S(1)} %copy-done.27), channel_id=1, source_target_pairs={{0,2},{1,3},{2,0},{3,1},{4,6},{5,7},{6,4},{7,5},{8,10},{9,11},{10,... | collective-permute-start | bytes 1548296 | tf_op jit(solution)/shard_map/ppermute | solution.py:453
  93.4 22.9 %collective-permute-start.18 = (bf16[3,84,512]{2,1,0:T(8,128)(2,1)S(1)}, bf16[3,84,512]{2,1,0:T(8,128)(2,1)S(1)}, u32[]{:S(2)}, u32[]{:S(2)}) collective-permute-start(bf16[3,84,512]{2,1,0:T(8,128)(2,1)S(1)} %copy-done.30), channel_id=1, source_target_pairs={{0,1},{1,0},{2,3},{3,2},{4,5},{5,4},{6,7},{7,6},{8,9},{9,8},{10,11... | collective-permute-start | bytes 774152 | tf_op jit(solution)/shard_map/ppermute | solution.py:453
  119.5 3.0 %collective-permute-start.21 = (bf16[2,576,512]{2,1,0:T(8,128)(2,1)S(1)}, bf16[2,576,512]{2,1,0:T(8,128)(2,1)}, u32[]{:S(2)}, u32[]{:S(2)}) collective-permute-start(bf16[2,576,512]{2,1,0:T(8,128)(2,1)S(1)} %get-tuple-element.133), channel_id=1, source_target_pairs={{0,1},{1,0},{2,3},{3,2},{4,5},{5,4},{6,7},{7,6},{8,9},{9,8},{10,11... | collective-permute-start | bytes 3538952 | tf_op jit(solution)/shard_map/ppermute | solution.py:453
  119.5 9.7 %collective-permute-start.25 = (bf16[272,512]{1,0:T(8,128)(2,1)}, bf16[272,512]{1,0:T(8,128)(2,1)S(1)}, u32[]{:S(2)}, u32[]{:S(2)}) collective-permute-start(bf16[272,512]{1,0:T(8,128)(2,1)} %slice_bitcast_fusion.5), channel_id=1, source_target_pairs={{0,2},{1,3},{2,0},{3,1},{4,6},{5,7},{6,4},{7,5},{8,10},{9,11},{10,... | collective-permute-start | bytes 835592 | tf_op jit(solution)/shard_map/ppermute | solution.py:453
  120.1 9.1 %collective-permute-start.24 = (bf16[272,512]{1,0:T(8,128)(2,1)}, bf16[272,512]{1,0:T(8,128)(2,1)S(1)}, u32[]{:S(2)}, u32[]{:S(2)}) collective-permute-start(bf16[272,512]{1,0:T(8,128)(2,1)} %constant_dynamic-slice_fusion.2), channel_id=1, source_target_pairs={{0,4},{4,0},{8,12},{12,8},{16,20},{20,16},{24,28},{28,24},{1,5},{5... | collective-permute-start | bytes 835592 | tf_op jit(solution)/shard_map/ppermute | solution.py:453
  121.6 4.9 %collective-permute-start.20 = (bf16[6,84,512]{2,1,0:T(8,128)(2,1)S(1)}, bf16[6,84,512]{2,1,0:T(8,128)(2,1)S(1)}, u32[]{:S(2)}, u32[]{:S(2)}) collective-permute-start(bf16[6,84,512]{2,1,0:T(8,128)(2,1)S(1)} %collective-permute-done.19.b2), channel_id=1, source_target_pairs={{0,1},{1,0},{2,3},{3,2},{4,5},{5,4},{6,7},{7,6},{8,9},{9,8},{10,11... | collective-permute-start | bytes 1548296 | tf_op jit(solution)/shard_map/ppermute | solution.py:453
  124.2 9.9 %collective-permute-start.23 = (bf16[2,144,512]{2,1,0:T(8,128)(2,1)S(1)}, bf16[2,144,512]{2,1,0:T(8,128)(2,1)S(1)}, u32[]{:S(2)}, u32[]{:S(2)}) collective-permute-start(bf16[2,144,512]{2,1,0:T(8,128)(2,1)S(1)} %constant_dynamic-slice_fusion.1), channel_id=1, source_target_pairs={{0,8},{4,12},{8,0},{12,4},{16,24},{20,28},{24,16},{28,20},{1,9},{5... | collective-permute-start | bytes 884744 | tf_op jit(solution)/shard_map/ppermute | solution.py:453
  125.8 3.4 %copy-start.18 = (bf16[2,272,512]{2,1,0:T(8,128)(2,1)S(1)}, bf16[2,272,512]{2,1,0:T(8,128)(2,1)}, u32[]{:S(2)}) copy-start(bf16[2,272,512]{2,1,0:T(8,128)(2,1)} %copy-done.17) | copy-start | bytes 1671172
  125.9 3.4 %copy-start.21 = (bf16[544,512]{1,0:T(8,128)(2,1)S(1)}, bf16[544,512]{1,0:T(8,128)(2,1)}, u32[]{:S(2)}) copy-start(bf16[544,512]{1,0:T(8,128)(2,1)} %copy-done.20) | copy-start | bytes 1671172
  125.9 9.3 %collective-permute-start.22 = (bf16[288,512]{1,0:T(8,128)(2,1)S(1)}, bf16[288,512]{1,0:T(8,128)(2,1)S(1)}, u32[]{:S(2)}, u32[]{:S(2)}) collective-permute-start(bf16[288,512]{1,0:T(8,128)(2,1)S(1)} %slice_bitcast_fusion.3), channel_id=1, source_target_pairs={{0,2},{1,3},{2,0},{3,1},{4,6},{5,7},{6,4},{7,5},{8,10},{9,11},{10,... | collective-permute-start | bytes 884744 | tf_op jit(solution)/shard_map/ppermute | solution.py:453
  129.8 10.3 %collective-permute-start.28 = (bf16[272,512]{1,0:T(8,128)(2,1)S(1)}, bf16[272,512]{1,0:T(8,128)(2,1)S(1)}, u32[]{:S(2)}, u32[]{:S(2)}) collective-permute-start(bf16[272,512]{1,0:T(8,128)(2,1)S(1)} %fusion.5), channel_id=1, source_target_pairs={{0,8},{4,12},{8,0},{12,4},{16,24},{20,28},{24,16},{28,20},{1,9},{5... | collective-permute-start | bytes 835592 | tf_op jit(solution)/shard_map/ppermute | solution.py:453
  135.2 7.9 %copy-start.5 = (bf16[6,84,512]{2,1,0:T(8,128)(2,1)S(1)}, bf16[6,84,512]{2,1,0:T(8,128)(2,1)}, u32[]{:S(2)}) copy-start(bf16[6,84,512]{2,1,0:T(8,128)(2,1)} %copy-done.4) | copy-start | bytes 1548292
  135.2 8.0 %copy-start.7 = (bf16[3,84,512]{2,1,0:T(8,128)(2,1)S(1)}, bf16[3,84,512]{2,1,0:T(8,128)(2,1)}, u32[]{:S(2)}) copy-start(bf16[3,84,512]{2,1,0:T(8,128)(2,1)} %copy-done.6) | copy-start | bytes 774148
  135.3 8.0 %collective-permute-start.27 = (bf16[144,512]{1,0:T(8,128)(2,1)S(1)}, bf16[144,512]{1,0:T(8,128)(2,1)S(1)}, u32[]{:S(2)}, u32[]{:S(2)}) collective-permute-start(bf16[144,512]{1,0:T(8,128)(2,1)S(1)} %slice_bitcast_fusion.7), channel_id=1, source_target_pairs={{0,2},{1,3},{2,0},{3,1},{4,6},{5,7},{6,4},{7,5},{8,10},{9,11},{10,... | collective-permute-start | bytes 442376 | tf_op jit(solution)/shard_map/ppermute | solution.py:453
  136.0 7.3 %collective-permute-start.26 = (bf16[144,512]{1,0:T(8,128)(2,1)S(1)}, bf16[144,512]{1,0:T(8,128)(2,1)S(1)}, u32[]{:S(2)}, u32[]{:S(2)}) collective-permute-start(bf16[144,512]{1,0:T(8,128)(2,1)S(1)} %constant_dynamic-slice_fusion), channel_id=1, source_target_pairs={{0,8},{4,12},{8,0},{12,4},{16,24},{20,28},{24,16},{28,20},{1,9},{5... | collective-permute-start | bytes 442376 | tf_op jit(solution)/shard_map/ppermute | solution.py:453
  140.5 14.0 %collective-permute-start.32 = (bf16[272,512]{1,0:T(8,128)(2,1)S(1)}, bf16[272,512]{1,0:T(8,128)(2,1)S(1)}, u32[]{:S(2)}, u32[]{:S(2)}) collective-permute-start(bf16[272,512]{1,0:T(8,128)(2,1)S(1)} %add_convert_fusion.5), channel_id=1, source_target_pairs={{0,16},{4,20},{8,24},{12,28},{16,0},{20,4},{24,8},{28,12},{1,17},{... | collective-permute-start | bytes 835592 | tf_op jit(solution)/shard_map/ppermute | solution.py:453
  143.1 12.7 %collective-permute-start.31 = (bf16[6,84,512]{2,1,0:T(8,128)(2,1)S(1)}, bf16[6,84,512]{2,1,0:T(8,128)(2,1)S(1)}, u32[]{:S(2)}, u32[]{:S(2)}) collective-permute-start(bf16[6,84,512]{2,1,0:T(8,128)(2,1)S(1)} %copy-done.5), channel_id=1, source_target_pairs={{0,2},{1,3},{2,0},{3,1},{4,6},{5,7},{6,4},{7,5},{8,10},{9,11},{10,... | collective-permute-start | bytes 1548296 | tf_op jit(solution)/shard_map/ppermute | solution.py:453
  143.2 12.6 %collective-permute-start.30 = (bf16[3,84,512]{2,1,0:T(8,128)(2,1)S(1)}, bf16[3,84,512]{2,1,0:T(8,128)(2,1)S(1)}, u32[]{:S(2)}, u32[]{:S(2)}) collective-permute-start(bf16[3,84,512]{2,1,0:T(8,128)(2,1)S(1)} %copy-done.7), channel_id=1, source_target_pairs={{0,1},{1,0},{2,3},{3,2},{4,5},{5,4},{6,7},{7,6},{8,9},{9,8},{10,11... | collective-permute-start | bytes 774152 | tf_op jit(solution)/shard_map/ppermute | solution.py:453
  143.5 12.3 %collective-permute-start.29 = (bf16[144,512]{1,0:T(8,128)(2,1)S(1)}, bf16[144,512]{1,0:T(8,128)(2,1)S(1)}, u32[]{:S(2)}, u32[]{:S(2)}) collective-permute-start(bf16[144,512]{1,0:T(8,128)(2,1)S(1)} %fusion.7), channel_id=1, source_target_pairs={{0,4},{4,0},{8,12},{12,8},{16,20},{20,16},{24,28},{28,24},{1,5},{5... | collective-permute-start | bytes 442376 | tf_op jit(solution)/shard_map/ppermute | solution.py:453
  154.6 5.1 %collective-permute-start.34 = (bf16[136,512]{1,0:T(8,128)(2,1)S(1)}, bf16[136,512]{1,0:T(8,128)(2,1)S(1)}, u32[]{:S(2)}, u32[]{:S(2)}) collective-permute-start(bf16[136,512]{1,0:T(8,128)(2,1)S(1)} %get-tuple-element.216), channel_id=1, source_target_pairs={{0,8},{4,12},{8,0},{12,4},{16,24},{20,28},{24,16},{28,20},{1,9},{5... | collective-permute-start | bytes 417800 | tf_op jit(solution)/shard_map/ppermute | solution.py:453
  155.3 5.3 %collective-permute-start.35 = (bf16[136,512]{1,0:T(8,128)(2,1)S(1)}, bf16[136,512]{1,0:T(8,128)(2,1)S(1)}, u32[]{:S(2)}, u32[]{:S(2)}) collective-permute-start(bf16[136,512]{1,0:T(8,128)(2,1)S(1)} %get-tuple-element.215), channel_id=1, source_target_pairs={{0,4},{4,0},{8,12},{12,8},{16,20},{20,16},{24,28},{28,24},{1,5},{5... | collective-permute-start | bytes 417800 | tf_op jit(solution)/shard_map/ppermute | solution.py:453
  156.0 6.5 %collective-permute-start.33 = (bf16[6,84,512]{2,1,0:T(8,128)(2,1)S(1)}, bf16[6,84,512]{2,1,0:T(8,128)(2,1)S(1)}, u32[]{:S(2)}, u32[]{:S(2)}) collective-permute-start(bf16[6,84,512]{2,1,0:T(8,128)(2,1)S(1)} %collective-permute-done.31.b2), channel_id=1, source_target_pairs={{0,1},{1,0},{2,3},{3,2},{4,5},{5,4},{6,7},{7,6},{8,9},{9,8},{10,11... | collective-permute-start | bytes 1548296 | tf_op jit(solution)/shard_map/ppermute | solution.py:453
  156.1 11.1 %collective-permute-start.36 = (bf16[144,512]{1,0:T(8,128)(2,1)S(1)}, bf16[144,512]{1,0:T(8,128)(2,1)S(1)}, u32[]{:S(2)}, u32[]{:S(2)}) collective-permute-start(bf16[144,512]{1,0:T(8,128)(2,1)S(1)} %add_convert_fusion.8), channel_id=1, source_target_pairs={{0,16},{4,20},{8,24},{12,28},{16,0},{20,4},{24,8},{28,12},{1,17},{... | collective-permute-start | bytes 442376 | tf_op jit(solution)/shard_map/ppermute | solution.py:453
  160.7 9.7 %collective-permute-start.40 = (bf16[2,136,512]{2,1,0:T(8,128)(2,1)S(1)}, bf16[2,136,512]{2,1,0:T(8,128)(2,1)S(1)}, u32[]{:S(2)}, u32[]{:S(2)}) collective-permute-start(bf16[2,136,512]{2,1,0:T(8,128)(2,1)S(1)} %maximum_select_fusion.5), channel_id=1, source_target_pairs={{0,8},{4,12},{8,0},{12,4},{16,24},{20,28},{24,16},{28,20},{1,9},{5... | collective-permute-start | bytes 835592 | tf_op jit(solution)/shard_map/ppermute | solution.py:453
  161.9 8.5 %collective-permute-start.39 = (bf16[2,136,512]{2,1,0:T(8,128)(2,1)S(1)}, bf16[2,136,512]{2,1,0:T(8,128)(2,1)S(1)}, u32[]{:S(2)}, u32[]{:S(2)}) collective-permute-start(bf16[2,136,512]{2,1,0:T(8,128)(2,1)S(1)} %maximum_select_fusion.4), channel_id=1, source_target_pairs={{0,4},{4,0},{8,12},{12,8},{16,20},{20,16},{24,28},{28,24},{1,5},{5... | collective-permute-start | bytes 835592 | tf_op jit(solution)/shard_map/ppermute | solution.py:453
  167.3 5.8 %collective-permute-start.37 = (bf16[72,512]{1,0:T(8,128)(2,1)S(1)}, bf16[72,512]{1,0:T(8,128)(2,1)S(1)}, u32[]{:S(2)}, u32[]{:S(2)}) collective-permute-start(bf16[72,512]{1,0:T(8,128)(2,1)S(1)} %get-tuple-element.222), channel_id=1, source_target_pairs={{0,4},{4,0},{8,12},{12,8},{16,20},{20,16},{24,28},{28,24},{1,5},{5... | collective-permute-start | bytes 221192 | tf_op jit(solution)/shard_map/ppermute | solution.py:453
  168.9 4.4 %collective-permute-start.38 = (bf16[72,512]{1,0:T(8,128)(2,1)S(1)}, bf16[72,512]{1,0:T(8,128)(2,1)S(1)}, u32[]{:S(2)}, u32[]{:S(2)}) collective-permute-start(bf16[72,512]{1,0:T(8,128)(2,1)S(1)} %get-tuple-element.221), channel_id=1, source_target_pairs={{0,8},{4,12},{8,0},{12,4},{16,24},{20,28},{24,16},{28,20},{1,9},{5... | collective-permute-start | bytes 221192 | tf_op jit(solution)/shard_map/ppermute | solution.py:453
  173.3 5.2 %collective-permute-start.41 = (bf16[2,72,512]{2,1,0:T(8,128)(2,1)S(1)}, bf16[2,72,512]{2,1,0:T(8,128)(2,1)S(1)}, u32[]{:S(2)}, u32[]{:S(2)}) collective-permute-start(bf16[2,72,512]{2,1,0:T(8,128)(2,1)S(1)} %maximum_select_fusion.9), channel_id=1, source_target_pairs={{0,8},{4,12},{8,0},{12,4},{16,24},{20,28},{24,16},{28,20},{1,9},{5... | collective-permute-start | bytes 442376 | tf_op jit(solution)/shard_map/ppermute | solution.py:453
  174.8 5.2 %collective-permute-start.42 = (bf16[2,72,512]{2,1,0:T(8,128)(2,1)S(1)}, bf16[2,72,512]{2,1,0:T(8,128)(2,1)S(1)}, u32[]{:S(2)}, u32[]{:S(2)}) collective-permute-start(bf16[2,72,512]{2,1,0:T(8,128)(2,1)S(1)} %maximum_select_fusion.11), channel_id=1, source_target_pairs={{0,4},{4,0},{8,12},{12,8},{16,20},{20,16},{24,28},{28,24},{1,5},{5... | collective-permute-start | bytes 442376 | tf_op jit(solution)/shard_map/ppermute | solution.py:453
  (10 other events, 14.7 us)
